TPU v7x, 1024 devices: a whole 4x4x32 slice. The times are simulated.
1024 devices in a mesh: dp: 128 (over y, z_lo, core), mp: 8 (over x, z_hi).
Axes of the slice: x: 4, y: 4, z: 32 (z_hi: 2, z_lo: 16; z = z_hi * 16 + z_lo), core: 2. Of those that a mesh axis runs over, the one named last changes fastest.
Arguments:
- queries: bfloat16 [128, 256, 3072], P('dp', None, 'mp'), may hold values from -6 to 6
- attn_keys: bfloat16 [128, 256, 3072], P('dp', None, 'mp'), may hold values from -6 to 6
- attn_values: bfloat16 [128, 256, 3072], P('dp', None, 'mp'), may hold values from -6 to 6
- out_weight: bfloat16 [3072, 3072], P('dp', 'mp'), may hold values from -0.109375 to 0.109375
- grad_out: bfloat16 [128, 256, 3072], P('dp', 'mp'), may hold values from -96 to 96
Outputs:
- grad_queries: bfloat16 [128, 256, 3072], P('dp', None, 'mp')
- grad_keys: bfloat16 [128, 256, 3072], P('dp', None, 'mp')
- grad_values: bfloat16 [128, 256, 3072], P('dp', None, 'mp')
All inputs are finite; a program needn't handle non-finite values.
Results may differ from a plain program's by a relative error of at most 0.0095.
Values may be sent and summed in bfloat16 or wider, within the bound.
No kernel may reach another device: no remote copies, remote signals or barrier semaphores. Data moves between devices by JAX's collectives and lax.ppermute only.
A program may use at most 32 MiB of HBM per device.

v0:
```python
import math

import jax
import jax.numpy as jnp
from jax import lax
from jax.sharding import PartitionSpec as P

HD = 128


def softmax_rows(scores):
    shifted = scores - jnp.max(scores, axis=-1, keepdims=True)
    raised = jnp.exp(shifted)
    return raised / jnp.sum(raised, axis=-1, keepdims=True)


def shards(queries, attn_keys, attn_values, out_weight, grad_out):
    images = queries.shape[0]
    patches = queries.shape[1]
    width_dev = queries.shape[2]
    head_count = width_dev // HD
    score_scale = 1.0 / math.sqrt(HD)
    query_heads = queries.reshape(images, patches, head_count, HD)
    key_heads = attn_keys.reshape(images, patches, head_count, HD)
    value_heads = attn_values.reshape(images, patches, head_count, HD)
    all_grads = lax.all_gather(grad_out, "mp", axis=1, tiled=True)
    model_width = all_grads.shape[2]
    flat_grads = all_grads.reshape(images * patches, model_width)
    scores = (
        jnp.einsum("bihe,bjhe->bhij", query_heads, key_heads, preferred_element_type=jnp.float32)
        * score_scale
    )
    attention = softmax_rows(scores)
    rounded = attention.astype(jnp.bfloat16)
    grad_attn = jnp.dot(
        flat_grads,
        lax.all_gather(out_weight, "dp", axis=0, tiled=True),
        preferred_element_type=jnp.float32,
    )
    grad_heads = grad_attn.astype(jnp.bfloat16).reshape(images, patches, head_count, HD)
    grad_vals = jnp.einsum(
        "bhij,bihe->bjhe", rounded, grad_heads, preferred_element_type=jnp.float32
    ).astype(jnp.bfloat16)
    grad_probs = jnp.einsum(
        "bihe,bjhe->bhij", grad_heads, value_heads, preferred_element_type=jnp.float32
    )
    row_inner = jnp.sum(attention * grad_probs, axis=-1, keepdims=True)
    grad_scores = (attention * (grad_probs - row_inner) * score_scale).astype(jnp.bfloat16)
    grad_query = jnp.einsum(
        "bhij,bjhe->bihe", grad_scores, key_heads, preferred_element_type=jnp.float32
    ).astype(jnp.bfloat16)
    grad_key = jnp.einsum(
        "bhij,bihe->bjhe", grad_scores, query_heads, preferred_element_type=jnp.float32
    ).astype(jnp.bfloat16)
    return (
        grad_query.reshape(images, patches, width_dev),
        grad_key.reshape(images, patches, width_dev),
        grad_vals.reshape(images, patches, width_dev),
    )


def solution(mesh):
    in_specs = (
        P("dp", None, "mp"),
        P("dp", None, "mp"),
        P("dp", None, "mp"),
        P("dp", "mp"),
        P("dp", "mp", None),
    )
    out_specs = (P("dp", None, "mp"), P("dp", None, "mp"), P("dp", None, "mp"))
    return jax.shard_map(shards, mesh=mesh, in_specs=in_specs, out_specs=out_specs, check_vma=False)
```

profile of v0, /device:TPU:1, one launch (start us, length us, event | category | flops | bytes accessed | tf_op | source)
XLA Modules:
  0.0 433.9 jit_solution(772320800455194126)
XLA Ops:
  7.2 0.0 all-gather.3.cloned.1.call-start
  7.2 0.7 all-gather.3.cloned.1.call-update
  7.9 0.0 all-gather.5.cloned.1.call-start
  7.9 0.7 all-gather.5.cloned.1.call-update
  8.6 1.1 copy.21
  9.7 1.1 copy.22
  10.8 1.1 copy.26
  11.8 0.5 fusion.26
  12.3 182.4 %all-gather.3.cloned.1.call-done = bf16[1,256,3072]{2,1,0:T(8,128)(2,1)} async-done(((bf16[1,32,3072]{2,1,0:T(8,128)(2,1)}), bf16[1,256,3072]{2,1,0:T(8,128)(2,1)}) %all-gather.3.cloned.1.call-update) | async-done | bytes 1572880 | tf_op jit(solution)/shard_map/all_gather | solution.py:26
  194.7 224.8 %all-gather.5.cloned.1.call-done = bf16[3072,384]{1,0:T(8,128)(2,1)} async-done(((bf16[24,384]{1,0:T(8,128)(2,1)}), bf16[3072,384]{1,0:T(8,128)(2,1)}) %all-gather.5.cloned.1.call-update) | async-done | bytes 2359312 | tf_op jit(solution)/shard_map/all_gather | solution.py:37
  419.5 3.1 fusion.10
  422.7 0.1 copy.25
  422.8 0.3 fusion.27
  423.1 0.6 convolution_convert_fusion.1
  423.8 0.4 convolution_convert_fusion.2
  424.2 0.4 convolution_convert_fusion
  424.6 0.8 copy.32
  425.4 0.8 copy.33
  426.2 0.8 copy.34
Async XLA Ops:
  7.2 187.5 %all-gather.3.cloned.1.call-start = ((), (), s32[]{:S(2)}) async-start(), calls=%async_computation | async-start | bytes 1769472 | tf_op jit(solution)/shard_map/all_gather | solution.py:26
  7.9 411.6 %all-gather.5.cloned.1.call-start = ((), (), s32[]{:S(2)}) async-start(), calls=%async_computation.1 | async-start | bytes 2377728 | tf_op jit(solution)/shard_map/all_gather | solution.py:37
Sparse Core Ops, SparseCore 0:
  12.3 182.2 all-gather.2
  197.4 222.0 all-gather.4
where the time goes:
time: 434 us
  waiting for transfers between devices  409 us (94%)
  between operations  14.1 us (3%)
  local copies, waits for them, and re-layouts  5.78 us (1%)
  matrix products  5.32 us (1%)
    all_gather x1, waiting for transfers between devices, shards(): lax.all_gather(out_weight, 'dp', axis=0, tiled=True)  225 us
    all_gather x1, waiting for transfers between devices, shards(): all_grads = lax.all_gather(grad_out, 'mp', axis=1, tiled=True)  182 us
  transfers between devices with their start and end apart: 2, of which 2 were waited for; matrix products, arithmetic and copies ran while one was open for 1% of the time, Pallas kernels for 0%

commit v1 on v0

v1 whole, which is shorter than its diff:
```python
import math

import jax
import jax.numpy as jnp
import numpy as np
from jax import lax
from jax.experimental import pallas as pl
from jax.experimental.pallas import tpu as pltpu
from jax.sharding import PartitionSpec as P

HD = 128
AXES = ("dp", "mp")
NY, NZ, NC, NX, NH = 4, 16, 2, 4, 2


def exchange(y=0, z=0, core=0, x=0, half=0):
    pairs = []
    for dp in range(NY * NZ * NC):
        other = dp ^ (y * NZ * NC + z * NC + core)
        for mp in range(NX * NH):
            pairs.append((dp * NX * NH + mp, other * NX * NH + (mp ^ (x * NH + half))))
    return pairs


def swap(value, **moves):
    return lax.ppermute(value, AXES, exchange(**moves))


def nt(a, b):
    return lax.dot_general(a, b, (((1,), (1,)), ((), ())), preferred_element_type=jnp.float32)


def tn(a, b):
    return lax.dot_general(a, b, (((0,), (0,)), ((), ())), preferred_element_type=jnp.float32)


def nn(a, b):
    return lax.dot_general(a, b, (((1,), (0,)), ((), ())), preferred_element_type=jnp.float32)


def attention_kernel(q_ref, k_ref, out_ref):
    scale = 1.0 / math.sqrt(HD)
    for head in range(q_ref.shape[1] // HD):
        cols = pl.ds(head * HD, HD)
        scores = nt(q_ref[:, cols], k_ref[:, cols]) * scale
        raised = jnp.exp(scores - jnp.max(scores, axis=-1, keepdims=True))
        out_ref[head] = raised / jnp.sum(raised, axis=-1, keepdims=True)


def tail_kernel(rows_ref, attn_ref, q_ref, k_ref, v_ref, *refs):
    n_g = NX * NH
    n_w = NY * NC
    g_refs, w_refs = refs[:n_g], refs[n_g:n_g + n_w]
    gq_ref, gk_ref, gv_ref, grad_ref = refs[n_g + n_w:]
    scale = 1.0 / math.sqrt(HD)
    part, depth = g_refs[0].shape[0], w_refs[0].shape[0]
    total = None
    for piece in range(n_w):
        cols = pl.ds(piece * depth, depth)
        left = jnp.concatenate([g[:, cols] for g in g_refs], axis=0)
        term = nn(left, w_refs[piece][...])
        total = term if total is None else total + term
    total = total.astype(jnp.bfloat16)
    for slot in range(n_g):
        row = pl.multiple_of(rows_ref[slot] * part, part)
        grad_ref[pl.ds(row, part), :] = total[slot * part:(slot + 1) * part]
    for head in range(q_ref.shape[1] // HD):
        cols = pl.ds(head * HD, HD)
        grad = grad_ref[:, cols]
        attn = attn_ref[head]
        gv_ref[:, cols] = tn(attn.astype(jnp.bfloat16), grad).astype(jnp.bfloat16)
        probs = nt(grad, v_ref[:, cols])
        inner = jnp.sum(attn * probs, axis=-1, keepdims=True)
        ds = (attn * (probs - inner) * scale).astype(jnp.bfloat16)
        gq_ref[:, cols] = nn(ds, k_ref[:, cols]).astype(jnp.bfloat16)
        gk_ref[:, cols] = tn(ds, q_ref[:, cols]).astype(jnp.bfloat16)


VMEM = pl.BlockSpec(memory_space=pltpu.VMEM)
SMEM = pl.BlockSpec(memory_space=pltpu.SMEM)
PARAMS = pltpu.CompilerParams(vmem_limit_bytes=24 * 1024 * 1024)


def shards(queries, attn_keys, attn_values, out_weight, grad_out):
    patches, width = queries.shape[1], queries.shape[2]
    heads = width // HD
    q, k, v = (a.reshape(patches, width) for a in (queries, attn_keys, attn_values))
    part, model = grad_out.shape[1], grad_out.shape[2]
    block = out_weight.shape[0]
    dp, mp = lax.axis_index("dp"), lax.axis_index("mp")
    core, z, y = dp % NC, (dp // NC) % NZ, dp // (NC * NZ)

    span = NZ * NC * block
    place = np.arange(span)
    z_bits = (place // block) % NZ
    z_xor = sum(((z_bits >> b) & 1) << (3 - b) for b in range(4))
    core_xor = place // (NZ * block)
    source = ((jnp.asarray(z_xor) ^ z) * NC + (jnp.asarray(core_xor) ^ core)) * block + jnp.asarray(place % block)
    pick = (jnp.arange(span)[:, None] == source[None, :]).astype(jnp.bfloat16)
    grads = jnp.dot(
        grad_out.reshape(part * NY, span), pick, preferred_element_type=jnp.float32
    ).astype(jnp.bfloat16).reshape(part, 2, 2, span)
    grads = jnp.where((y & 2) != 0, jnp.flip(grads, 1), grads)
    grads = jnp.where((y & 1) != 0, jnp.flip(grads, 2), grads)
    own = grads.reshape(part, model)

    weight = out_weight
    weight = jnp.concatenate([weight, swap(weight, z=8)], 0)
    weight = jnp.concatenate([weight, swap(weight, z=4)], 0)
    weight = jnp.concatenate([weight, swap(weight, z=2)], 0)
    weight = jnp.concatenate([weight, swap(weight, z=1)], 0)
    by_y = [weight] + [swap(weight, y=i) for i in (1, 2, 3)]
    weights = []
    for piece in by_y:
        weights += [piece, swap(piece, core=1)]

    far = swap(own, half=1)
    pieces = [own] + [swap(own, x=i) for i in (1, 2, 3)]
    pieces += [far] + [swap(far, x=i) for i in (1, 2, 3)]
    rows = jnp.stack([mp ^ (i * NH + h) for h in range(NH) for i in range(NX)]).astype(jnp.int32)

    attn = pl.pallas_call(
        attention_kernel,
        out_shape=jax.ShapeDtypeStruct((heads, patches, patches), jnp.float32),
        in_specs=[VMEM] * 2,
        out_specs=VMEM,
        compiler_params=PARAMS,
        cost_estimate=pl.CostEstimate(flops=2 * patches * patches * width, bytes_accessed=1 << 20, transcendentals=0),
    )(q, k)
    grad_shape = jax.ShapeDtypeStruct((patches, width), jnp.bfloat16)
    outs = pl.pallas_call(
        tail_kernel,
        out_shape=(grad_shape,) * 3,
        in_specs=[SMEM] + [VMEM] * (4 + len(pieces) + len(weights)),
        out_specs=(VMEM,) * 3,
        scratch_shapes=[pltpu.VMEM((patches, width), jnp.bfloat16)],
        compiler_params=PARAMS,
        cost_estimate=pl.CostEstimate(flops=2 * patches * width * (model + 4 * patches), bytes_accessed=6 << 20, transcendentals=0),
    )(rows, attn, q, k, v, *pieces, *weights)
    return tuple(o.reshape(1, patches, width) for o in outs)


def solution(mesh):
    in_specs = (
        P("dp", None, "mp"),
        P("dp", None, "mp"),
        P("dp", None, "mp"),
        P("dp", "mp"),
        P("dp", "mp", None),
    )
    out_specs = (P("dp", None, "mp"), P("dp", None, "mp"), P("dp", None, "mp"))
    return jax.shard_map(shards, mesh=mesh, in_specs=in_specs, out_specs=out_specs, check_vma=False)
```

time: 434 us -> 140 us (0.32)
  waiting for transfers between devices: 409 us -> 41.4 us
  starting transfers between devices: 0.08 us -> 84.9 us
  between operations: 14.1 us -> 1.15 us
  matrix products: 5.32 us -> 0.55 us
  Pallas kernels: 0 us -> 4.4 us
    all_gather x2 -> x0, waiting for transfers between devices: 407 us -> none  [the longest x1 225 us: shards(): lax.all_gather(out_weight, 'dp', axis=0, tiled=True)]
    ppermute x0 -> x18, starting transfers between devices: none -> 84.9 us  [swap(): return lax.ppermute(value, AXES, exchange(**moves))]
    ppermute x0 -> x18, waiting for transfers between devices: none -> 41.4 us  [swap(): return lax.ppermute(value, AXES, exchange(**moves))]
    pallas_call x0 -> x2, Pallas kernels: none -> 4.4 us  [the longest x1 3.93 us: shards(): pl.pallas_call(tail_kernel, out_shape=(grad_shape,) * 3, in_specs=[SMEM]...]
  transfers between devices with their start and end apart: 2 -> 18, of which waited for: 2 -> 5; matrix products, arithmetic and copies ran while one was open for 1% -> 3% of each run, Pallas kernels for 0% -> 0%
where the time goes in v1:
time: 140 us; the launch traced here: 139 us
  starting transfers between devices  84.9 us (61%)
  waiting for transfers between devices  41.4 us (30%)
  local copies, waits for them, and re-layouts  5.23 us (4%)
  Pallas kernels  4.4 us (3%)
    ppermute x18, starting transfers between devices, swap(): return lax.ppermute(value, AXES, exchange(**moves))  84.9 us
    ppermute x18, waiting for transfers between devices, swap(): return lax.ppermute(value, AXES, exchange(**moves))  41.4 us
    pallas_call x1, Pallas kernels, shards(): pl.pallas_call(tail_kernel, out_shape=(grad_shape,) * 3, in_specs=[SMEM]...  3.93 us
  transfers between devices with their start and end apart: 18, of which 5 were waited for; matrix products, arithmetic and copies ran while one was open for 3% of the time, Pallas kernels for 0%

profile of v1, /device:TPU:1, one launch (start us, length us, event | category | flops | bytes accessed | tf_op | source)
XLA Modules:
  0.0 138.8 jit_solution(12597413370169766583)
XLA Ops:
  0.6 16.3 %collective-permute-start.7 = (bf16[24,384]{1,0:T(8,128)(2,1)}, bf16[24,384]{1,0:T(8,128)(2,1)S(1)}, u32[]{:S(2)}, u32[]{:S(2)}) collective-permute-start(bf16[24,384]{1,0:T(8,128)(2,1)} %param.11), channel_id=1, source_target_pairs={{0,128},{1,129},{2,130},{3,131},{4,132},{5,133},{6,134},{7,135},{8... | collective-permute-start | bytes 55304 | tf_op jit(solution)/shard_map/ppermute | solution.py:26
  19.6 1.1 rev.9
  21.2 19.2 %collective-permute-start.3 = (bf16[32,3072]{1,0:T(8,128)(2,1)S(1)}, bf16[32,3072]{1,0:T(8,128)(2,1)S(1)}, u32[]{:S(2)}, u32[]{:S(2)}) collective-permute-start(bf16[32,3072]{1,0:T(8,128)(2,1)S(1)} %reshape.39.refs_0_), channel_id=1, source_target_pairs={{0,1},{1,0},{2,3},{3,2},{4,5},{5,4},{6,7},{7,6},{8,9},{9,8},{10,11... | collective-permute-start | bytes 589832 | tf_op jit(solution)/shard_map/ppermute | solution.py:26
  40.4 4.4 %collective-permute-start.2 = (bf16[32,3072]{1,0:T(8,128)(2,1)S(1)}, bf16[32,3072]{1,0:T(8,128)(2,1)S(1)}, u32[]{:S(2)}, u32[]{:S(2)}) collective-permute-start(bf16[32,3072]{1,0:T(8,128)(2,1)S(1)} %reshape.39.refs_0_), channel_id=1, source_target_pairs={{0,6},{1,7},{2,4},{3,5},{4,2},{5,3},{6,0},{7,1},{8,14},{9,15},{10,... | collective-permute-start | bytes 589832 | tf_op jit(solution)/shard_map/ppermute | solution.py:26
  44.8 2.4 %collective-permute-start.1 = (bf16[32,3072]{1,0:T(8,128)(2,1)S(1)}, bf16[32,3072]{1,0:T(8,128)(2,1)S(1)}, u32[]{:S(2)}, u32[]{:S(2)}) collective-permute-start(bf16[32,3072]{1,0:T(8,128)(2,1)S(1)} %reshape.39.refs_0_), channel_id=1, source_target_pairs={{0,4},{1,5},{2,6},{3,7},{4,0},{5,1},{6,2},{7,3},{8,12},{9,13},{10,... | collective-permute-start | bytes 589832 | tf_op jit(solution)/shard_map/ppermute | solution.py:26
  47.3 2.2 %collective-permute-start = (bf16[32,3072]{1,0:T(8,128)(2,1)S(1)}, bf16[32,3072]{1,0:T(8,128)(2,1)S(1)}, u32[]{:S(2)}, u32[]{:S(2)}) collective-permute-start(bf16[32,3072]{1,0:T(8,128)(2,1)S(1)} %reshape.39.refs_0_), channel_id=1, source_target_pairs={{0,2},{1,3},{2,0},{3,1},{4,6},{5,7},{6,4},{7,5},{8,10},{9,11},{10,... | collective-permute-start | bytes 589832 | tf_op jit(solution)/shard_map/ppermute | solution.py:26
  49.5 4.0 %collective-permute-start.8 = (bf16[48,384]{1,0:T(8,128)(2,1)S(1)}, bf16[48,384]{1,0:T(8,128)(2,1)S(1)}, u32[]{:S(2)}, u32[]{:S(2)}) collective-permute-start(bf16[48,384]{1,0:T(8,128)(2,1)S(1)} %pad_maximum_fusion.2), channel_id=1, source_target_pairs={{0,64},{1,65},{2,66},{3,67},{4,68},{5,69},{6,70},{7,71},{8,72},{9,... | collective-permute-start | bytes 110600 | tf_op jit(solution)/shard_map/ppermute | solution.py:26
  53.5 25.5 %collective-permute-done.8 = bf16[48,384]{1,0:T(8,128)(2,1)S(1)} collective-permute-done((bf16[48,384]{1,0:T(8,128)(2,1)S(1)}, bf16[48,384]{1,0:T(8,128)(2,1)S(1)}, u32[]{:S(2)}, u32[]{:S(2)}) %collective-permute-start.8) | collective-permute-done | bytes 36896 | tf_op jit(solution)/shard_map/ppermute | solution.py:26
  79.0 1.9 %collective-permute-start.9 = (bf16[96,384]{1,0:T(8,128)(2,1)S(1)}, bf16[96,384]{1,0:T(8,128)(2,1)S(1)}, u32[]{:S(2)}, u32[]{:S(2)}) collective-permute-start(bf16[96,384]{1,0:T(8,128)(2,1)S(1)} %pad_maximum_fusion.1), channel_id=1, source_target_pairs={{0,32},{1,33},{2,34},{3,35},{4,36},{5,37},{6,38},{7,39},{8,40},{9,... | collective-permute-start | bytes 221192 | tf_op jit(solution)/shard_map/ppermute | solution.py:26
  81.0 5.5 %collective-permute-done.9 = bf16[96,384]{1,0:T(8,128)(2,1)S(1)} collective-permute-done((bf16[96,384]{1,0:T(8,128)(2,1)S(1)}, bf16[96,384]{1,0:T(8,128)(2,1)S(1)}, u32[]{:S(2)}, u32[]{:S(2)}) %collective-permute-start.9) | collective-permute-done | bytes 73760 | tf_op jit(solution)/shard_map/ppermute | solution.py:26
  86.5 1.9 %collective-permute-start.10 = (bf16[192,384]{1,0:T(8,128)(2,1)S(1)}, bf16[192,384]{1,0:T(8,128)(2,1)S(1)}, u32[]{:S(2)}, u32[]{:S(2)}) collective-permute-start(bf16[192,384]{1,0:T(8,128)(2,1)S(1)} %pad_maximum_fusion), channel_id=1, source_target_pairs={{0,16},{1,17},{2,18},{3,19},{4,20},{5,21},{6,22},{7,23},{8,24},{9,... | collective-permute-start | bytes 442376 | tf_op jit(solution)/shard_map/ppermute | solution.py:26
  88.5 4.5 %collective-permute-done.10 = bf16[192,384]{1,0:T(8,128)(2,1)S(1)} collective-permute-done((bf16[192,384]{1,0:T(8,128)(2,1)S(1)}, bf16[192,384]{1,0:T(8,128)(2,1)S(1)}, u32[]{:S(2)}, u32[]{:S(2)}) %collective-permute-start.10) | collective-permute-done | bytes 147488 | tf_op jit(solution)/shard_map/ppermute | solution.py:26
  93.0 4.6 %collective-permute-start.16 = (bf16[384,384]{1,0:T(8,128)(2,1)S(1)}, bf16[384,384]{1,0:T(8,128)(2,1)S(1)}, u32[]{:S(2)}, u32[]{:S(2)}) collective-permute-start(bf16[384,384]{1,0:T(8,128)(2,1)S(1)} %constant_dynamic-update-slice_fusion.refs_8_), channel_id=1, source_target_pairs={{0,768},{1,769},{2,770},{3,771},{4,772},{5,773},{6,774},{7,775},{8... | collective-permute-start | bytes 884744 | tf_op jit(solution)/shard_map/ppermute | solution.py:26
  97.6 2.3 %collective-permute-start.14 = (bf16[384,384]{1,0:T(8,128)(2,1)S(1)}, bf16[384,384]{1,0:T(8,128)(2,1)S(1)}, u32[]{:S(2)}, u32[]{:S(2)}) collective-permute-start(bf16[384,384]{1,0:T(8,128)(2,1)S(1)} %constant_dynamic-update-slice_fusion.refs_8_), channel_id=1, source_target_pairs={{0,512},{1,513},{2,514},{3,515},{4,516},{5,517},{6,518},{7,519},{8... | collective-permute-start | bytes 884744 | tf_op jit(solution)/shard_map/ppermute | solution.py:26
  99.9 2.1 %collective-permute-start.12 = (bf16[384,384]{1,0:T(8,128)(2,1)S(1)}, bf16[384,384]{1,0:T(8,128)(2,1)S(1)}, u32[]{:S(2)}, u32[]{:S(2)}) collective-permute-start(bf16[384,384]{1,0:T(8,128)(2,1)S(1)} %constant_dynamic-update-slice_fusion.refs_8_), channel_id=1, source_target_pairs={{0,256},{1,257},{2,258},{3,259},{4,260},{5,261},{6,262},{7,263},{8... | collective-permute-start | bytes 884744 | tf_op jit(solution)/shard_map/ppermute | solution.py:26
  102.7 4.4 %collective-permute-start.6 = (bf16[32,3072]{1,0:T(8,128)(2,1)S(1)}, bf16[32,3072]{1,0:T(8,128)(2,1)S(1)}, u32[]{:S(2)}, u32[]{:S(2)}) collective-permute-start(bf16[32,3072]{1,0:T(8,128)(2,1)S(1)} %collective-permute-done.3.refs_4_), channel_id=1, source_target_pairs={{0,6},{1,7},{2,4},{3,5},{4,2},{5,3},{6,0},{7,1},{8,14},{9,15},{10,... | collective-permute-start | bytes 589832 | tf_op jit(solution)/shard_map/ppermute | solution.py:26
  107.8 2.4 %collective-permute-start.5 = (bf16[32,3072]{1,0:T(8,128)(2,1)S(1)}, bf16[32,3072]{1,0:T(8,128)(2,1)S(1)}, u32[]{:S(2)}, u32[]{:S(2)}) collective-permute-start(bf16[32,3072]{1,0:T(8,128)(2,1)S(1)} %collective-permute-done.3.refs_4_), channel_id=1, source_target_pairs={{0,4},{1,5},{2,6},{3,7},{4,0},{5,1},{6,2},{7,3},{8,12},{9,13},{10,... | collective-permute-start | bytes 589832 | tf_op jit(solution)/shard_map/ppermute | solution.py:26
  111.3 8.5 %collective-permute-start.11 = (bf16[384,384]{1,0:T(8,128)(2,1)S(1)}, bf16[384,384]{1,0:T(8,128)(2,1)S(1)}, u32[]{:S(2)}, u32[]{:S(2)}) collective-permute-start(bf16[384,384]{1,0:T(8,128)(2,1)S(1)} %constant_dynamic-update-slice_fusion.refs_8_), channel_id=1, source_target_pairs={{0,8},{1,9},{2,10},{3,11},{4,12},{5,13},{6,14},{7,15},{8,0},{9,1},... | collective-permute-start | bytes 884744 | tf_op jit(solution)/shard_map/ppermute | solution.py:26
  119.9 1.9 %collective-permute-start.17 = (bf16[384,384]{1,0:T(8,128)(2,1)S(1)}, bf16[384,384]{1,0:T(8,128)(2,1)S(1)}, u32[]{:S(2)}, u32[]{:S(2)}) collective-permute-start(bf16[384,384]{1,0:T(8,128)(2,1)S(1)} %collective-permute-done.16.refs_14_), channel_id=1, source_target_pairs={{0,8},{1,9},{2,10},{3,11},{4,12},{5,13},{6,14},{7,15},{8,0},{9,1},... | collective-permute-start | bytes 884744 | tf_op jit(solution)/shard_map/ppermute | solution.py:26
  121.8 2.4 %collective-permute-start.15 = (bf16[384,384]{1,0:T(8,128)(2,1)S(1)}, bf16[384,384]{1,0:T(8,128)(2,1)S(1)}, u32[]{:S(2)}, u32[]{:S(2)}) collective-permute-start(bf16[384,384]{1,0:T(8,128)(2,1)S(1)} %collective-permute-done.14.refs_12_), channel_id=1, source_target_pairs={{0,8},{1,9},{2,10},{3,11},{4,12},{5,13},{6,14},{7,15},{8,0},{9,1},... | collective-permute-start | bytes 884744 | tf_op jit(solution)/shard_map/ppermute | solution.py:26
  124.3 1.9 %collective-permute-start.13 = (bf16[384,384]{1,0:T(8,128)(2,1)S(1)}, bf16[384,384]{1,0:T(8,128)(2,1)S(1)}, u32[]{:S(2)}, u32[]{:S(2)}) collective-permute-start(bf16[384,384]{1,0:T(8,128)(2,1)S(1)} %collective-permute-done.12.refs_10_), channel_id=1, source_target_pairs={{0,8},{1,9},{2,10},{3,11},{4,12},{5,13},{6,14},{7,15},{8,0},{9,1},... | collective-permute-start | bytes 884744 | tf_op jit(solution)/shard_map/ppermute | solution.py:26
  126.9 1.9 %collective-permute-start.4 = (bf16[32,3072]{1,0:T(8,128)(2,1)S(1)}, bf16[32,3072]{1,0:T(8,128)(2,1)}, u32[]{:S(2)}, u32[]{:S(2)}) collective-permute-start(bf16[32,3072]{1,0:T(8,128)(2,1)S(1)} %collective-permute-done.3.refs_4_), channel_id=1, source_target_pairs={{0,2},{1,3},{2,0},{3,1},{4,6},{5,7},{6,4},{7,5},{8,10},{9,11},{10,... | collective-permute-start | bytes 589832 | tf_op jit(solution)/shard_map/ppermute | solution.py:26
  129.4 5.4 %collective-permute-done.4.refs_5_ = bf16[32,3072]{1,0:T(8,128)(2,1)} collective-permute-done((bf16[32,3072]{1,0:T(8,128)(2,1)S(1)}, bf16[32,3072]{1,0:T(8,128)(2,1)}, u32[]{:S(2)}, u32[]{:S(2)}) %collective-permute-start.4) | collective-permute-done | bytes 196640 | tf_op jit(solution)/shard_map/ppermute | solution.py:26
  134.9 3.9 %shard_map.104 = (bf16[256,384]{1,0:T(8,128)(2,1)}, bf16[256,384]{1,0:T(8,128)(2,1)}, bf16[256,384]{1,0:T(8,128)(2,1)}) custom-call(s32[8]{0:T(128)S(1)} %stack.35.rows_ref, f32[3,256,256]{2,1,0:T(8,128)S(1)} %shard_map.103.attn_ref, bf16[256,384]{1,0:T(8,128)(2,1)S(1)} %bitcast.18, bf16[256,384]{1,0:T(8,128)(2,1)S(1)} %bitcast.20, ...), custom_call_target="tpu_custom_call" | custom-call | flops 805306368 | bytes 6291456 | tf_op jit(solution)/shard_map/pallas_call | solution.py:131
  (55 shorter events, 6.9 us)
Async XLA Ops:
  0.6 48.8 %collective-permute-start.7 = (bf16[24,384]{1,0:T(8,128)(2,1)}, bf16[24,384]{1,0:T(8,128)(2,1)S(1)}, u32[]{:S(2)}, u32[]{:S(2)}) collective-permute-start(bf16[24,384]{1,0:T(8,128)(2,1)} %param.11), channel_id=1, source_target_pairs={{0,128},{1,129},{2,130},{3,131},{4,132},{5,133},{6,134},{7,135},{8... | collective-permute-start | bytes 55304 | tf_op jit(solution)/shard_map/ppermute | solution.py:26
  19.6 29.8 %copy-start.11 = (bf16[24,384]{1,0:T(8,128)(2,1)S(1)}, bf16[24,384]{1,0:T(8,128)(2,1)}, u32[]{:S(2)}) copy-start(bf16[24,384]{1,0:T(8,128)(2,1)} %param.11) | copy-start | bytes 55300
  21.0 107.9 %copy-start = (bf16[1,256,384]{2,1,0:T(8,128)(2,1)S(1)}, bf16[1,256,384]{2,1,0:T(8,128)(2,1)}, u32[]{:S(2)}) copy-start(bf16[1,256,384]{2,1,0:T(8,128)(2,1)} %param.8) | copy-start | bytes 589828
  21.1 107.9 %copy-start.1 = (bf16[1,256,384]{2,1,0:T(8,128)(2,1)S(1)}, bf16[1,256,384]{2,1,0:T(8,128)(2,1)}, u32[]{:S(2)}) copy-start(bf16[1,256,384]{2,1,0:T(8,128)(2,1)} %param.9) | copy-start | bytes 589828
  21.2 76.4 %collective-permute-start.3 = (bf16[32,3072]{1,0:T(8,128)(2,1)S(1)}, bf16[32,3072]{1,0:T(8,128)(2,1)S(1)}, u32[]{:S(2)}, u32[]{:S(2)}) collective-permute-start(bf16[32,3072]{1,0:T(8,128)(2,1)S(1)} %reshape.39.refs_0_), channel_id=1, source_target_pairs={{0,1},{1,0},{2,3},{3,2},{4,5},{5,4},{6,7},{7,6},{8,9},{9,8},{10,11... | collective-permute-start | bytes 589832 | tf_op jit(solution)/shard_map/ppermute | solution.py:26
  40.4 59.5 %collective-permute-start.2 = (bf16[32,3072]{1,0:T(8,128)(2,1)S(1)}, bf16[32,3072]{1,0:T(8,128)(2,1)S(1)}, u32[]{:S(2)}, u32[]{:S(2)}) collective-permute-start(bf16[32,3072]{1,0:T(8,128)(2,1)S(1)} %reshape.39.refs_0_), channel_id=1, source_target_pairs={{0,6},{1,7},{2,4},{3,5},{4,2},{5,3},{6,0},{7,1},{8,14},{9,15},{10,... | collective-permute-start | bytes 589832 | tf_op jit(solution)/shard_map/ppermute | solution.py:26
  44.8 57.2 %collective-permute-start.1 = (bf16[32,3072]{1,0:T(8,128)(2,1)S(1)}, bf16[32,3072]{1,0:T(8,128)(2,1)S(1)}, u32[]{:S(2)}, u32[]{:S(2)}) collective-permute-start(bf16[32,3072]{1,0:T(8,128)(2,1)S(1)} %reshape.39.refs_0_), channel_id=1, source_target_pairs={{0,4},{1,5},{2,6},{3,7},{4,0},{5,1},{6,2},{7,3},{8,12},{9,13},{10,... | collective-permute-start | bytes 589832 | tf_op jit(solution)/shard_map/ppermute | solution.py:26
  47.3 59.9 %collective-permute-start = (bf16[32,3072]{1,0:T(8,128)(2,1)S(1)}, bf16[32,3072]{1,0:T(8,128)(2,1)S(1)}, u32[]{:S(2)}, u32[]{:S(2)}) collective-permute-start(bf16[32,3072]{1,0:T(8,128)(2,1)S(1)} %reshape.39.refs_0_), channel_id=1, source_target_pairs={{0,2},{1,3},{2,0},{3,1},{4,6},{5,7},{6,4},{7,5},{8,10},{9,11},{10,... | collective-permute-start | bytes 589832 | tf_op jit(solution)/shard_map/ppermute | solution.py:26
  49.5 29.6 %collective-permute-start.8 = (bf16[48,384]{1,0:T(8,128)(2,1)S(1)}, bf16[48,384]{1,0:T(8,128)(2,1)S(1)}, u32[]{:S(2)}, u32[]{:S(2)}) collective-permute-start(bf16[48,384]{1,0:T(8,128)(2,1)S(1)} %pad_maximum_fusion.2), channel_id=1, source_target_pairs={{0,64},{1,65},{2,66},{3,67},{4,68},{5,69},{6,70},{7,71},{8,72},{9,... | collective-permute-start | bytes 110600 | tf_op jit(solution)/shard_map/ppermute | solution.py:26
  79.0 7.4 %collective-permute-start.9 = (bf16[96,384]{1,0:T(8,128)(2,1)S(1)}, bf16[96,384]{1,0:T(8,128)(2,1)S(1)}, u32[]{:S(2)}, u32[]{:S(2)}) collective-permute-start(bf16[96,384]{1,0:T(8,128)(2,1)S(1)} %pad_maximum_fusion.1), channel_id=1, source_target_pairs={{0,32},{1,33},{2,34},{3,35},{4,36},{5,37},{6,38},{7,39},{8,40},{9,... | collective-permute-start | bytes 221192 | tf_op jit(solution)/shard_map/ppermute | solution.py:26
  86.5 6.4 %collective-permute-start.10 = (bf16[192,384]{1,0:T(8,128)(2,1)S(1)}, bf16[192,384]{1,0:T(8,128)(2,1)S(1)}, u32[]{:S(2)}, u32[]{:S(2)}) collective-permute-start(bf16[192,384]{1,0:T(8,128)(2,1)S(1)} %pad_maximum_fusion), channel_id=1, source_target_pairs={{0,16},{1,17},{2,18},{3,19},{4,20},{5,21},{6,22},{7,23},{8,24},{9,... | collective-permute-start | bytes 442376 | tf_op jit(solution)/shard_map/ppermute | solution.py:26
  88.5 46.4 %copy-start.2 = (bf16[1,256,384]{2,1,0:T(8,128)(2,1)S(1)}, bf16[1,256,384]{2,1,0:T(8,128)(2,1)}, u32[]{:S(2)}) copy-start(bf16[1,256,384]{2,1,0:T(8,128)(2,1)} %param.10) | copy-start | bytes 589828
  93.0 26.9 %collective-permute-start.16 = (bf16[384,384]{1,0:T(8,128)(2,1)S(1)}, bf16[384,384]{1,0:T(8,128)(2,1)S(1)}, u32[]{:S(2)}, u32[]{:S(2)}) collective-permute-start(bf16[384,384]{1,0:T(8,128)(2,1)S(1)} %constant_dynamic-update-slice_fusion.refs_8_), channel_id=1, source_target_pairs={{0,768},{1,769},{2,770},{3,771},{4,772},{5,773},{6,774},{7,775},{8... | collective-permute-start | bytes 884744 | tf_op jit(solution)/shard_map/ppermute | solution.py:26
  97.6 24.2 %collective-permute-start.14 = (bf16[384,384]{1,0:T(8,128)(2,1)S(1)}, bf16[384,384]{1,0:T(8,128)(2,1)S(1)}, u32[]{:S(2)}, u32[]{:S(2)}) collective-permute-start(bf16[384,384]{1,0:T(8,128)(2,1)S(1)} %constant_dynamic-update-slice_fusion.refs_8_), channel_id=1, source_target_pairs={{0,512},{1,513},{2,514},{3,515},{4,516},{5,517},{6,518},{7,519},{8... | collective-permute-start | bytes 884744 | tf_op jit(solution)/shard_map/ppermute | solution.py:26
  99.9 24.4 %collective-permute-start.12 = (bf16[384,384]{1,0:T(8,128)(2,1)S(1)}, bf16[384,384]{1,0:T(8,128)(2,1)S(1)}, u32[]{:S(2)}, u32[]{:S(2)}) collective-permute-start(bf16[384,384]{1,0:T(8,128)(2,1)S(1)} %constant_dynamic-update-slice_fusion.refs_8_), channel_id=1, source_target_pairs={{0,256},{1,257},{2,258},{3,259},{4,260},{5,261},{6,262},{7,263},{8... | collective-permute-start | bytes 884744 | tf_op jit(solution)/shard_map/ppermute | solution.py:26
  102.7 7.9 %collective-permute-start.6 = (bf16[32,3072]{1,0:T(8,128)(2,1)S(1)}, bf16[32,3072]{1,0:T(8,128)(2,1)S(1)}, u32[]{:S(2)}, u32[]{:S(2)}) collective-permute-start(bf16[32,3072]{1,0:T(8,128)(2,1)S(1)} %collective-permute-done.3.refs_4_), channel_id=1, source_target_pairs={{0,6},{1,7},{2,4},{3,5},{4,2},{5,3},{6,0},{7,1},{8,14},{9,15},{10,... | collective-permute-start | bytes 589832 | tf_op jit(solution)/shard_map/ppermute | solution.py:26
  107.8 18.4 %collective-permute-start.5 = (bf16[32,3072]{1,0:T(8,128)(2,1)S(1)}, bf16[32,3072]{1,0:T(8,128)(2,1)S(1)}, u32[]{:S(2)}, u32[]{:S(2)}) collective-permute-start(bf16[32,3072]{1,0:T(8,128)(2,1)S(1)} %collective-permute-done.3.refs_4_), channel_id=1, source_target_pairs={{0,4},{1,5},{2,6},{3,7},{4,0},{5,1},{6,2},{7,3},{8,12},{9,13},{10,... | collective-permute-start | bytes 589832 | tf_op jit(solution)/shard_map/ppermute | solution.py:26
  111.3 23.5 %collective-permute-start.11 = (bf16[384,384]{1,0:T(8,128)(2,1)S(1)}, bf16[384,384]{1,0:T(8,128)(2,1)S(1)}, u32[]{:S(2)}, u32[]{:S(2)}) collective-permute-start(bf16[384,384]{1,0:T(8,128)(2,1)S(1)} %constant_dynamic-update-slice_fusion.refs_8_), channel_id=1, source_target_pairs={{0,8},{1,9},{2,10},{3,11},{4,12},{5,13},{6,14},{7,15},{8,0},{9,1},... | collective-permute-start | bytes 884744 | tf_op jit(solution)/shard_map/ppermute | solution.py:26
  119.9 14.9 %collective-permute-start.17 = (bf16[384,384]{1,0:T(8,128)(2,1)S(1)}, bf16[384,384]{1,0:T(8,128)(2,1)S(1)}, u32[]{:S(2)}, u32[]{:S(2)}) collective-permute-start(bf16[384,384]{1,0:T(8,128)(2,1)S(1)} %collective-permute-done.16.refs_14_), channel_id=1, source_target_pairs={{0,8},{1,9},{2,10},{3,11},{4,12},{5,13},{6,14},{7,15},{8,0},{9,1},... | collective-permute-start | bytes 884744 | tf_op jit(solution)/shard_map/ppermute | solution.py:26
  121.8 13.0 %collective-permute-start.15 = (bf16[384,384]{1,0:T(8,128)(2,1)S(1)}, bf16[384,384]{1,0:T(8,128)(2,1)S(1)}, u32[]{:S(2)}, u32[]{:S(2)}) collective-permute-start(bf16[384,384]{1,0:T(8,128)(2,1)S(1)} %collective-permute-done.14.refs_12_), channel_id=1, source_target_pairs={{0,8},{1,9},{2,10},{3,11},{4,12},{5,13},{6,14},{7,15},{8,0},{9,1},... | collective-permute-start | bytes 884744 | tf_op jit(solution)/shard_map/ppermute | solution.py:26
  124.3 10.6 %collective-permute-start.13 = (bf16[384,384]{1,0:T(8,128)(2,1)S(1)}, bf16[384,384]{1,0:T(8,128)(2,1)S(1)}, u32[]{:S(2)}, u32[]{:S(2)}) collective-permute-start(bf16[384,384]{1,0:T(8,128)(2,1)S(1)} %collective-permute-done.12.refs_10_), channel_id=1, source_target_pairs={{0,8},{1,9},{2,10},{3,11},{4,12},{5,13},{6,14},{7,15},{8,0},{9,1},... | collective-permute-start | bytes 884744 | tf_op jit(solution)/shard_map/ppermute | solution.py:26
  126.9 8.0 %collective-permute-start.4 = (bf16[32,3072]{1,0:T(8,128)(2,1)S(1)}, bf16[32,3072]{1,0:T(8,128)(2,1)}, u32[]{:S(2)}, u32[]{:S(2)}) collective-permute-start(bf16[32,3072]{1,0:T(8,128)(2,1)S(1)} %collective-permute-done.3.refs_4_), channel_id=1, source_target_pairs={{0,2},{1,3},{2,0},{3,1},{4,6},{5,7},{6,4},{7,5},{8,10},{9,11},{10,... | collective-permute-start | bytes 589832 | tf_op jit(solution)/shard_map/ppermute | solution.py:26
  128.9 6.0 %copy-start.8 = (bf16[32,3072]{1,0:T(8,128)(2,1)S(1)}, bf16[32,3072]{1,0:T(8,128)(2,1)}, u32[]{:S(2)}) copy-start(bf16[32,3072]{1,0:T(8,128)(2,1)} %copy-done.7) | copy-start | bytes 589828
  128.9 6.0 %copy-start.10 = (bf16[32,3072]{1,0:T(8,128)(2,1)S(1)}, bf16[32,3072]{1,0:T(8,128)(2,1)}, u32[]{:S(2)}) copy-start(bf16[32,3072]{1,0:T(8,128)(2,1)} %copy-done.9) | copy-start | bytes 589828
  (6 other events, 14.7 us)

commit v2 on v1

--- a/solution.py
+++ b/solution.py
@@ -26,6 +26,22 @@
     return lax.ppermute(value, AXES, exchange(**moves))
 
 
+def after(*values):
+    return lax.optimization_barrier(values)
+
+
+def quarter_turn(value):
+    pairs = []
+    for dp in range(NY * NZ * NC):
+        y, z, core = dp // (NZ * NC), dp // NC % NZ, dp % NC
+        for mp in range(NX * NH):
+            x, half = mp // NH, mp % NH
+            ring = (half * NZ + z + (1 - 2 * core) * (NZ // 2)) % (NH * NZ)
+            target = (y * NZ + ring % NZ) * NC + core
+            pairs.append((dp * NX * NH + mp, target * NX * NH + x * NH + ring // NZ))
+    return lax.ppermute(value, AXES, pairs)
+
+
 def nt(a, b):
     return lax.dot_general(a, b, (((1,), (1,)), ((), ())), preferred_element_type=jnp.float32)
 
@@ -36,6 +52,15 @@
 
 def nn(a, b):
     return lax.dot_general(a, b, (((1,), (0,)), ((), ())), preferred_element_type=jnp.float32)
+
+
+def reorder_kernel(y_ref, source_ref, in_ref, out_ref):
+    span = source_ref.shape[1]
+    wanted = lax.broadcasted_iota(jnp.int32, (span, span), 0) == source_ref[...]
+    pick = jnp.where(wanted, 1.0, 0.0).astype(jnp.bfloat16)
+    for i in range(NY):
+        start = pl.multiple_of((y_ref[0] ^ i) * span, span)
+        out_ref[:, i * span:(i + 1) * span] = nn(in_ref[:, pl.ds(start, span)], pick).astype(jnp.bfloat16)
 
 
 def attention_kernel(q_ref, k_ref, out_ref):
@@ -78,7 +103,7 @@
 
 VMEM = pl.BlockSpec(memory_space=pltpu.VMEM)
 SMEM = pl.BlockSpec(memory_space=pltpu.SMEM)
-PARAMS = pltpu.CompilerParams(vmem_limit_bytes=24 * 1024 * 1024)
+PARAMS = pltpu.CompilerParams(vmem_limit_bytes=16 * 1024 * 1024)
 
 
 def shards(queries, attn_keys, attn_values, out_weight, grad_out):
@@ -96,26 +121,31 @@
     z_xor = sum(((z_bits >> b) & 1) << (3 - b) for b in range(4))
     core_xor = place // (NZ * block)
     source = ((jnp.asarray(z_xor) ^ z) * NC + (jnp.asarray(core_xor) ^ core)) * block + jnp.asarray(place % block)
-    pick = (jnp.arange(span)[:, None] == source[None, :]).astype(jnp.bfloat16)
-    grads = jnp.dot(
-        grad_out.reshape(part * NY, span), pick, preferred_element_type=jnp.float32
-    ).astype(jnp.bfloat16).reshape(part, 2, 2, span)
-    grads = jnp.where((y & 2) != 0, jnp.flip(grads, 1), grads)
-    grads = jnp.where((y & 1) != 0, jnp.flip(grads, 2), grads)
-    own = grads.reshape(part, model)
+    own = pl.pallas_call(
+        reorder_kernel,
+        out_shape=jax.ShapeDtypeStruct((part, model), jnp.bfloat16),
+        in_specs=[SMEM, VMEM, VMEM],
+        out_specs=VMEM,
+        compiler_params=PARAMS,
+        cost_estimate=pl.CostEstimate(flops=2 * part * model * span, bytes_accessed=4 * part * model, transcendentals=0),
+    )(y.reshape(1), source.astype(jnp.int32).reshape(1, span), grad_out.reshape(part, model))
 
     weight = out_weight
-    weight = jnp.concatenate([weight, swap(weight, z=8)], 0)
+    arrived = swap(weight, z=8)
+    half_way = quarter_turn(own)
+    own, arrived = after(own, arrived)
+    weight = jnp.concatenate([weight, arrived], 0)
     weight = jnp.concatenate([weight, swap(weight, z=4)], 0)
+    pieces = [own] + [swap(own, x=i) for i in (1, 2, 3)]
+    weight, half_way = after(weight, half_way)
+    far = quarter_turn(half_way)
     weight = jnp.concatenate([weight, swap(weight, z=2)], 0)
     weight = jnp.concatenate([weight, swap(weight, z=1)], 0)
+    weight, far = after(weight, far)
     by_y = [weight] + [swap(weight, y=i) for i in (1, 2, 3)]
     weights = []
     for piece in by_y:
         weights += [piece, swap(piece, core=1)]
-
-    far = swap(own, half=1)
-    pieces = [own] + [swap(own, x=i) for i in (1, 2, 3)]
     pieces += [far] + [swap(far, x=i) for i in (1, 2, 3)]
     rows = jnp.stack([mp ^ (i * NH + h) for h in range(NH) for i in range(NX)]).astype(jnp.int32)
 

time: 140 us -> 137 us (0.979)
  waiting for transfers between devices: 41.4 us -> 28.9 us
  starting transfers between devices: 84.9 us -> 97.3 us
  local copies, waits for them, and re-layouts: 5.23 us -> 3.76 us
    ppermute x0 -> x2, starting transfers between devices: none -> 27.3 us  [quarter_turn(): return lax.ppermute(value, AXES, pairs)]
    ppermute x18 -> x17, waiting for transfers between devices: 41.4 us -> 26 us  [swap(): return lax.ppermute(value, AXES, exchange(**moves))]
    ppermute x18 -> x17, starting transfers between devices: 84.9 us -> 70 us  [swap(): return lax.ppermute(value, AXES, exchange(**moves))]
    ppermute x0 -> x2, waiting for transfers between devices: none -> 2.97 us  [quarter_turn(): return lax.ppermute(value, AXES, pairs)]
  transfers between devices with their start and end apart: 18 -> 19, of which waited for: 5 -> 5; matrix products, arithmetic and copies ran while one was open for 3% -> 0% of each run, Pallas kernels for 0% -> 1%
where the time goes in v2:
time: 137 us
  starting transfers between devices  97.3 us (71%)
  waiting for transfers between devices  28.9 us (21%)
  Pallas kernels  5.33 us (4%)
  local copies, waits for them, and re-layouts  3.76 us (3%)
    ppermute x17, starting transfers between devices, swap(): return lax.ppermute(value, AXES, exchange(**moves))  70 us
    ppermute x2, starting transfers between devices, quarter_turn(): return lax.ppermute(value, AXES, pairs)  27.3 us
    ppermute x17, waiting for transfers between devices, swap(): return lax.ppermute(value, AXES, exchange(**moves))  26 us
    pallas_call x1, Pallas kernels, shards(): pl.pallas_call(tail_kernel, out_shape=(grad_shape,) * 3, in_specs=[SMEM]...  3.93 us
    unnamed x28, local copies, waits for them, and re-layouts  3.67 us
    ppermute x2, waiting for transfers between devices, quarter_turn(): return lax.ppermute(value, AXES, pairs)  2.97 us
  transfers between devices with their start and end apart: 19, of which 5 were waited for; matrix products, arithmetic and copies ran while one was open for 0% of the time, Pallas kernels for 1%

profile of v2, /device:TPU:1, one launch (start us, length us, event | category | flops | bytes accessed | tf_op | source)
XLA Modules:
  0.0 136.5 jit_solution(5167951548669401226)
XLA Ops:
  0.6 16.3 %collective-permute-start = (bf16[24,384]{1,0:T(8,128)(2,1)}, bf16[24,384]{1,0:T(8,128)(2,1)S(1)}, u32[]{:S(2)}, u32[]{:S(2)}) collective-permute-start(bf16[24,384]{1,0:T(8,128)(2,1)} %param.11), channel_id=1, source_target_pairs={{0,128},{1,129},{2,130},{3,131},{4,132},{5,133},{6,134},{7,135},{8... | collective-permute-start | bytes 55304 | tf_op jit(solution)/shard_map/ppermute | solution.py:26
  19.6 15.5 %collective-permute-start.5 = (bf16[32,3072]{1,0:T(8,128)(2,1)S(1)}, bf16[32,3072]{1,0:T(8,128)(2,1)S(1)}, u32[]{:S(2)}, u32[]{:S(2)}) collective-permute-start(bf16[32,3072]{1,0:T(8,128)(2,1)S(1)} %shard_map.104.refs_0_), channel_id=1, source_target_pairs={{0,128},{1,129},{2,130},{3,131},{4,132},{5,133},{6,134},{7,135},{8... | collective-permute-start | bytes 589832 | tf_op jit(solution)/shard_map/ppermute | solution.py:42
  35.0 4.0 %collective-permute-start.4 = (bf16[48,384]{1,0:T(8,128)(2,1)S(1)}, bf16[48,384]{1,0:T(8,128)(2,1)S(1)}, u32[]{:S(2)}, u32[]{:S(2)}) collective-permute-start(bf16[48,384]{1,0:T(8,128)(2,1)S(1)} %pad_maximum_fusion.3), channel_id=1, source_target_pairs={{0,64},{1,65},{2,66},{3,67},{4,68},{5,69},{6,70},{7,71},{8,72},{9,... | collective-permute-start | bytes 110600 | tf_op jit(solution)/shard_map/ppermute | solution.py:26
  39.1 13.5 %collective-permute-done.4 = bf16[48,384]{1,0:T(8,128)(2,1)S(1)} collective-permute-done((bf16[48,384]{1,0:T(8,128)(2,1)S(1)}, bf16[48,384]{1,0:T(8,128)(2,1)S(1)}, u32[]{:S(2)}, u32[]{:S(2)}) %collective-permute-start.4) | collective-permute-done | bytes 36896 | tf_op jit(solution)/shard_map/ppermute | solution.py:26
  52.6 1.9 %collective-permute-start.6 = (bf16[96,384]{1,0:T(8,128)(2,1)S(1)}, bf16[96,384]{1,0:T(8,128)(2,1)S(1)}, u32[]{:S(2)}, u32[]{:S(2)}) collective-permute-start(bf16[96,384]{1,0:T(8,128)(2,1)S(1)} %pad_maximum_fusion.2), channel_id=1, source_target_pairs={{0,32},{1,33},{2,34},{3,35},{4,36},{5,37},{6,38},{7,39},{8,40},{9,... | collective-permute-start | bytes 221192 | tf_op jit(solution)/shard_map/ppermute | solution.py:26
  54.5 5.5 %collective-permute-done.6 = bf16[96,384]{1,0:T(8,128)(2,1)S(1)} collective-permute-done((bf16[96,384]{1,0:T(8,128)(2,1)S(1)}, bf16[96,384]{1,0:T(8,128)(2,1)S(1)}, u32[]{:S(2)}, u32[]{:S(2)}) %collective-permute-start.6) | collective-permute-done | bytes 73760 | tf_op jit(solution)/shard_map/ppermute | solution.py:26
  60.1 2.1 %collective-permute-start.7 = (bf16[192,384]{1,0:T(8,128)(2,1)S(1)}, bf16[192,384]{1,0:T(8,128)(2,1)S(1)}, u32[]{:S(2)}, u32[]{:S(2)}) collective-permute-start(bf16[192,384]{1,0:T(8,128)(2,1)S(1)} %pad_maximum_fusion.1), channel_id=1, source_target_pairs={{0,16},{1,17},{2,18},{3,19},{4,20},{5,21},{6,22},{7,23},{8,24},{9,... | collective-permute-start | bytes 442376 | tf_op jit(solution)/shard_map/ppermute | solution.py:26
  62.1 11.9 %collective-permute-start.8 = (bf16[32,3072]{1,0:T(8,128)(2,1)S(1)}, bf16[32,3072]{1,0:T(8,128)(2,1)S(1)}, u32[]{:S(2)}, u32[]{:S(2)}) collective-permute-start(bf16[32,3072]{1,0:T(8,128)(2,1)S(1)} %collective-permute-done.5), channel_id=1, source_target_pairs={{0,128},{1,129},{2,130},{3,131},{4,132},{5,133},{6,134},{7,135},{8... | collective-permute-start | bytes 589832 | tf_op jit(solution)/shard_map/ppermute | solution.py:42
  74.0 4.4 %collective-permute-start.3 = (bf16[32,3072]{1,0:T(8,128)(2,1)S(1)}, bf16[32,3072]{1,0:T(8,128)(2,1)S(1)}, u32[]{:S(2)}, u32[]{:S(2)}) collective-permute-start(bf16[32,3072]{1,0:T(8,128)(2,1)S(1)} %shard_map.104.refs_0_), channel_id=1, source_target_pairs={{0,6},{1,7},{2,4},{3,5},{4,2},{5,3},{6,0},{7,1},{8,14},{9,15},{10,... | collective-permute-start | bytes 589832 | tf_op jit(solution)/shard_map/ppermute | solution.py:26
  78.4 2.4 %collective-permute-start.2 = (bf16[32,3072]{1,0:T(8,128)(2,1)S(1)}, bf16[32,3072]{1,0:T(8,128)(2,1)S(1)}, u32[]{:S(2)}, u32[]{:S(2)}) collective-permute-start(bf16[32,3072]{1,0:T(8,128)(2,1)S(1)} %shard_map.104.refs_0_), channel_id=1, source_target_pairs={{0,4},{1,5},{2,6},{3,7},{4,0},{5,1},{6,2},{7,3},{8,12},{9,13},{10,... | collective-permute-start | bytes 589832 | tf_op jit(solution)/shard_map/ppermute | solution.py:26
  80.8 2.2 %collective-permute-start.1 = (bf16[32,3072]{1,0:T(8,128)(2,1)S(1)}, bf16[32,3072]{1,0:T(8,128)(2,1)S(1)}, u32[]{:S(2)}, u32[]{:S(2)}) collective-permute-start(bf16[32,3072]{1,0:T(8,128)(2,1)S(1)} %shard_map.104.refs_0_), channel_id=1, source_target_pairs={{0,2},{1,3},{2,0},{3,1},{4,6},{5,7},{6,4},{7,5},{8,10},{9,11},{10,... | collective-permute-start | bytes 589832 | tf_op jit(solution)/shard_map/ppermute | solution.py:26
  83.1 3.0 %collective-permute-done.8.refs_4_ = bf16[32,3072]{1,0:T(8,128)(2,1)S(1)} collective-permute-done((bf16[32,3072]{1,0:T(8,128)(2,1)S(1)}, bf16[32,3072]{1,0:T(8,128)(2,1)S(1)}, u32[]{:S(2)}, u32[]{:S(2)}) %collective-permute-start.8) | collective-permute-done | bytes 196640 | tf_op jit(solution)/shard_map/ppermute | solution.py:42
  86.0 9.9 %collective-permute-start.17 = (bf16[384,384]{1,0:T(8,128)(2,1)S(1)}, bf16[384,384]{1,0:T(8,128)(2,1)S(1)}, u32[]{:S(2)}, u32[]{:S(2)}) collective-permute-start(bf16[384,384]{1,0:T(8,128)(2,1)S(1)} %pad_maximum_fusion.refs_8_), channel_id=1, source_target_pairs={{0,768},{1,769},{2,770},{3,771},{4,772},{5,773},{6,774},{7,775},{8... | collective-permute-start | bytes 884744 | tf_op jit(solution)/shard_map/ppermute | solution.py:26
  95.9 2.3 %collective-permute-start.15 = (bf16[384,384]{1,0:T(8,128)(2,1)S(1)}, bf16[384,384]{1,0:T(8,128)(2,1)S(1)}, u32[]{:S(2)}, u32[]{:S(2)}) collective-permute-start(bf16[384,384]{1,0:T(8,128)(2,1)S(1)} %pad_maximum_fusion.refs_8_), channel_id=1, source_target_pairs={{0,512},{1,513},{2,514},{3,515},{4,516},{5,517},{6,518},{7,519},{8... | collective-permute-start | bytes 884744 | tf_op jit(solution)/shard_map/ppermute | solution.py:26
  98.2 2.1 %collective-permute-start.13 = (bf16[384,384]{1,0:T(8,128)(2,1)S(1)}, bf16[384,384]{1,0:T(8,128)(2,1)S(1)}, u32[]{:S(2)}, u32[]{:S(2)}) collective-permute-start(bf16[384,384]{1,0:T(8,128)(2,1)S(1)} %pad_maximum_fusion.refs_8_), channel_id=1, source_target_pairs={{0,256},{1,257},{2,258},{3,259},{4,260},{5,261},{6,262},{7,263},{8... | collective-permute-start | bytes 884744 | tf_op jit(solution)/shard_map/ppermute | solution.py:26
  100.3 4.4 %collective-permute-start.11 = (bf16[32,3072]{1,0:T(8,128)(2,1)S(1)}, bf16[32,3072]{1,0:T(8,128)(2,1)S(1)}, u32[]{:S(2)}, u32[]{:S(2)}) collective-permute-start(bf16[32,3072]{1,0:T(8,128)(2,1)S(1)} %collective-permute-done.8.refs_4_), channel_id=1, source_target_pairs={{0,6},{1,7},{2,4},{3,5},{4,2},{5,3},{6,0},{7,1},{8,14},{9,15},{10,... | collective-permute-start | bytes 589832 | tf_op jit(solution)/shard_map/ppermute | solution.py:26
  105.4 2.4 %collective-permute-start.10 = (bf16[32,3072]{1,0:T(8,128)(2,1)S(1)}, bf16[32,3072]{1,0:T(8,128)(2,1)S(1)}, u32[]{:S(2)}, u32[]{:S(2)}) collective-permute-start(bf16[32,3072]{1,0:T(8,128)(2,1)S(1)} %collective-permute-done.8.refs_4_), channel_id=1, source_target_pairs={{0,4},{1,5},{2,6},{3,7},{4,0},{5,1},{6,2},{7,3},{8,12},{9,13},{10,... | collective-permute-start | bytes 589832 | tf_op jit(solution)/shard_map/ppermute | solution.py:26
  110.0 7.5 %collective-permute-start.12 = (bf16[384,384]{1,0:T(8,128)(2,1)S(1)}, bf16[384,384]{1,0:T(8,128)(2,1)S(1)}, u32[]{:S(2)}, u32[]{:S(2)}) collective-permute-start(bf16[384,384]{1,0:T(8,128)(2,1)S(1)} %pad_maximum_fusion.refs_8_), channel_id=1, source_target_pairs={{0,8},{1,9},{2,10},{3,11},{4,12},{5,13},{6,14},{7,15},{8,0},{9,1},... | collective-permute-start | bytes 884744 | tf_op jit(solution)/shard_map/ppermute | solution.py:26
  117.6 1.9 %collective-permute-start.18 = (bf16[384,384]{1,0:T(8,128)(2,1)S(1)}, bf16[384,384]{1,0:T(8,128)(2,1)S(1)}, u32[]{:S(2)}, u32[]{:S(2)}) collective-permute-start(bf16[384,384]{1,0:T(8,128)(2,1)S(1)} %collective-permute-done.17.refs_14_), channel_id=1, source_target_pairs={{0,8},{1,9},{2,10},{3,11},{4,12},{5,13},{6,14},{7,15},{8,0},{9,1},... | collective-permute-start | bytes 884744 | tf_op jit(solution)/shard_map/ppermute | solution.py:26
  119.5 2.4 %collective-permute-start.16 = (bf16[384,384]{1,0:T(8,128)(2,1)S(1)}, bf16[384,384]{1,0:T(8,128)(2,1)S(1)}, u32[]{:S(2)}, u32[]{:S(2)}) collective-permute-start(bf16[384,384]{1,0:T(8,128)(2,1)S(1)} %collective-permute-done.15.refs_12_), channel_id=1, source_target_pairs={{0,8},{1,9},{2,10},{3,11},{4,12},{5,13},{6,14},{7,15},{8,0},{9,1},... | collective-permute-start | bytes 884744 | tf_op jit(solution)/shard_map/ppermute | solution.py:26
  121.9 1.9 %collective-permute-start.14 = (bf16[384,384]{1,0:T(8,128)(2,1)S(1)}, bf16[384,384]{1,0:T(8,128)(2,1)S(1)}, u32[]{:S(2)}, u32[]{:S(2)}) collective-permute-start(bf16[384,384]{1,0:T(8,128)(2,1)S(1)} %collective-permute-done.13.refs_10_), channel_id=1, source_target_pairs={{0,8},{1,9},{2,10},{3,11},{4,12},{5,13},{6,14},{7,15},{8,0},{9,1},... | collective-permute-start | bytes 884744 | tf_op jit(solution)/shard_map/ppermute | solution.py:26
  124.6 1.9 %collective-permute-start.9 = (bf16[32,3072]{1,0:T(8,128)(2,1)S(1)}, bf16[32,3072]{1,0:T(8,128)(2,1)}, u32[]{:S(2)}, u32[]{:S(2)}) collective-permute-start(bf16[32,3072]{1,0:T(8,128)(2,1)S(1)} %collective-permute-done.8.refs_4_), channel_id=1, source_target_pairs={{0,2},{1,3},{2,0},{3,1},{4,6},{5,7},{6,4},{7,5},{8,10},{9,11},{10,... | collective-permute-start | bytes 589832 | tf_op jit(solution)/shard_map/ppermute | solution.py:26
  127.1 5.4 %collective-permute-done.9.refs_5_ = bf16[32,3072]{1,0:T(8,128)(2,1)} collective-permute-done((bf16[32,3072]{1,0:T(8,128)(2,1)S(1)}, bf16[32,3072]{1,0:T(8,128)(2,1)}, u32[]{:S(2)}, u32[]{:S(2)}) %collective-permute-start.9) | collective-permute-done | bytes 196640 | tf_op jit(solution)/shard_map/ppermute | solution.py:26
  132.6 3.9 %shard_map.105 = (bf16[256,384]{1,0:T(8,128)(2,1)}, bf16[256,384]{1,0:T(8,128)(2,1)}, bf16[256,384]{1,0:T(8,128)(2,1)}) custom-call(s32[8]{0:T(128)S(1)} %stack.35.rows_ref, f32[3,256,256]{2,1,0:T(8,128)S(1)} %shard_map.103.attn_ref, bf16[256,384]{1,0:T(8,128)(2,1)S(1)} %bitcast.17, bf16[256,384]{1,0:T(8,128)(2,1)S(1)} %bitcast.19, ...), custom_call_target="tpu_custom_call" | custom-call | flops 805306368 | bytes 6291456 | tf_op jit(solution)/shard_map/pallas_call | solution.py:161
  (52 shorter events, 6.8 us)
Async XLA Ops:
  0.6 34.4 %collective-permute-start = (bf16[24,384]{1,0:T(8,128)(2,1)}, bf16[24,384]{1,0:T(8,128)(2,1)S(1)}, u32[]{:S(2)}, u32[]{:S(2)}) collective-permute-start(bf16[24,384]{1,0:T(8,128)(2,1)} %param.11), channel_id=1, source_target_pairs={{0,128},{1,129},{2,130},{3,131},{4,132},{5,133},{6,134},{7,135},{8... | collective-permute-start | bytes 55304 | tf_op jit(solution)/shard_map/ppermute | solution.py:26
  18.6 16.4 %copy-start.10 = (bf16[24,384]{1,0:T(8,128)(2,1)S(1)}, bf16[24,384]{1,0:T(8,128)(2,1)}, u32[]{:S(2)}) copy-start(bf16[24,384]{1,0:T(8,128)(2,1)} %param.11) | copy-start | bytes 55300
  19.6 33.1 %collective-permute-start.5 = (bf16[32,3072]{1,0:T(8,128)(2,1)S(1)}, bf16[32,3072]{1,0:T(8,128)(2,1)S(1)}, u32[]{:S(2)}, u32[]{:S(2)}) collective-permute-start(bf16[32,3072]{1,0:T(8,128)(2,1)S(1)} %shard_map.104.refs_0_), channel_id=1, source_target_pairs={{0,128},{1,129},{2,130},{3,131},{4,132},{5,133},{6,134},{7,135},{8... | collective-permute-start | bytes 589832 | tf_op jit(solution)/shard_map/ppermute | solution.py:42
  35.0 17.5 %collective-permute-start.4 = (bf16[48,384]{1,0:T(8,128)(2,1)S(1)}, bf16[48,384]{1,0:T(8,128)(2,1)S(1)}, u32[]{:S(2)}, u32[]{:S(2)}) collective-permute-start(bf16[48,384]{1,0:T(8,128)(2,1)S(1)} %pad_maximum_fusion.3), channel_id=1, source_target_pairs={{0,64},{1,65},{2,66},{3,67},{4,68},{5,69},{6,70},{7,71},{8,72},{9,... | collective-permute-start | bytes 110600 | tf_op jit(solution)/shard_map/ppermute | solution.py:26
  52.6 7.4 %collective-permute-start.6 = (bf16[96,384]{1,0:T(8,128)(2,1)S(1)}, bf16[96,384]{1,0:T(8,128)(2,1)S(1)}, u32[]{:S(2)}, u32[]{:S(2)}) collective-permute-start(bf16[96,384]{1,0:T(8,128)(2,1)S(1)} %pad_maximum_fusion.2), channel_id=1, source_target_pairs={{0,32},{1,33},{2,34},{3,35},{4,36},{5,37},{6,38},{7,39},{8,40},{9,... | collective-permute-start | bytes 221192 | tf_op jit(solution)/shard_map/ppermute | solution.py:26
  60.0 66.5 %copy-start = (bf16[1,256,384]{2,1,0:T(8,128)(2,1)S(1)}, bf16[1,256,384]{2,1,0:T(8,128)(2,1)}, u32[]{:S(2)}) copy-start(bf16[1,256,384]{2,1,0:T(8,128)(2,1)} %param.8) | copy-start | bytes 589828
  60.0 66.5 %copy-start.1 = (bf16[1,256,384]{2,1,0:T(8,128)(2,1)S(1)}, bf16[1,256,384]{2,1,0:T(8,128)(2,1)}, u32[]{:S(2)}) copy-start(bf16[1,256,384]{2,1,0:T(8,128)(2,1)} %param.9) | copy-start | bytes 589828
  60.1 23.0 %collective-permute-start.7 = (bf16[192,384]{1,0:T(8,128)(2,1)S(1)}, bf16[192,384]{1,0:T(8,128)(2,1)S(1)}, u32[]{:S(2)}, u32[]{:S(2)}) collective-permute-start(bf16[192,384]{1,0:T(8,128)(2,1)S(1)} %pad_maximum_fusion.1), channel_id=1, source_target_pairs={{0,16},{1,17},{2,18},{3,19},{4,20},{5,21},{6,22},{7,23},{8,24},{9,... | collective-permute-start | bytes 442376 | tf_op jit(solution)/shard_map/ppermute | solution.py:26
  62.1 23.9 %collective-permute-start.8 = (bf16[32,3072]{1,0:T(8,128)(2,1)S(1)}, bf16[32,3072]{1,0:T(8,128)(2,1)S(1)}, u32[]{:S(2)}, u32[]{:S(2)}) collective-permute-start(bf16[32,3072]{1,0:T(8,128)(2,1)S(1)} %collective-permute-done.5), channel_id=1, source_target_pairs={{0,128},{1,129},{2,130},{3,131},{4,132},{5,133},{6,134},{7,135},{8... | collective-permute-start | bytes 589832 | tf_op jit(solution)/shard_map/ppermute | solution.py:42
  74.0 24.2 %collective-permute-start.3 = (bf16[32,3072]{1,0:T(8,128)(2,1)S(1)}, bf16[32,3072]{1,0:T(8,128)(2,1)S(1)}, u32[]{:S(2)}, u32[]{:S(2)}) collective-permute-start(bf16[32,3072]{1,0:T(8,128)(2,1)S(1)} %shard_map.104.refs_0_), channel_id=1, source_target_pairs={{0,6},{1,7},{2,4},{3,5},{4,2},{5,3},{6,0},{7,1},{8,14},{9,15},{10,... | collective-permute-start | bytes 589832 | tf_op jit(solution)/shard_map/ppermute | solution.py:26
  78.4 21.9 %collective-permute-start.2 = (bf16[32,3072]{1,0:T(8,128)(2,1)S(1)}, bf16[32,3072]{1,0:T(8,128)(2,1)S(1)}, u32[]{:S(2)}, u32[]{:S(2)}) collective-permute-start(bf16[32,3072]{1,0:T(8,128)(2,1)S(1)} %shard_map.104.refs_0_), channel_id=1, source_target_pairs={{0,4},{1,5},{2,6},{3,7},{4,0},{5,1},{6,2},{7,3},{8,12},{9,13},{10,... | collective-permute-start | bytes 589832 | tf_op jit(solution)/shard_map/ppermute | solution.py:26
  80.8 23.9 %collective-permute-start.1 = (bf16[32,3072]{1,0:T(8,128)(2,1)S(1)}, bf16[32,3072]{1,0:T(8,128)(2,1)S(1)}, u32[]{:S(2)}, u32[]{:S(2)}) collective-permute-start(bf16[32,3072]{1,0:T(8,128)(2,1)S(1)} %shard_map.104.refs_0_), channel_id=1, source_target_pairs={{0,2},{1,3},{2,0},{3,1},{4,6},{5,7},{6,4},{7,5},{8,10},{9,11},{10,... | collective-permute-start | bytes 589832 | tf_op jit(solution)/shard_map/ppermute | solution.py:26
  86.0 31.5 %collective-permute-start.17 = (bf16[384,384]{1,0:T(8,128)(2,1)S(1)}, bf16[384,384]{1,0:T(8,128)(2,1)S(1)}, u32[]{:S(2)}, u32[]{:S(2)}) collective-permute-start(bf16[384,384]{1,0:T(8,128)(2,1)S(1)} %pad_maximum_fusion.refs_8_), channel_id=1, source_target_pairs={{0,768},{1,769},{2,770},{3,771},{4,772},{5,773},{6,774},{7,775},{8... | collective-permute-start | bytes 884744 | tf_op jit(solution)/shard_map/ppermute | solution.py:26
  95.9 23.6 %collective-permute-start.15 = (bf16[384,384]{1,0:T(8,128)(2,1)S(1)}, bf16[384,384]{1,0:T(8,128)(2,1)S(1)}, u32[]{:S(2)}, u32[]{:S(2)}) collective-permute-start(bf16[384,384]{1,0:T(8,128)(2,1)S(1)} %pad_maximum_fusion.refs_8_), channel_id=1, source_target_pairs={{0,512},{1,513},{2,514},{3,515},{4,516},{5,517},{6,518},{7,519},{8... | collective-permute-start | bytes 884744 | tf_op jit(solution)/shard_map/ppermute | solution.py:26
  98.2 23.8 %collective-permute-start.13 = (bf16[384,384]{1,0:T(8,128)(2,1)S(1)}, bf16[384,384]{1,0:T(8,128)(2,1)S(1)}, u32[]{:S(2)}, u32[]{:S(2)}) collective-permute-start(bf16[384,384]{1,0:T(8,128)(2,1)S(1)} %pad_maximum_fusion.refs_8_), channel_id=1, source_target_pairs={{0,256},{1,257},{2,258},{3,259},{4,260},{5,261},{6,262},{7,263},{8... | collective-permute-start | bytes 884744 | tf_op jit(solution)/shard_map/ppermute | solution.py:26
  100.3 9.0 %collective-permute-start.11 = (bf16[32,3072]{1,0:T(8,128)(2,1)S(1)}, bf16[32,3072]{1,0:T(8,128)(2,1)S(1)}, u32[]{:S(2)}, u32[]{:S(2)}) collective-permute-start(bf16[32,3072]{1,0:T(8,128)(2,1)S(1)} %collective-permute-done.8.refs_4_), channel_id=1, source_target_pairs={{0,6},{1,7},{2,4},{3,5},{4,2},{5,3},{6,0},{7,1},{8,14},{9,15},{10,... | collective-permute-start | bytes 589832 | tf_op jit(solution)/shard_map/ppermute | solution.py:26
  105.4 18.4 %collective-permute-start.10 = (bf16[32,3072]{1,0:T(8,128)(2,1)S(1)}, bf16[32,3072]{1,0:T(8,128)(2,1)S(1)}, u32[]{:S(2)}, u32[]{:S(2)}) collective-permute-start(bf16[32,3072]{1,0:T(8,128)(2,1)S(1)} %collective-permute-done.8.refs_4_), channel_id=1, source_target_pairs={{0,4},{1,5},{2,6},{3,7},{4,0},{5,1},{6,2},{7,3},{8,12},{9,13},{10,... | collective-permute-start | bytes 589832 | tf_op jit(solution)/shard_map/ppermute | solution.py:26
  110.0 22.5 %collective-permute-start.12 = (bf16[384,384]{1,0:T(8,128)(2,1)S(1)}, bf16[384,384]{1,0:T(8,128)(2,1)S(1)}, u32[]{:S(2)}, u32[]{:S(2)}) collective-permute-start(bf16[384,384]{1,0:T(8,128)(2,1)S(1)} %pad_maximum_fusion.refs_8_), channel_id=1, source_target_pairs={{0,8},{1,9},{2,10},{3,11},{4,12},{5,13},{6,14},{7,15},{8,0},{9,1},... | collective-permute-start | bytes 884744 | tf_op jit(solution)/shard_map/ppermute | solution.py:26
  117.6 14.9 %collective-permute-start.18 = (bf16[384,384]{1,0:T(8,128)(2,1)S(1)}, bf16[384,384]{1,0:T(8,128)(2,1)S(1)}, u32[]{:S(2)}, u32[]{:S(2)}) collective-permute-start(bf16[384,384]{1,0:T(8,128)(2,1)S(1)} %collective-permute-done.17.refs_14_), channel_id=1, source_target_pairs={{0,8},{1,9},{2,10},{3,11},{4,12},{5,13},{6,14},{7,15},{8,0},{9,1},... | collective-permute-start | bytes 884744 | tf_op jit(solution)/shard_map/ppermute | solution.py:26
  119.5 13.0 %collective-permute-start.16 = (bf16[384,384]{1,0:T(8,128)(2,1)S(1)}, bf16[384,384]{1,0:T(8,128)(2,1)S(1)}, u32[]{:S(2)}, u32[]{:S(2)}) collective-permute-start(bf16[384,384]{1,0:T(8,128)(2,1)S(1)} %collective-permute-done.15.refs_12_), channel_id=1, source_target_pairs={{0,8},{1,9},{2,10},{3,11},{4,12},{5,13},{6,14},{7,15},{8,0},{9,1},... | collective-permute-start | bytes 884744 | tf_op jit(solution)/shard_map/ppermute | solution.py:26
  121.9 10.6 %collective-permute-start.14 = (bf16[384,384]{1,0:T(8,128)(2,1)S(1)}, bf16[384,384]{1,0:T(8,128)(2,1)S(1)}, u32[]{:S(2)}, u32[]{:S(2)}) collective-permute-start(bf16[384,384]{1,0:T(8,128)(2,1)S(1)} %collective-permute-done.13.refs_10_), channel_id=1, source_target_pairs={{0,8},{1,9},{2,10},{3,11},{4,12},{5,13},{6,14},{7,15},{8,0},{9,1},... | collective-permute-start | bytes 884744 | tf_op jit(solution)/shard_map/ppermute | solution.py:26
  124.6 8.0 %collective-permute-start.9 = (bf16[32,3072]{1,0:T(8,128)(2,1)S(1)}, bf16[32,3072]{1,0:T(8,128)(2,1)}, u32[]{:S(2)}, u32[]{:S(2)}) collective-permute-start(bf16[32,3072]{1,0:T(8,128)(2,1)S(1)} %collective-permute-done.8.refs_4_), channel_id=1, source_target_pairs={{0,2},{1,3},{2,0},{3,1},{4,6},{5,7},{6,4},{7,5},{8,10},{9,11},{10,... | collective-permute-start | bytes 589832 | tf_op jit(solution)/shard_map/ppermute | solution.py:26
  126.6 6.0 %copy-start.2 = (bf16[1,256,384]{2,1,0:T(8,128)(2,1)S(1)}, bf16[1,256,384]{2,1,0:T(8,128)(2,1)}, u32[]{:S(2)}) copy-start(bf16[1,256,384]{2,1,0:T(8,128)(2,1)} %param.10) | copy-start | bytes 589828
  126.6 6.0 %copy-start.4 = (bf16[32,3072]{1,0:T(8,128)(2,1)S(1)}, bf16[32,3072]{1,0:T(8,128)(2,1)}, u32[]{:S(2)}) copy-start(bf16[32,3072]{1,0:T(8,128)(2,1)} %copy-done.3) | copy-start | bytes 589828
  (9 other events, 17.0 us)

commit v3 on v2

--- a/solution.py
+++ b/solution.py
@@ -11,6 +11,7 @@
 HD = 128
 AXES = ("dp", "mp")
 NY, NZ, NC, NX, NH = 4, 16, 2, 4, 2
+Y_ORDER = (0, 2, 1, 3)
 
 
 def exchange(y=0, z=0, core=0, x=0, half=0):
@@ -24,6 +25,11 @@
 
 def swap(value, **moves):
     return lax.ppermute(value, AXES, exchange(**moves))
+
+
+def gather_x(value):
+    groups = [[i * NH + h for i in range(NX)] for h in range(NH)]
+    return lax.all_gather(value, "mp", axis_index_groups=groups, axis=0, tiled=True)
 
 
 def after(*values):
@@ -58,9 +64,9 @@
     span = source_ref.shape[1]
     wanted = lax.broadcasted_iota(jnp.int32, (span, span), 0) == source_ref[...]
     pick = jnp.where(wanted, 1.0, 0.0).astype(jnp.bfloat16)
-    for i in range(NY):
+    for slot, i in enumerate(Y_ORDER):
         start = pl.multiple_of((y_ref[0] ^ i) * span, span)
-        out_ref[:, i * span:(i + 1) * span] = nn(in_ref[:, pl.ds(start, span)], pick).astype(jnp.bfloat16)
+        out_ref[:, slot * span:(slot + 1) * span] = nn(in_ref[:, pl.ds(start, span)], pick).astype(jnp.bfloat16)
 
 
 def attention_kernel(q_ref, k_ref, out_ref):
@@ -72,18 +78,16 @@
         out_ref[head] = raised / jnp.sum(raised, axis=-1, keepdims=True)
 
 
-def tail_kernel(rows_ref, attn_ref, q_ref, k_ref, v_ref, *refs):
-    n_g = NX * NH
-    n_w = NY * NC
-    g_refs, w_refs = refs[:n_g], refs[n_g:n_g + n_w]
-    gq_ref, gk_ref, gv_ref, grad_ref = refs[n_g + n_w:]
+def tail_kernel(rows_ref, attn_ref, q_ref, k_ref, v_ref, own_ref, far_ref, w_ref, wc_ref, *refs):
+    gq_ref, gk_ref, gv_ref, grad_ref = refs
     scale = 1.0 / math.sqrt(HD)
-    part, depth = g_refs[0].shape[0], w_refs[0].shape[0]
+    n_g, depth = NX * NH, w_ref.shape[0] // NY
+    part = q_ref.shape[0] // n_g
+    parts = [ref[i * depth:(i + 1) * depth] for i in range(NY) for ref in (w_ref, wc_ref)]
+    left = jnp.concatenate([own_ref[...], far_ref[...]], axis=0)
     total = None
-    for piece in range(n_w):
-        cols = pl.ds(piece * depth, depth)
-        left = jnp.concatenate([g[:, cols] for g in g_refs], axis=0)
-        term = nn(left, w_refs[piece][...])
+    for i, piece in enumerate(parts):
+        term = nn(left[:, i * depth:(i + 1) * depth], piece)
         total = term if total is None else total + term
     total = total.astype(jnp.bfloat16)
     for slot in range(n_g):
@@ -130,25 +134,6 @@
         cost_estimate=pl.CostEstimate(flops=2 * part * model * span, bytes_accessed=4 * part * model, transcendentals=0),
     )(y.reshape(1), source.astype(jnp.int32).reshape(1, span), grad_out.reshape(part, model))
 
-    weight = out_weight
-    arrived = swap(weight, z=8)
-    half_way = quarter_turn(own)
-    own, arrived = after(own, arrived)
-    weight = jnp.concatenate([weight, arrived], 0)
-    weight = jnp.concatenate([weight, swap(weight, z=4)], 0)
-    pieces = [own] + [swap(own, x=i) for i in (1, 2, 3)]
-    weight, half_way = after(weight, half_way)
-    far = quarter_turn(half_way)
-    weight = jnp.concatenate([weight, swap(weight, z=2)], 0)
-    weight = jnp.concatenate([weight, swap(weight, z=1)], 0)
-    weight, far = after(weight, far)
-    by_y = [weight] + [swap(weight, y=i) for i in (1, 2, 3)]
-    weights = []
-    for piece in by_y:
-        weights += [piece, swap(piece, core=1)]
-    pieces += [far] + [swap(far, x=i) for i in (1, 2, 3)]
-    rows = jnp.stack([mp ^ (i * NH + h) for h in range(NH) for i in range(NX)]).astype(jnp.int32)
-
     attn = pl.pallas_call(
         attention_kernel,
         out_shape=jax.ShapeDtypeStruct((heads, patches, patches), jnp.float32),
@@ -157,16 +142,34 @@
         compiler_params=PARAMS,
         cost_estimate=pl.CostEstimate(flops=2 * patches * patches * width, bytes_accessed=1 << 20, transcendentals=0),
     )(q, k)
+    weight = out_weight
+    arrived = swap(weight, z=8)
+    half_way = quarter_turn(own)
+    own, arrived = after(own, arrived)
+    weight = jnp.concatenate([weight, arrived], 0)
+    weight = jnp.concatenate([weight, swap(weight, z=4)], 0)
+    own = gather_x(own)
+    weight, half_way, own = after(weight, half_way, own)
+    far = quarter_turn(half_way)
+    weight = jnp.concatenate([weight, swap(weight, z=2)], 0)
+    weight = jnp.concatenate([weight, swap(weight, z=1)], 0)
+    weight = jnp.concatenate([weight] + [swap(weight, y=i) for i in Y_ORDER[1:]], 0)
+    far = gather_x(far)
+    weight, far, attn = after(weight, far, attn)
+    weights = [weight, swap(weight, core=1)]
+    half = mp % NH
+    rows = jnp.stack([i * NH + h for h in (half, 1 - half) for i in range(NX)]).astype(jnp.int32)
+
     grad_shape = jax.ShapeDtypeStruct((patches, width), jnp.bfloat16)
     outs = pl.pallas_call(
         tail_kernel,
         out_shape=(grad_shape,) * 3,
-        in_specs=[SMEM] + [VMEM] * (4 + len(pieces) + len(weights)),
+        in_specs=[SMEM] + [VMEM] * (6 + len(weights)),
         out_specs=(VMEM,) * 3,
         scratch_shapes=[pltpu.VMEM((patches, width), jnp.bfloat16)],
         compiler_params=PARAMS,
         cost_estimate=pl.CostEstimate(flops=2 * patches * width * (model + 4 * patches), bytes_accessed=6 << 20, transcendentals=0),
-    )(rows, attn, q, k, v, *pieces, *weights)
+    )(rows, attn, q, k, v, own, far, *weights)
     return tuple(o.reshape(1, patches, width) for o in outs)
 
 

time: 137 us -> 120 us (0.88)
  the two profiles are of different devices: /device:TPU:1 before, /device:TPU:65 now
where the time goes in v3:
time: 120 us
  starting transfers between devices  74.1 us (62%)
  blocking collectives  29.1 us (24%)
  Pallas kernels  5.67 us (5%)
  waiting for transfers between devices  4.44 us (4%)
  local copies, waits for them, and re-layouts  4.04 us (3%)
  other arithmetic  1.49 us (1%)
    ppermute x8, starting transfers between devices, swap(): return lax.ppermute(value, AXES, exchange(**moves))  49.1 us
    all_gather x2, blocking collectives, gather_x(): lax.all_gather(value, 'mp', axis_index_groups=groups, axis=0, tiled=True)  29.1 us
    ppermute x2, starting transfers between devices, quarter_turn(): return lax.ppermute(value, AXES, pairs)  25 us
    ppermute x8, waiting for transfers between devices, swap(): return lax.ppermute(value, AXES, exchange(**moves))  4.44 us
    pallas_call x1, Pallas kernels, shards(): pl.pallas_call(tail_kernel, out_shape=(grad_shape,) * 3, in_specs=[SMEM]...  4.26 us
    unnamed x18, local copies, waits for them, and re-layouts  3.85 us
  transfers between devices with their start and end apart: 10, of which 2 were waited for; matrix products, arithmetic and copies ran while one was open for 1% of the time, Pallas kernels for 1%

profile of v3, /device:TPU:65, one launch (start us, length us, event | category | flops | bytes accessed | tf_op | source)
XLA Modules:
  0.0 119.8 jit_solution(17855162556268120293)
XLA Ops:
  0.7 15.6 %collective-permute-start = (bf16[24,384]{1,0:T(8,128)(2,1)}, bf16[24,384]{1,0:T(8,128)(2,1)S(1)}, u32[]{:S(2)}, u32[]{:S(2)}) collective-permute-start(bf16[24,384]{1,0:T(8,128)(2,1)} %param.11), channel_id=1, source_target_pairs={{0,128},{1,129},{2,130},{3,131},{4,132},{5,133},{6,134},{7,135},{8... | collective-permute-start | bytes 55304 | tf_op jit(solution)/shard_map/ppermute | solution.py:27
  16.3 0.7 multiply_add_fusion
  17.0 0.9 copy-done.5
  17.9 0.9 shard_map.103
  18.9 13.7 %collective-permute-start.2 = (bf16[32,3072]{1,0:T(8,128)(2,1)S(1)}, bf16[32,3072]{1,0:T(8,128)(2,1)S(1)}, u32[]{:S(2)}, u32[]{:S(2)}) collective-permute-start(bf16[32,3072]{1,0:T(8,128)(2,1)S(1)} %shard_map.103), channel_id=1, source_target_pairs={{0,128},{1,129},{2,130},{3,131},{4,132},{5,133},{6,134},{7,135},{8... | collective-permute-start | bytes 589832 | tf_op jit(solution)/shard_map/ppermute | solution.py:48
  32.6 0.7 pad_maximum_fusion.2
  33.3 4.0 %collective-permute-start.1 = (bf16[48,384]{1,0:T(8,128)(2,1)S(1)}, bf16[48,384]{1,0:T(8,128)(2,1)S(1)}, u32[]{:S(2)}, u32[]{:S(2)}) collective-permute-start(bf16[48,384]{1,0:T(8,128)(2,1)S(1)} %pad_maximum_fusion.2), channel_id=1, source_target_pairs={{0,64},{1,65},{2,66},{3,67},{4,68},{5,69},{6,70},{7,71},{8,72},{9,... | collective-permute-start | bytes 110600 | tf_op jit(solution)/shard_map/ppermute | solution.py:27
  37.3 11.9 %all_gather.6.own_ref = bf16[128,3072]{1,0:T(8,128)(2,1)S(1)} all-gather(bf16[32,3072]{1,0:T(8,128)(2,1)S(1)} %shard_map.103), channel_id=1, replica_groups={{0,2,4,6},{1,3,5,7},{8,10,12,14},{9,11,13,15},{16,18,20,22},{17,19,21,2..., dimensions={0}, use_global_device_ids=true | all-gather | bytes 983040 | tf_op jit(solution)/shard_map/all_gather | solution.py:32
  49.2 4.1 %collective-permute-start.3 = (bf16[96,384]{1,0:T(8,128)(2,1)S(1)}, bf16[96,384]{1,0:T(8,128)(2,1)S(1)}, u32[]{:S(2)}, u32[]{:S(2)}) collective-permute-start(bf16[96,384]{1,0:T(8,128)(2,1)S(1)} %pad_maximum_fusion.1), channel_id=1, source_target_pairs={{0,32},{1,33},{2,34},{3,35},{4,36},{5,37},{6,38},{7,39},{8,40},{9,... | collective-permute-start | bytes 221192 | tf_op jit(solution)/shard_map/ppermute | solution.py:27
  53.3 0.5 shard_map.104.attn_ref
  53.7 1.9 %collective-permute-done.3 = bf16[96,384]{1,0:T(8,128)(2,1)S(1)} collective-permute-done((bf16[96,384]{1,0:T(8,128)(2,1)S(1)}, bf16[96,384]{1,0:T(8,128)(2,1)S(1)}, u32[]{:S(2)}, u32[]{:S(2)}) %collective-permute-start.3) | collective-permute-done | bytes 73760 | tf_op jit(solution)/shard_map/ppermute | solution.py:27
  55.7 3.8 %collective-permute-start.4 = (bf16[192,384]{1,0:T(8,128)(2,1)S(1)}, bf16[192,384]{1,0:T(8,128)(2,1)S(1)}, u32[]{:S(2)}, u32[]{:S(2)}) collective-permute-start(bf16[192,384]{1,0:T(8,128)(2,1)S(1)} %pad_maximum_fusion), channel_id=1, source_target_pairs={{0,16},{1,17},{2,18},{3,19},{4,20},{5,21},{6,22},{7,23},{8,24},{9,... | collective-permute-start | bytes 442376 | tf_op jit(solution)/shard_map/ppermute | solution.py:27
  59.5 11.4 %collective-permute-start.8 = (bf16[32,3072]{1,0:T(8,128)(2,1)S(1)}, bf16[32,3072]{1,0:T(8,128)(2,1)S(1)}, u32[]{:S(2)}, u32[]{:S(2)}) collective-permute-start(bf16[32,3072]{1,0:T(8,128)(2,1)S(1)} %collective-permute-done.2), channel_id=1, source_target_pairs={{0,128},{1,129},{2,130},{3,131},{4,132},{5,133},{6,134},{7,135},{8... | collective-permute-start | bytes 589832 | tf_op jit(solution)/shard_map/ppermute | solution.py:48
  71.0 6.3 %collective-permute-start.5 = (bf16[384,384]{1,0:T(8,128)(2,1)S(1)}, bf16[384,384]{1,0:T(8,128)(2,1)S(1)}, u32[]{:S(2)}, u32[]{:S(2)}) collective-permute-start(bf16[384,384]{1,0:T(8,128)(2,1)S(1)} %get-tuple-element.25), channel_id=1, source_target_pairs={{0,512},{1,513},{2,514},{3,515},{4,516},{5,517},{6,518},{7,519},{8... | collective-permute-start | bytes 884744 | tf_op jit(solution)/shard_map/ppermute | solution.py:27
  77.3 2.3 %collective-permute-start.6 = (bf16[384,384]{1,0:T(8,128)(2,1)S(1)}, bf16[384,384]{1,0:T(8,128)(2,1)S(1)}, u32[]{:S(2)}, u32[]{:S(2)}) collective-permute-start(bf16[384,384]{1,0:T(8,128)(2,1)S(1)} %get-tuple-element.25), channel_id=1, source_target_pairs={{0,256},{1,257},{2,258},{3,259},{4,260},{5,261},{6,262},{7,263},{8... | collective-permute-start | bytes 884744 | tf_op jit(solution)/shard_map/ppermute | solution.py:27
  79.6 2.3 %collective-permute-start.7 = (bf16[384,384]{1,0:T(8,128)(2,1)S(1)}, bf16[384,384]{1,0:T(8,128)(2,1)S(1)}, u32[]{:S(2)}, u32[]{:S(2)}) collective-permute-start(bf16[384,384]{1,0:T(8,128)(2,1)S(1)} %get-tuple-element.25), channel_id=1, source_target_pairs={{0,768},{1,769},{2,770},{3,771},{4,772},{5,773},{6,774},{7,775},{8... | collective-permute-start | bytes 884744 | tf_op jit(solution)/shard_map/ppermute | solution.py:27
  81.9 17.3 %all_gather.7.far_ref = bf16[128,3072]{1,0:T(8,128)(2,1)S(1)} all-gather(bf16[32,3072]{1,0:T(8,128)(2,1)S(1)} %collective-permute-done.8), channel_id=1, replica_groups={{0,2,4,6},{1,3,5,7},{8,10,12,14},{9,11,13,15},{16,18,20,22},{17,19,21,2..., dimensions={0}, use_global_device_ids=true | all-gather | bytes 983040 | tf_op jit(solution)/shard_map/all_gather | solution.py:32
  99.4 10.8 %collective-permute-start.9 = (bf16[1536,384]{1,0:T(8,128)(2,1)S(1)}, bf16[1536,384]{1,0:T(8,128)(2,1)}, u32[]{:S(2)}, u32[]{:S(2)}) collective-permute-start(bf16[1536,384]{1,0:T(8,128)(2,1)S(1)} %constant_dynamic-update-slice_fusion.3.w_ref), channel_id=1, source_target_pairs={{0,8},{1,9},{2,10},{3,11},{4,12},{5,13},{6,14},{7,15},{8,0},{9,1},... | collective-permute-start | bytes 3538952 | tf_op jit(solution)/shard_map/ppermute | solution.py:27
  110.2 0.1 stack.35.rows_ref
  110.3 2.5 %collective-permute-done.9.wc_ref = bf16[1536,384]{1,0:T(8,128)(2,1)} collective-permute-done((bf16[1536,384]{1,0:T(8,128)(2,1)S(1)}, bf16[1536,384]{1,0:T(8,128)(2,1)}, u32[]{:S(2)}, u32[]{:S(2)}) %collective-permute-start.9) | collective-permute-done | bytes 1179680 | tf_op jit(solution)/shard_map/ppermute | solution.py:27
  112.8 0.9 copy-done.1
  113.7 0.9 copy-done.3
  114.7 0.9 copy-done.4
  115.6 4.3 %shard_map.105 = (bf16[256,384]{1,0:T(8,128)(2,1)}, bf16[256,384]{1,0:T(8,128)(2,1)}, bf16[256,384]{1,0:T(8,128)(2,1)}) custom-call(s32[8]{0:T(128)S(1)} %stack.35.rows_ref, f32[3,256,256]{2,1,0:T(8,128)S(1)} %shard_map.104.attn_ref, bf16[256,384]{1,0:T(8,128)(2,1)S(1)} %bitcast.17, bf16[256,384]{1,0:T(8,128)(2,1)S(1)} %bitcast.19, ...), custom_call_target="tpu_custom_call" | custom-call | flops 805306368 | bytes 6291456 | tf_op jit(solution)/shard_map/pallas_call | solution.py:164
  (27 shorter events, 0.3 us)
Async XLA Ops:
  0.6 52.6 %copy-start = (bf16[1,256,384]{2,1,0:T(8,128)(2,1)S(1)}, bf16[1,256,384]{2,1,0:T(8,128)(2,1)}, u32[]{:S(2)}) copy-start(bf16[1,256,384]{2,1,0:T(8,128)(2,1)} %param.8) | copy-start | bytes 589828
  0.6 52.6 %copy-start.2 = (bf16[1,256,384]{2,1,0:T(8,128)(2,1)S(1)}, bf16[1,256,384]{2,1,0:T(8,128)(2,1)}, u32[]{:S(2)}) copy-start(bf16[1,256,384]{2,1,0:T(8,128)(2,1)} %param.9) | copy-start | bytes 589828
  0.7 31.9 %collective-permute-start = (bf16[24,384]{1,0:T(8,128)(2,1)}, bf16[24,384]{1,0:T(8,128)(2,1)S(1)}, u32[]{:S(2)}, u32[]{:S(2)}) collective-permute-start(bf16[24,384]{1,0:T(8,128)(2,1)} %param.11), channel_id=1, source_target_pairs={{0,128},{1,129},{2,130},{3,131},{4,132},{5,133},{6,134},{7,135},{8... | collective-permute-start | bytes 55304 | tf_op jit(solution)/shard_map/ppermute | solution.py:27
  17.0 0.9 copy-start.5
  17.9 31.2 %copy-start.6 = (bf16[24,384]{1,0:T(8,128)(2,1)S(1)}, bf16[24,384]{1,0:T(8,128)(2,1)}, u32[]{:S(2)}) copy-start(bf16[24,384]{1,0:T(8,128)(2,1)} %param.11) | copy-start | bytes 55300
  18.9 30.3 %collective-permute-start.2 = (bf16[32,3072]{1,0:T(8,128)(2,1)S(1)}, bf16[32,3072]{1,0:T(8,128)(2,1)S(1)}, u32[]{:S(2)}, u32[]{:S(2)}) collective-permute-start(bf16[32,3072]{1,0:T(8,128)(2,1)S(1)} %shard_map.103), channel_id=1, source_target_pairs={{0,128},{1,129},{2,130},{3,131},{4,132},{5,133},{6,134},{7,135},{8... | collective-permute-start | bytes 589832 | tf_op jit(solution)/shard_map/ppermute | solution.py:48
  33.3 15.9 %collective-permute-start.1 = (bf16[48,384]{1,0:T(8,128)(2,1)S(1)}, bf16[48,384]{1,0:T(8,128)(2,1)S(1)}, u32[]{:S(2)}, u32[]{:S(2)}) collective-permute-start(bf16[48,384]{1,0:T(8,128)(2,1)S(1)} %pad_maximum_fusion.2), channel_id=1, source_target_pairs={{0,64},{1,65},{2,66},{3,67},{4,68},{5,69},{6,70},{7,71},{8,72},{9,... | collective-permute-start | bytes 110600 | tf_op jit(solution)/shard_map/ppermute | solution.py:27
  49.2 6.5 %collective-permute-start.3 = (bf16[96,384]{1,0:T(8,128)(2,1)S(1)}, bf16[96,384]{1,0:T(8,128)(2,1)S(1)}, u32[]{:S(2)}, u32[]{:S(2)}) collective-permute-start(bf16[96,384]{1,0:T(8,128)(2,1)S(1)} %pad_maximum_fusion.1), channel_id=1, source_target_pairs={{0,32},{1,33},{2,34},{3,35},{4,36},{5,37},{6,38},{7,39},{8,40},{9,... | collective-permute-start | bytes 221192 | tf_op jit(solution)/shard_map/ppermute | solution.py:27
  55.7 15.2 %collective-permute-start.4 = (bf16[192,384]{1,0:T(8,128)(2,1)S(1)}, bf16[192,384]{1,0:T(8,128)(2,1)S(1)}, u32[]{:S(2)}, u32[]{:S(2)}) collective-permute-start(bf16[192,384]{1,0:T(8,128)(2,1)S(1)} %pad_maximum_fusion), channel_id=1, source_target_pairs={{0,16},{1,17},{2,18},{3,19},{4,20},{5,21},{6,22},{7,23},{8,24},{9,... | collective-permute-start | bytes 442376 | tf_op jit(solution)/shard_map/ppermute | solution.py:27
  59.5 22.4 %collective-permute-start.8 = (bf16[32,3072]{1,0:T(8,128)(2,1)S(1)}, bf16[32,3072]{1,0:T(8,128)(2,1)S(1)}, u32[]{:S(2)}, u32[]{:S(2)}) collective-permute-start(bf16[32,3072]{1,0:T(8,128)(2,1)S(1)} %collective-permute-done.2), channel_id=1, source_target_pairs={{0,128},{1,129},{2,130},{3,131},{4,132},{5,133},{6,134},{7,135},{8... | collective-permute-start | bytes 589832 | tf_op jit(solution)/shard_map/ppermute | solution.py:48
  71.0 28.2 %collective-permute-start.5 = (bf16[384,384]{1,0:T(8,128)(2,1)S(1)}, bf16[384,384]{1,0:T(8,128)(2,1)S(1)}, u32[]{:S(2)}, u32[]{:S(2)}) collective-permute-start(bf16[384,384]{1,0:T(8,128)(2,1)S(1)} %get-tuple-element.25), channel_id=1, source_target_pairs={{0,512},{1,513},{2,514},{3,515},{4,516},{5,517},{6,518},{7,519},{8... | collective-permute-start | bytes 884744 | tf_op jit(solution)/shard_map/ppermute | solution.py:27
  77.3 22.0 %collective-permute-start.6 = (bf16[384,384]{1,0:T(8,128)(2,1)S(1)}, bf16[384,384]{1,0:T(8,128)(2,1)S(1)}, u32[]{:S(2)}, u32[]{:S(2)}) collective-permute-start(bf16[384,384]{1,0:T(8,128)(2,1)S(1)} %get-tuple-element.25), channel_id=1, source_target_pairs={{0,256},{1,257},{2,258},{3,259},{4,260},{5,261},{6,262},{7,263},{8... | collective-permute-start | bytes 884744 | tf_op jit(solution)/shard_map/ppermute | solution.py:27
  79.6 19.7 %collective-permute-start.7 = (bf16[384,384]{1,0:T(8,128)(2,1)S(1)}, bf16[384,384]{1,0:T(8,128)(2,1)S(1)}, u32[]{:S(2)}, u32[]{:S(2)}) collective-permute-start(bf16[384,384]{1,0:T(8,128)(2,1)S(1)} %get-tuple-element.25), channel_id=1, source_target_pairs={{0,768},{1,769},{2,770},{3,771},{4,772},{5,773},{6,774},{7,775},{8... | collective-permute-start | bytes 884744 | tf_op jit(solution)/shard_map/ppermute | solution.py:27
  99.4 13.4 %collective-permute-start.9 = (bf16[1536,384]{1,0:T(8,128)(2,1)S(1)}, bf16[1536,384]{1,0:T(8,128)(2,1)}, u32[]{:S(2)}, u32[]{:S(2)}) collective-permute-start(bf16[1536,384]{1,0:T(8,128)(2,1)S(1)} %constant_dynamic-update-slice_fusion.3.w_ref), channel_id=1, source_target_pairs={{0,8},{1,9},{2,10},{3,11},{4,12},{5,13},{6,14},{7,15},{8,0},{9,1},... | collective-permute-start | bytes 3538952 | tf_op jit(solution)/shard_map/ppermute | solution.py:27
  112.8 0.9 copy-start.1
  113.7 0.9 copy-start.3
  114.7 0.9 copy-start.4

commit v4 on v3

--- a/solution.py
+++ b/solution.py
@@ -12,6 +12,7 @@
 AXES = ("dp", "mp")
 NY, NZ, NC, NX, NH = 4, 16, 2, 4, 2
 Y_ORDER = (0, 2, 1, 3)
+X_ORDER = (0, 2, 1, 3)
 
 
 def exchange(y=0, z=0, core=0, x=0, half=0):
@@ -60,13 +61,15 @@
     return lax.dot_general(a, b, (((1,), (0,)), ((), ())), preferred_element_type=jnp.float32)
 
 
-def reorder_kernel(y_ref, source_ref, in_ref, out_ref):
+def reorder_kernel(y_ref, source_ref, in_ref, out_ref, wide_ref):
     span = source_ref.shape[1]
     wanted = lax.broadcasted_iota(jnp.int32, (span, span), 0) == source_ref[...]
     pick = jnp.where(wanted, 1.0, 0.0).astype(jnp.bfloat16)
     for slot, i in enumerate(Y_ORDER):
         start = pl.multiple_of((y_ref[0] ^ i) * span, span)
-        out_ref[:, slot * span:(slot + 1) * span] = nn(in_ref[:, pl.ds(start, span)], pick).astype(jnp.bfloat16)
+        moved = nn(in_ref[:, pl.ds(start, span)], pick)
+        out_ref[:, slot * span:(slot + 1) * span] = moved.astype(jnp.bfloat16)
+        wide_ref[:, slot * span:(slot + 1) * span] = moved
 
 
 def attention_kernel(q_ref, k_ref, out_ref):
@@ -78,21 +81,36 @@
         out_ref[head] = raised / jnp.sum(raised, axis=-1, keepdims=True)
 
 
-def tail_kernel(rows_ref, attn_ref, q_ref, k_ref, v_ref, own_ref, far_ref, w_ref, wc_ref, *refs):
-    gq_ref, gk_ref, gv_ref, grad_ref = refs
+def tail_kernel(rows_ref, attn_any, q_any, k_any, v_any, own_any, *refs):
+    far_refs, (w_ref, wc_ref, *refs) = refs[:NX], refs[NX:]
+    gq_ref, gk_ref, gv_ref, grad_ref, q_ref, k_ref, v_ref, attn_ref, own_ref, sems, own_sems = refs
+    copies = [
+        pltpu.make_async_copy(src, dst, sems.at[i])
+        for i, (src, dst) in enumerate(((attn_any, attn_ref), (v_any, v_ref), (k_any, k_ref), (q_any, q_ref)))
+    ]
+    depth = w_ref.shape[0] // NY
+    bands = [pl.ds(i * depth, depth) for i in range(NY * NC)]
+    own_copies = [
+        pltpu.make_async_copy(own_any.at[:, band], own_ref.at[:, band], own_sems.at[i])
+        for i, band in enumerate(bands)
+    ]
+    for copy in own_copies + copies:
+        copy.start()
     scale = 1.0 / math.sqrt(HD)
-    n_g, depth = NX * NH, w_ref.shape[0] // NY
-    part = q_ref.shape[0] // n_g
+    n_g = NX * NH
+    part = q_any.shape[0] // n_g
     parts = [ref[i * depth:(i + 1) * depth] for i in range(NY) for ref in (w_ref, wc_ref)]
-    left = jnp.concatenate([own_ref[...], far_ref[...]], axis=0)
     total = None
-    for i, piece in enumerate(parts):
-        term = nn(left[:, i * depth:(i + 1) * depth], piece)
+    for band, copy, piece in zip(bands, own_copies, parts):
+        copy.wait()
+        term = nn(jnp.concatenate([own_ref[:, band].astype(jnp.bfloat16)] + [ref[:, band] for ref in far_refs], axis=0), piece)
         total = term if total is None else total + term
     total = total.astype(jnp.bfloat16)
     for slot in range(n_g):
         row = pl.multiple_of(rows_ref[slot] * part, part)
         grad_ref[pl.ds(row, part), :] = total[slot * part:(slot + 1) * part]
+    for copy in copies:
+        copy.wait()
     for head in range(q_ref.shape[1] // HD):
         cols = pl.ds(head * HD, HD)
         grad = grad_ref[:, cols]
@@ -106,6 +124,7 @@
 
 
 VMEM = pl.BlockSpec(memory_space=pltpu.VMEM)
+HBM = pl.BlockSpec(memory_space=pltpu.HBM)
 SMEM = pl.BlockSpec(memory_space=pltpu.SMEM)
 PARAMS = pltpu.CompilerParams(vmem_limit_bytes=16 * 1024 * 1024)
 
@@ -125,15 +144,25 @@
     z_xor = sum(((z_bits >> b) & 1) << (3 - b) for b in range(4))
     core_xor = place // (NZ * block)
     source = ((jnp.asarray(z_xor) ^ z) * NC + (jnp.asarray(core_xor) ^ core)) * block + jnp.asarray(place % block)
-    own = pl.pallas_call(
+    own, wide = pl.pallas_call(
         reorder_kernel,
-        out_shape=jax.ShapeDtypeStruct((part, model), jnp.bfloat16),
+        out_shape=tuple(jax.ShapeDtypeStruct((part, model), t) for t in (jnp.bfloat16, jnp.float32)),
         in_specs=[SMEM, VMEM, VMEM],
-        out_specs=VMEM,
+        out_specs=(VMEM, VMEM),
         compiler_params=PARAMS,
         cost_estimate=pl.CostEstimate(flops=2 * part * model * span, bytes_accessed=4 * part * model, transcendentals=0),
     )(y.reshape(1), source.astype(jnp.int32).reshape(1, span), grad_out.reshape(part, model))
 
+    weight = out_weight
+    arrived = swap(weight, z=8)
+    half_way = quarter_turn(own)
+    own = gather_x(wide)
+    weight = jnp.concatenate([weight, arrived], 0)
+    weight = jnp.concatenate([weight, swap(weight, z=4)], 0)
+    weight, half_way = after(weight, half_way)
+    far = quarter_turn(half_way)
+    weight = jnp.concatenate([weight, swap(weight, z=2)], 0)
+    q_late, weight = after(q, weight)
     attn = pl.pallas_call(
         attention_kernel,
         out_shape=jax.ShapeDtypeStruct((heads, patches, patches), jnp.float32),
@@ -141,35 +170,30 @@
         out_specs=VMEM,
         compiler_params=PARAMS,
         cost_estimate=pl.CostEstimate(flops=2 * patches * patches * width, bytes_accessed=1 << 20, transcendentals=0),
-    )(q, k)
-    weight = out_weight
-    arrived = swap(weight, z=8)
-    half_way = quarter_turn(own)
-    own, arrived = after(own, arrived)
-    weight = jnp.concatenate([weight, arrived], 0)
-    weight = jnp.concatenate([weight, swap(weight, z=4)], 0)
-    own = gather_x(own)
-    weight, half_way, own = after(weight, half_way, own)
-    far = quarter_turn(half_way)
-    weight = jnp.concatenate([weight, swap(weight, z=2)], 0)
+    )(q_late, k)
     weight = jnp.concatenate([weight, swap(weight, z=1)], 0)
-    weight = jnp.concatenate([weight] + [swap(weight, y=i) for i in Y_ORDER[1:]], 0)
-    far = gather_x(far)
-    weight, far, attn = after(weight, far, attn)
+    opposite = swap(weight, y=2)
+    weight, far = after(weight, far)
+    weight = jnp.concatenate([weight, opposite, swap(weight, y=1), swap(weight, y=3)], 0)
+    far = [far] + [swap(far, x=i) for i in X_ORDER[1:]]
+    weight, attn, *far = after(weight, attn, *far)
     weights = [weight, swap(weight, core=1)]
     half = mp % NH
-    rows = jnp.stack([i * NH + h for h in (half, 1 - half) for i in range(NX)]).astype(jnp.int32)
+    rows = [i * NH + half for i in range(NX)] + [mp ^ (i * NH + 1) for i in X_ORDER]
+    rows = jnp.stack(rows).astype(jnp.int32)
 
     grad_shape = jax.ShapeDtypeStruct((patches, width), jnp.bfloat16)
     outs = pl.pallas_call(
         tail_kernel,
         out_shape=(grad_shape,) * 3,
-        in_specs=[SMEM] + [VMEM] * (6 + len(weights)),
+        in_specs=[SMEM, HBM] + [HBM] * 4 + [VMEM] * (len(far) + len(weights)),
         out_specs=(VMEM,) * 3,
-        scratch_shapes=[pltpu.VMEM((patches, width), jnp.bfloat16)],
+        scratch_shapes=[pltpu.VMEM((patches, width), jnp.bfloat16)] * 4
+        + [pltpu.VMEM(a.shape, a.dtype) for a in (attn, own)]
+        + [pltpu.SemaphoreType.DMA((4,)), pltpu.SemaphoreType.DMA((NY * NC,))],
         compiler_params=PARAMS,
         cost_estimate=pl.CostEstimate(flops=2 * patches * width * (model + 4 * patches), bytes_accessed=6 << 20, transcendentals=0),
-    )(rows, attn, q, k, v, own, far, *weights)
+    )(rows, attn, q, k, v, own, *far, *weights)
     return tuple(o.reshape(1, patches, width) for o in outs)
 
 

time: 120 us -> 151 us (1.26)
  the two profiles are of different devices: /device:TPU:65 before, /device:TPU:1 now
where the time goes in v4:
time: 151 us; the launch traced here: 149 us
  starting transfers between devices  80.1 us (53%)
  waiting for transfers between devices  35.2 us (23%)
  between operations  14.3 us (9%)
  local copies, waits for them, and re-layouts  9.13 us (6%)
  Pallas kernels  7.52 us (5%)
  other arithmetic  2.33 us (2%)
    ppermute x11, starting transfers between devices, swap(): return lax.ppermute(value, AXES, exchange(**moves))  52.5 us
    ppermute x2, starting transfers between devices, quarter_turn(): return lax.ppermute(value, AXES, pairs)  27.5 us
    ppermute x11, waiting for transfers between devices, swap(): return lax.ppermute(value, AXES, exchange(**moves))  23.3 us
    ppermute x2, waiting for transfers between devices, quarter_turn(): return lax.ppermute(value, AXES, pairs)  11.9 us
    unnamed x27, local copies, waits for them, and re-layouts  9.01 us
    pallas_call x1, Pallas kernels, shards(): pl.pallas_call(tail_kernel, out_shape=(grad_shape,) * 3, in_specs=[SMEM,...  5.31 us
  transfers between devices with their start and end apart: 14, of which 6 were waited for; matrix products, arithmetic and copies ran while one was open for 2% of the time, Pallas kernels for 1%

profile of v4, /device:TPU:1, one launch (start us, length us, event | category | flops | bytes accessed | tf_op | source)
XLA Modules:
  0.0 148.6 jit_solution(15043197775411919735)
XLA Ops:
  7.2 16.4 %collective-permute-start = (bf16[24,384]{1,0:T(8,128)(2,1)}, bf16[24,384]{1,0:T(8,128)(2,1)S(1)}, u32[]{:S(2)}, u32[]{:S(2)}) collective-permute-start(bf16[24,384]{1,0:T(8,128)(2,1)} %param.11), channel_id=1, source_target_pairs={{0,128},{1,129},{2,130},{3,131},{4,132},{5,133},{6,134},{7,135},{8... | collective-permute-start | bytes 55304 | tf_op jit(solution)/shard_map/ppermute | solution.py:28
  25.3 1.7 %shard_map.103 = (bf16[32,3072]{1,0:T(8,128)(2,1)S(1)}, f32[32,3072]{1,0:T(8,128)}) custom-call(s32[1]{0:T(128)} %bitcast.9.y_ref, s32[1,768]{1,0:T(1,128)S(1)} %reshape.35.source_ref, bf16[32,3072]{1,0:T(8,128)(2,1)S(1)} %bitcast.21), custom_call_target="tpu_custom_call" | custom-call | flops 150994944 | bytes 393216 | tf_op jit(solution)/shard_map/pallas_call | solution.py:147
  27.1 15.4 %collective-permute-start.2 = (bf16[32,3072]{1,0:T(8,128)(2,1)S(1)}, bf16[32,3072]{1,0:T(8,128)(2,1)S(1)}, u32[]{:S(2)}, u32[]{:S(2)}) collective-permute-start(bf16[32,3072]{1,0:T(8,128)(2,1)S(1)} %get-tuple-element.20), channel_id=1, source_target_pairs={{0,128},{1,129},{2,130},{3,131},{4,132},{5,133},{6,134},{7,135},{8... | collective-permute-start | bytes 589832 | tf_op jit(solution)/shard_map/ppermute | solution.py:49
  43.3 4.0 %collective-permute-start.1 = (bf16[48,384]{1,0:T(8,128)(2,1)S(1)}, bf16[48,384]{1,0:T(8,128)(2,1)S(1)}, u32[]{:S(2)}, u32[]{:S(2)}) collective-permute-start(bf16[48,384]{1,0:T(8,128)(2,1)S(1)} %pad_maximum_fusion.3), channel_id=1, source_target_pairs={{0,64},{1,65},{2,66},{3,67},{4,68},{5,69},{6,70},{7,71},{8,72},{9,... | collective-permute-start | bytes 110600 | tf_op jit(solution)/shard_map/ppermute | solution.py:28
  47.3 12.8 %collective-permute-done.1 = bf16[48,384]{1,0:T(8,128)(2,1)S(1)} collective-permute-done((bf16[48,384]{1,0:T(8,128)(2,1)S(1)}, bf16[48,384]{1,0:T(8,128)(2,1)S(1)}, u32[]{:S(2)}, u32[]{:S(2)}) %collective-permute-start.1) | collective-permute-done | bytes 36896 | tf_op jit(solution)/shard_map/ppermute | solution.py:28
  60.9 1.9 %collective-permute-start.3 = (bf16[96,384]{1,0:T(8,128)(2,1)S(1)}, bf16[96,384]{1,0:T(8,128)(2,1)S(1)}, u32[]{:S(2)}, u32[]{:S(2)}) collective-permute-start(bf16[96,384]{1,0:T(8,128)(2,1)S(1)} %pad_maximum_fusion.2), channel_id=1, source_target_pairs={{0,32},{1,33},{2,34},{3,35},{4,36},{5,37},{6,38},{7,39},{8,40},{9,... | collective-permute-start | bytes 221192 | tf_op jit(solution)/shard_map/ppermute | solution.py:28
  62.8 4.9 %collective-permute-done.3 = bf16[96,384]{1,0:T(8,128)(2,1)S(1)} collective-permute-done((bf16[96,384]{1,0:T(8,128)(2,1)S(1)}, bf16[96,384]{1,0:T(8,128)(2,1)S(1)}, u32[]{:S(2)}, u32[]{:S(2)}) %collective-permute-start.3) | collective-permute-done | bytes 73760 | tf_op jit(solution)/shard_map/ppermute | solution.py:28
  67.7 1.9 %collective-permute-start.4 = (bf16[192,384]{1,0:T(8,128)(2,1)S(1)}, bf16[192,384]{1,0:T(8,128)(2,1)S(1)}, u32[]{:S(2)}, u32[]{:S(2)}) collective-permute-start(bf16[192,384]{1,0:T(8,128)(2,1)S(1)} %pad_maximum_fusion.1), channel_id=1, source_target_pairs={{0,16},{1,17},{2,18},{3,19},{4,20},{5,21},{6,22},{7,23},{8,24},{9,... | collective-permute-start | bytes 442376 | tf_op jit(solution)/shard_map/ppermute | solution.py:28
  69.6 12.1 %collective-permute-start.5 = (bf16[32,3072]{1,0:T(8,128)(2,1)S(1)}, bf16[32,3072]{1,0:T(8,128)(2,1)S(1)}, u32[]{:S(2)}, u32[]{:S(2)}) collective-permute-start(bf16[32,3072]{1,0:T(8,128)(2,1)S(1)} %collective-permute-done.2), channel_id=1, source_target_pairs={{0,128},{1,129},{2,130},{3,131},{4,132},{5,133},{6,134},{7,135},{8... | collective-permute-start | bytes 589832 | tf_op jit(solution)/shard_map/ppermute | solution.py:49
  81.8 11.9 %collective-permute-done.5.refs_0_ = bf16[32,3072]{1,0:T(8,128)(2,1)S(1)} collective-permute-done((bf16[32,3072]{1,0:T(8,128)(2,1)S(1)}, bf16[32,3072]{1,0:T(8,128)(2,1)S(1)}, u32[]{:S(2)}, u32[]{:S(2)}) %collective-permute-start.5) | collective-permute-done | bytes 196640 | tf_op jit(solution)/shard_map/ppermute | solution.py:49
  93.7 5.2 %collective-permute-start.8 = (bf16[384,384]{1,0:T(8,128)(2,1)S(1)}, bf16[384,384]{1,0:T(8,128)(2,1)S(1)}, u32[]{:S(2)}, u32[]{:S(2)}) collective-permute-start(bf16[384,384]{1,0:T(8,128)(2,1)S(1)} %constant_dynamic-update-slice_fusion), channel_id=1, source_target_pairs={{0,768},{1,769},{2,770},{3,771},{4,772},{5,773},{6,774},{7,775},{8... | collective-permute-start | bytes 884744 | tf_op jit(solution)/shard_map/ppermute | solution.py:28
  98.8 1.9 %collective-permute-start.7 = (bf16[384,384]{1,0:T(8,128)(2,1)S(1)}, bf16[384,384]{1,0:T(8,128)(2,1)S(1)}, u32[]{:S(2)}, u32[]{:S(2)}) collective-permute-start(bf16[384,384]{1,0:T(8,128)(2,1)S(1)} %constant_dynamic-update-slice_fusion), channel_id=1, source_target_pairs={{0,256},{1,257},{2,258},{3,259},{4,260},{5,261},{6,262},{7,263},{8... | collective-permute-start | bytes 884744 | tf_op jit(solution)/shard_map/ppermute | solution.py:28
  100.8 3.1 %collective-permute-start.6 = (bf16[384,384]{1,0:T(8,128)(2,1)S(1)}, bf16[384,384]{1,0:T(8,128)(2,1)S(1)}, u32[]{:S(2)}, u32[]{:S(2)}) collective-permute-start(bf16[384,384]{1,0:T(8,128)(2,1)S(1)} %constant_dynamic-update-slice_fusion), channel_id=1, source_target_pairs={{0,512},{1,513},{2,514},{3,515},{4,516},{5,517},{6,518},{7,519},{8... | collective-permute-start | bytes 884744 | tf_op jit(solution)/shard_map/ppermute | solution.py:28
  104.4 4.4 %collective-permute-start.11 = (bf16[32,3072]{1,0:T(8,128)(2,1)S(1)}, bf16[32,3072]{1,0:T(8,128)(2,1)S(1)}, u32[]{:S(2)}, u32[]{:S(2)}) collective-permute-start(bf16[32,3072]{1,0:T(8,128)(2,1)S(1)} %collective-permute-done.5.refs_0_), channel_id=1, source_target_pairs={{0,6},{1,7},{2,4},{3,5},{4,2},{5,3},{6,0},{7,1},{8,14},{9,15},{10,... | collective-permute-start | bytes 589832 | tf_op jit(solution)/shard_map/ppermute | solution.py:28
  108.8 1.9 %collective-permute-start.10 = (bf16[32,3072]{1,0:T(8,128)(2,1)S(1)}, bf16[32,3072]{1,0:T(8,128)(2,1)S(1)}, u32[]{:S(2)}, u32[]{:S(2)}) collective-permute-start(bf16[32,3072]{1,0:T(8,128)(2,1)S(1)} %collective-permute-done.5.refs_0_), channel_id=1, source_target_pairs={{0,2},{1,3},{2,0},{3,1},{4,6},{5,7},{6,4},{7,5},{8,10},{9,11},{10,... | collective-permute-start | bytes 589832 | tf_op jit(solution)/shard_map/ppermute | solution.py:28
  110.7 3.3 %collective-permute-start.9 = (bf16[32,3072]{1,0:T(8,128)(2,1)S(1)}, bf16[32,3072]{1,0:T(8,128)(2,1)S(1)}, u32[]{:S(2)}, u32[]{:S(2)}) collective-permute-start(bf16[32,3072]{1,0:T(8,128)(2,1)S(1)} %collective-permute-done.5.refs_0_), channel_id=1, source_target_pairs={{0,4},{1,5},{2,6},{3,7},{4,0},{5,1},{6,2},{7,3},{8,12},{9,13},{10,... | collective-permute-start | bytes 589832 | tf_op jit(solution)/shard_map/ppermute | solution.py:28
  116.2 2.6 %collective-permute-done.9.refs_1_ = bf16[32,3072]{1,0:T(8,128)(2,1)S(1)} collective-permute-done((bf16[32,3072]{1,0:T(8,128)(2,1)S(1)}, bf16[32,3072]{1,0:T(8,128)(2,1)S(1)}, u32[]{:S(2)}, u32[]{:S(2)}) %collective-permute-start.9) | collective-permute-done | bytes 196640 | tf_op jit(solution)/shard_map/ppermute | solution.py:28
  119.4 8.5 %collective-permute-start.12 = (bf16[1536,384]{1,0:T(8,128)(2,1)S(1)}, bf16[1536,384]{1,0:T(8,128)(2,1)S(1)}, u32[]{:S(2)}, u32[]{:S(2)}) collective-permute-start(bf16[1536,384]{1,0:T(8,128)(2,1)S(1)} %pad_maximum_fusion.refs_4_), channel_id=1, source_target_pairs={{0,8},{1,9},{2,10},{3,11},{4,12},{5,13},{6,14},{7,15},{8,0},{9,1},... | collective-permute-start | bytes 3538952 | tf_op jit(solution)/shard_map/ppermute | solution.py:28
  128.0 2.4 %collective-permute-done.12.refs_5_ = bf16[1536,384]{1,0:T(8,128)(2,1)S(1)} collective-permute-done((bf16[1536,384]{1,0:T(8,128)(2,1)S(1)}, bf16[1536,384]{1,0:T(8,128)(2,1)S(1)}, u32[]{:S(2)}, u32[]{:S(2)}) %collective-permute-start.12) | collective-permute-done | bytes 1179680 | tf_op jit(solution)/shard_map/ppermute | solution.py:28
  130.4 1.4 copy-done
  131.8 0.9 copy-done.3
  133.7 0.9 copy-done.7
  134.6 0.9 copy-done.9
  136.4 5.3 %shard_map.105 = (bf16[256,384]{1,0:T(8,128)(2,1)}, bf16[256,384]{1,0:T(8,128)(2,1)}, bf16[256,384]{1,0:T(8,128)(2,1)}) custom-call(s32[8]{0:T(128)S(1)} %stack.35.rows_ref, f32[3,256,256]{2,1,0:T(8,128)S(1)} %shard_map.104.attn_any, bf16[256,384]{1,0:T(8,128)(2,1)S(1)} %bitcast.17, bf16[256,384]{1,0:T(8,128)(2,1)S(1)} %bitcast.19, ...), custom_call_target="tpu_custom_call" | custom-call | flops 805306368 | bytes 6291456 | tf_op jit(solution)/shard_map/pallas_call | solution.py:186
  (43 shorter events, 8.5 us)
Async XLA Ops:
  7.2 96.7 %copy-start.1 = (bf16[1,256,384]{2,1,0:T(8,128)(2,1)S(1)}, bf16[1,256,384]{2,1,0:T(8,128)(2,1)}, u32[]{:S(2)}) copy-start(bf16[1,256,384]{2,1,0:T(8,128)(2,1)} %param.8) | copy-start | bytes 589828
  7.2 96.7 %copy-start.2 = (bf16[1,256,384]{2,1,0:T(8,128)(2,1)S(1)}, bf16[1,256,384]{2,1,0:T(8,128)(2,1)}, u32[]{:S(2)}) copy-start(bf16[1,256,384]{2,1,0:T(8,128)(2,1)} %param.9) | copy-start | bytes 589828
  7.2 123.2 %all-gather.2.cloned.1.call-start = ((), (), s32[]{:S(2)}) async-start(), calls=%async_computation | async-start | bytes 1966080 | tf_op jit(solution)/shard_map/all_gather | solution.py:33
  7.2 35.3 %collective-permute-start = (bf16[24,384]{1,0:T(8,128)(2,1)}, bf16[24,384]{1,0:T(8,128)(2,1)S(1)}, u32[]{:S(2)}, u32[]{:S(2)}) collective-permute-start(bf16[24,384]{1,0:T(8,128)(2,1)} %param.11), channel_id=1, source_target_pairs={{0,128},{1,129},{2,130},{3,131},{4,132},{5,133},{6,134},{7,135},{8... | collective-permute-start | bytes 55304 | tf_op jit(solution)/shard_map/ppermute | solution.py:28
  24.4 0.9 copy-start.12
  27.1 33.8 %collective-permute-start.2 = (bf16[32,3072]{1,0:T(8,128)(2,1)S(1)}, bf16[32,3072]{1,0:T(8,128)(2,1)S(1)}, u32[]{:S(2)}, u32[]{:S(2)}) collective-permute-start(bf16[32,3072]{1,0:T(8,128)(2,1)S(1)} %get-tuple-element.20), channel_id=1, source_target_pairs={{0,128},{1,129},{2,130},{3,131},{4,132},{5,133},{6,134},{7,135},{8... | collective-permute-start | bytes 589832 | tf_op jit(solution)/shard_map/ppermute | solution.py:49
  43.3 16.8 %collective-permute-start.1 = (bf16[48,384]{1,0:T(8,128)(2,1)S(1)}, bf16[48,384]{1,0:T(8,128)(2,1)S(1)}, u32[]{:S(2)}, u32[]{:S(2)}) collective-permute-start(bf16[48,384]{1,0:T(8,128)(2,1)S(1)} %pad_maximum_fusion.3), channel_id=1, source_target_pairs={{0,64},{1,65},{2,66},{3,67},{4,68},{5,69},{6,70},{7,71},{8,72},{9,... | collective-permute-start | bytes 110600 | tf_op jit(solution)/shard_map/ppermute | solution.py:28
  60.9 6.8 %collective-permute-start.3 = (bf16[96,384]{1,0:T(8,128)(2,1)S(1)}, bf16[96,384]{1,0:T(8,128)(2,1)S(1)}, u32[]{:S(2)}, u32[]{:S(2)}) collective-permute-start(bf16[96,384]{1,0:T(8,128)(2,1)S(1)} %pad_maximum_fusion.2), channel_id=1, source_target_pairs={{0,32},{1,33},{2,34},{3,35},{4,36},{5,37},{6,38},{7,39},{8,40},{9,... | collective-permute-start | bytes 221192 | tf_op jit(solution)/shard_map/ppermute | solution.py:28
  67.7 14.0 %collective-permute-start.4 = (bf16[192,384]{1,0:T(8,128)(2,1)S(1)}, bf16[192,384]{1,0:T(8,128)(2,1)S(1)}, u32[]{:S(2)}, u32[]{:S(2)}) collective-permute-start(bf16[192,384]{1,0:T(8,128)(2,1)S(1)} %pad_maximum_fusion.1), channel_id=1, source_target_pairs={{0,16},{1,17},{2,18},{3,19},{4,20},{5,21},{6,22},{7,23},{8,24},{9,... | collective-permute-start | bytes 442376 | tf_op jit(solution)/shard_map/ppermute | solution.py:28
  69.6 24.0 %collective-permute-start.5 = (bf16[32,3072]{1,0:T(8,128)(2,1)S(1)}, bf16[32,3072]{1,0:T(8,128)(2,1)S(1)}, u32[]{:S(2)}, u32[]{:S(2)}) collective-permute-start(bf16[32,3072]{1,0:T(8,128)(2,1)S(1)} %collective-permute-done.2), channel_id=1, source_target_pairs={{0,128},{1,129},{2,130},{3,131},{4,132},{5,133},{6,134},{7,135},{8... | collective-permute-start | bytes 589832 | tf_op jit(solution)/shard_map/ppermute | solution.py:49
  93.7 20.5 %copy-start.4 = (bf16[32,3072]{1,0:T(8,128)(2,1)}, bf16[32,3072]{1,0:T(8,128)(2,1)S(1)}, u32[]{:S(2)}) copy-start(bf16[32,3072]{1,0:T(8,128)(2,1)S(1)} %collective-permute-done.5.refs_0_) | copy-start | bytes 589828
  93.7 17.0 %collective-permute-start.8 = (bf16[384,384]{1,0:T(8,128)(2,1)S(1)}, bf16[384,384]{1,0:T(8,128)(2,1)S(1)}, u32[]{:S(2)}, u32[]{:S(2)}) collective-permute-start(bf16[384,384]{1,0:T(8,128)(2,1)S(1)} %constant_dynamic-update-slice_fusion), channel_id=1, source_target_pairs={{0,768},{1,769},{2,770},{3,771},{4,772},{5,773},{6,774},{7,775},{8... | collective-permute-start | bytes 884744 | tf_op jit(solution)/shard_map/ppermute | solution.py:28
  98.8 15.1 %collective-permute-start.7 = (bf16[384,384]{1,0:T(8,128)(2,1)S(1)}, bf16[384,384]{1,0:T(8,128)(2,1)S(1)}, u32[]{:S(2)}, u32[]{:S(2)}) collective-permute-start(bf16[384,384]{1,0:T(8,128)(2,1)S(1)} %constant_dynamic-update-slice_fusion), channel_id=1, source_target_pairs={{0,256},{1,257},{2,258},{3,259},{4,260},{5,261},{6,262},{7,263},{8... | collective-permute-start | bytes 884744 | tf_op jit(solution)/shard_map/ppermute | solution.py:28
  100.8 13.2 %collective-permute-start.6 = (bf16[384,384]{1,0:T(8,128)(2,1)S(1)}, bf16[384,384]{1,0:T(8,128)(2,1)S(1)}, u32[]{:S(2)}, u32[]{:S(2)}) collective-permute-start(bf16[384,384]{1,0:T(8,128)(2,1)S(1)} %constant_dynamic-update-slice_fusion), channel_id=1, source_target_pairs={{0,512},{1,513},{2,514},{3,515},{4,516},{5,517},{6,518},{7,519},{8... | collective-permute-start | bytes 884744 | tf_op jit(solution)/shard_map/ppermute | solution.py:28
  104.4 9.8 %collective-permute-start.11 = (bf16[32,3072]{1,0:T(8,128)(2,1)S(1)}, bf16[32,3072]{1,0:T(8,128)(2,1)S(1)}, u32[]{:S(2)}, u32[]{:S(2)}) collective-permute-start(bf16[32,3072]{1,0:T(8,128)(2,1)S(1)} %collective-permute-done.5.refs_0_), channel_id=1, source_target_pairs={{0,6},{1,7},{2,4},{3,5},{4,2},{5,3},{6,0},{7,1},{8,14},{9,15},{10,... | collective-permute-start | bytes 589832 | tf_op jit(solution)/shard_map/ppermute | solution.py:28
  108.8 6.7 %collective-permute-start.10 = (bf16[32,3072]{1,0:T(8,128)(2,1)S(1)}, bf16[32,3072]{1,0:T(8,128)(2,1)S(1)}, u32[]{:S(2)}, u32[]{:S(2)}) collective-permute-start(bf16[32,3072]{1,0:T(8,128)(2,1)S(1)} %collective-permute-done.5.refs_0_), channel_id=1, source_target_pairs={{0,2},{1,3},{2,0},{3,1},{4,6},{5,7},{6,4},{7,5},{8,10},{9,11},{10,... | collective-permute-start | bytes 589832 | tf_op jit(solution)/shard_map/ppermute | solution.py:28
  110.7 8.0 %collective-permute-start.9 = (bf16[32,3072]{1,0:T(8,128)(2,1)S(1)}, bf16[32,3072]{1,0:T(8,128)(2,1)S(1)}, u32[]{:S(2)}, u32[]{:S(2)}) collective-permute-start(bf16[32,3072]{1,0:T(8,128)(2,1)S(1)} %collective-permute-done.5.refs_0_), channel_id=1, source_target_pairs={{0,4},{1,5},{2,6},{3,7},{4,0},{5,1},{6,2},{7,3},{8,12},{9,13},{10,... | collective-permute-start | bytes 589832 | tf_op jit(solution)/shard_map/ppermute | solution.py:28
  119.4 11.0 %collective-permute-start.12 = (bf16[1536,384]{1,0:T(8,128)(2,1)S(1)}, bf16[1536,384]{1,0:T(8,128)(2,1)S(1)}, u32[]{:S(2)}, u32[]{:S(2)}) collective-permute-start(bf16[1536,384]{1,0:T(8,128)(2,1)S(1)} %pad_maximum_fusion.refs_4_), channel_id=1, source_target_pairs={{0,8},{1,9},{2,10},{3,11},{4,12},{5,13},{6,14},{7,15},{8,0},{9,1},... | collective-permute-start | bytes 3538952 | tf_op jit(solution)/shard_map/ppermute | solution.py:28
  130.4 1.4 copy-start
  131.8 0.9 copy-start.3
  132.7 0.9 copy-start.5
  133.7 0.9 copy-start.7
  134.6 0.9 copy-start.9
  135.5 0.9 copy-start.11
  (3 other events, 2.0 us)
Sparse Core Ops, SparseCore 0:
  27.2 42.0 all-gather.1

commit v5 on v3

--- a/solution.py
+++ b/solution.py
@@ -2,7 +2,6 @@
 
 import jax
 import jax.numpy as jnp
-import numpy as np
 from jax import lax
 from jax.experimental import pallas as pl
 from jax.experimental.pallas import tpu as pltpu
@@ -30,6 +29,16 @@
 def gather_x(value):
     groups = [[i * NH + h for i in range(NX)] for h in range(NH)]
     return lax.all_gather(value, "mp", axis_index_groups=groups, axis=0, tiled=True)
+
+
+def share_quad(value):
+    groups = [
+        [((y * NZ) + quad * 4 + i) * NC + core for i in range(4)]
+        for y in range(NY) for quad in range(NZ // 4) for core in range(NC)
+    ]
+    copies = jnp.broadcast_to(value[None], (4,) + value.shape)
+    shared = lax.all_to_all(copies, "dp", 0, 0, axis_index_groups=groups)
+    return shared.reshape(4 * value.shape[0], value.shape[1])
 
 
 def after(*values):
@@ -60,12 +69,24 @@
     return lax.dot_general(a, b, (((1,), (0,)), ((), ())), preferred_element_type=jnp.float32)
 
 
-def reorder_kernel(y_ref, source_ref, in_ref, out_ref):
-    span = source_ref.shape[1]
-    wanted = lax.broadcasted_iota(jnp.int32, (span, span), 0) == source_ref[...]
+def reorder_kernel(at_ref, in_any, out_ref, in_ref, sem):
+    load = pltpu.make_async_copy(in_any, in_ref, sem)
+    load.start()
+    span = in_ref.shape[1] // NY
+    block = span // (NZ * NC)
+    y, z, core = at_ref[0], at_ref[1], at_ref[2]
+    place = lax.broadcasted_iota(jnp.int32, (8, span), 1)
+    half = sum((place >= i * NZ * block).astype(jnp.int32) for i in range(1, NC))
+    slot = sum((place >= i * block).astype(jnp.int32) for i in range(1, NC * NZ))
+    inside = place - slot * block
+    slot = slot & (NZ - 1)
+    quad = ((slot & 1) << 3) | ((slot & 2) << 1)
+    source = (((quad ^ (z & 12)) | (slot >> 2)) * NC + (half ^ core)) * block + inside
+    wanted = lax.broadcasted_iota(jnp.int32, (span, span), 0) == source[0:1]
     pick = jnp.where(wanted, 1.0, 0.0).astype(jnp.bfloat16)
+    load.wait()
     for slot, i in enumerate(Y_ORDER):
-        start = pl.multiple_of((y_ref[0] ^ i) * span, span)
+        start = pl.multiple_of((y ^ i) * span, span)
         out_ref[:, slot * span:(slot + 1) * span] = nn(in_ref[:, pl.ds(start, span)], pick).astype(jnp.bfloat16)
 
 
@@ -78,17 +99,36 @@
         out_ref[head] = raised / jnp.sum(raised, axis=-1, keepdims=True)
 
 
-def tail_kernel(rows_ref, attn_ref, q_ref, k_ref, v_ref, own_ref, far_ref, w_ref, wc_ref, *refs):
-    gq_ref, gk_ref, gv_ref, grad_ref = refs
+def tail_kernel(rows_ref, attn_ref, w_ref, wc_ref, q_any, k_any, v_any, own_any, far_any, *refs):
+    gq_ref, gk_ref, gv_ref, grad_ref, q_ref, k_ref, v_ref, g_ref, sems, band_sems = refs
     scale = 1.0 / math.sqrt(HD)
-    n_g, depth = NX * NH, w_ref.shape[0] // NY
+    n_g = NX * NH
     part = q_ref.shape[0] // n_g
-    parts = [ref[i * depth:(i + 1) * depth] for i in range(NY) for ref in (w_ref, wc_ref)]
-    left = jnp.concatenate([own_ref[...], far_ref[...]], axis=0)
+    rows, depth = own_any.shape[0], w_ref.shape[0] // NY
+    band_copies = []
+    for i in range(NY):
+        band = pl.ds(i * NC * depth, NC * depth)
+        pairs = (
+            (own_any.at[:, band], g_ref.at[:rows, band]),
+            (far_any.at[:, band], g_ref.at[rows:, band]),
+        )
+        band_copies.append([pltpu.make_async_copy(*pair, band_sems.at[i, j]) for j, pair in enumerate(pairs)])
+    copies = [
+        pltpu.make_async_copy(src, dst, sems.at[i])
+        for i, (src, dst) in enumerate(((v_any, v_ref), (k_any, k_ref), (q_any, q_ref)))
+    ]
+    for copy in sum(band_copies, []) + copies:
+        copy.start()
+    weights = [ref[i * depth:(i + 1) * depth] for i in range(NY) for ref in (w_ref, wc_ref)]
     total = None
-    for i, piece in enumerate(parts):
-        term = nn(left[:, i * depth:(i + 1) * depth], piece)
+    for i in range(NY * NC):
+        if i % NC == 0:
+            for copy in band_copies[i // NC]:
+                copy.wait()
+        term = nn(g_ref[:, i * depth:(i + 1) * depth], weights[i])
         total = term if total is None else total + term
+    for copy in copies:
+        copy.wait()
     total = total.astype(jnp.bfloat16)
     for slot in range(n_g):
         row = pl.multiple_of(rows_ref[slot] * part, part)
@@ -106,6 +146,8 @@
 
 
 VMEM = pl.BlockSpec(memory_space=pltpu.VMEM)
+ANY = pl.BlockSpec(memory_space=pl.ANY)
+TAIL_VMEM = 52 * 1024 * 1024
 SMEM = pl.BlockSpec(memory_space=pltpu.SMEM)
 PARAMS = pltpu.CompilerParams(vmem_limit_bytes=16 * 1024 * 1024)
 
@@ -115,24 +157,18 @@
     heads = width // HD
     q, k, v = (a.reshape(patches, width) for a in (queries, attn_keys, attn_values))
     part, model = grad_out.shape[1], grad_out.shape[2]
-    block = out_weight.shape[0]
     dp, mp = lax.axis_index("dp"), lax.axis_index("mp")
     core, z, y = dp % NC, (dp // NC) % NZ, dp // (NC * NZ)
 
-    span = NZ * NC * block
-    place = np.arange(span)
-    z_bits = (place // block) % NZ
-    z_xor = sum(((z_bits >> b) & 1) << (3 - b) for b in range(4))
-    core_xor = place // (NZ * block)
-    source = ((jnp.asarray(z_xor) ^ z) * NC + (jnp.asarray(core_xor) ^ core)) * block + jnp.asarray(place % block)
     own = pl.pallas_call(
         reorder_kernel,
         out_shape=jax.ShapeDtypeStruct((part, model), jnp.bfloat16),
-        in_specs=[SMEM, VMEM, VMEM],
+        in_specs=[SMEM, ANY],
         out_specs=VMEM,
+        scratch_shapes=[pltpu.VMEM((part, model), jnp.bfloat16), pltpu.SemaphoreType.DMA],
         compiler_params=PARAMS,
-        cost_estimate=pl.CostEstimate(flops=2 * part * model * span, bytes_accessed=4 * part * model, transcendentals=0),
-    )(y.reshape(1), source.astype(jnp.int32).reshape(1, span), grad_out.reshape(part, model))
+        cost_estimate=pl.CostEstimate(flops=2 * part * model * model // NY, bytes_accessed=4 * part * model, transcendentals=0),
+    )(jnp.stack([y, z, core]).astype(jnp.int32), grad_out.reshape(part, model))
 
     attn = pl.pallas_call(
         attention_kernel,
@@ -151,8 +187,7 @@
     own = gather_x(own)
     weight, half_way, own = after(weight, half_way, own)
     far = quarter_turn(half_way)
-    weight = jnp.concatenate([weight, swap(weight, z=2)], 0)
-    weight = jnp.concatenate([weight, swap(weight, z=1)], 0)
+    weight = share_quad(weight)
     weight = jnp.concatenate([weight] + [swap(weight, y=i) for i in Y_ORDER[1:]], 0)
     far = gather_x(far)
     weight, far, attn = after(weight, far, attn)
@@ -164,12 +199,18 @@
     outs = pl.pallas_call(
         tail_kernel,
         out_shape=(grad_shape,) * 3,
-        in_specs=[SMEM] + [VMEM] * (6 + len(weights)),
+        in_specs=[SMEM] + [VMEM] * 3 + [ANY] * 5,
         out_specs=(VMEM,) * 3,
-        scratch_shapes=[pltpu.VMEM((patches, width), jnp.bfloat16)],
-        compiler_params=PARAMS,
+        scratch_shapes=[
+            pltpu.VMEM((patches, width), jnp.bfloat16),
+            *[pltpu.VMEM((patches, width), jnp.bfloat16)] * 3,
+            pltpu.VMEM((patches, model), jnp.bfloat16),
+            pltpu.SemaphoreType.DMA((3,)),
+            pltpu.SemaphoreType.DMA((NY, 2)),
+        ],
+        compiler_params=pltpu.CompilerParams(vmem_limit_bytes=TAIL_VMEM),
         cost_estimate=pl.CostEstimate(flops=2 * patches * width * (model + 4 * patches), bytes_accessed=6 << 20, transcendentals=0),
-    )(rows, attn, q, k, v, own, far, *weights)
+    )(rows, attn, *weights, q, k, v, own, far)
     return tuple(o.reshape(1, patches, width) for o in outs)
 
 

time: 120 us -> 118 us (0.983)
  the two profiles are of different devices: /device:TPU:65 before, /device:TPU:129 now
where the time goes in v5:
time: 118 us; the launch traced here: 117 us
  starting transfers between devices  58.6 us (50%)
  blocking collectives  24.8 us (21%)
  waiting for transfers between devices  22 us (19%)
  Pallas kernels  8.43 us (7%)
  local copies, waits for them, and re-layouts  1.78 us (2%)
    ppermute x6, starting transfers between devices, swap(): return lax.ppermute(value, AXES, exchange(**moves))  39.2 us
    all_gather x2, blocking collectives, gather_x(): lax.all_gather(value, 'mp', axis_index_groups=groups, axis=0, tiled=True)  24.8 us
    all_to_all x1, waiting for transfers between devices, share_quad(): shared = lax.all_to_all(copies, 'dp', 0, 0, axis_index_groups=groups)  16.6 us
    ppermute x2, starting transfers between devices, quarter_turn(): return lax.ppermute(value, AXES, pairs)  16 us
    pallas_call x1, Pallas kernels, shards(): pl.pallas_call(tail_kernel, out_shape=(grad_shape,) * 3, in_specs=[SMEM]...  5.92 us
    all_to_all x1, starting transfers between devices, share_quad(): shared = lax.all_to_all(copies, 'dp', 0, 0, axis_index_groups=groups)  3.45 us
    ppermute x6, waiting for transfers between devices, swap(): return lax.ppermute(value, AXES, exchange(**moves))  3.35 us
  transfers between devices with their start and end apart: 9, of which 4 were waited for; matrix products, arithmetic and copies ran while one was open for 1% of the time, Pallas kernels for 2%

profile of v5, /device:TPU:129, one launch (start us, length us, event | category | flops | bytes accessed | tf_op | source)
XLA Modules:
  0.0 117.3 jit_solution(1261549175353533711)
XLA Ops:
  0.6 15.4 %collective-permute-start = (bf16[24,384]{1,0:T(8,128)(2,1)}, bf16[24,384]{1,0:T(8,128)(2,1)S(1)}, u32[]{:S(2)}, u32[]{:S(2)}) collective-permute-start(bf16[24,384]{1,0:T(8,128)(2,1)} %param.8), channel_id=1, source_target_pairs={{0,128},{1,129},{2,130},{3,131},{4,132},{5,133},{6,134},{7,135},{8... | collective-permute-start | bytes 55304 | tf_op jit(solution)/shard_map/ppermute | solution.py:26
  16.1 0.1 pad_add_fusion.at_ref
  16.2 0.9 copy-done.3
  17.1 2.0 %shard_map.76 = bf16[32,3072]{1,0:T(8,128)(2,1)S(1)} custom-call(s32[3]{0:T(128)S(1)} %pad_add_fusion.at_ref, bf16[32,3072]{1,0:T(8,128)(2,1)S(1)} %bitcast.24), custom_call_target="tpu_custom_call" | custom-call | flops 150994944 | bytes 393216 | tf_op jit(solution)/shard_map/pallas_call | solution.py:163
  19.2 10.8 %collective-permute-start.2 = (bf16[32,3072]{1,0:T(8,128)(2,1)S(1)}, bf16[32,3072]{1,0:T(8,128)(2,1)S(1)}, u32[]{:S(2)}, u32[]{:S(2)}) collective-permute-start(bf16[32,3072]{1,0:T(8,128)(2,1)S(1)} %shard_map.76), channel_id=1, source_target_pairs={{0,128},{1,129},{2,130},{3,131},{4,132},{5,133},{6,134},{7,135},{8... | collective-permute-start | bytes 589832 | tf_op jit(solution)/shard_map/ppermute | solution.py:57
  30.0 0.7 pad_maximum_fusion.2
  30.7 5.2 %collective-permute-start.1 = (bf16[48,384]{1,0:T(8,128)(2,1)S(1)}, bf16[48,384]{1,0:T(8,128)(2,1)S(1)}, u32[]{:S(2)}, u32[]{:S(2)}) collective-permute-start(bf16[48,384]{1,0:T(8,128)(2,1)S(1)} %pad_maximum_fusion.2), channel_id=1, source_target_pairs={{0,64},{1,65},{2,66},{3,67},{4,68},{5,69},{6,70},{7,71},{8,72},{9,... | collective-permute-start | bytes 110600 | tf_op jit(solution)/shard_map/ppermute | solution.py:26
  35.9 13.2 %all_gather.6.own_any = bf16[128,3072]{1,0:T(8,128)(2,1)} all-gather(bf16[32,3072]{1,0:T(8,128)(2,1)S(1)} %shard_map.76), channel_id=1, replica_groups={{0,2,4,6},{1,3,5,7},{8,10,12,14},{9,11,13,15},{16,18,20,22},{17,19,21,2..., dimensions={0}, use_global_device_ids=true | all-gather | bytes 983040 | tf_op jit(solution)/shard_map/all_gather | solution.py:31
  49.1 0.9 collective-permute-done.1
  50.0 2.0 %collective-permute-done.2 = bf16[32,3072]{1,0:T(8,128)(2,1)S(1)} collective-permute-done((bf16[32,3072]{1,0:T(8,128)(2,1)S(1)}, bf16[32,3072]{1,0:T(8,128)(2,1)S(1)}, u32[]{:S(2)}, u32[]{:S(2)}) %collective-permute-start.2) | collective-permute-done | bytes 196640 | tf_op jit(solution)/shard_map/ppermute | solution.py:57
  52.0 0.7 broadcast_in_dim.2
  52.7 3.5 %all-to-all-start = ((bf16[4,96,384]{2,1,0:T(8,128)(2,1)}), bf16[4,96,384]{2,1,0:T(8,128)(2,1)S(1)}, u32[]{:S(2)}, u32[]{:S(2)}) async-start(bf16[4,96,384]{2,1,0:T(8,128)(2,1)} %broadcast_in_dim.2), calls=%async_computation | async-start | bytes 589824 | tf_op jit(solution)/shard_map/all_to_all | solution.py:40
  56.2 5.2 %collective-permute-start.6 = (bf16[32,3072]{1,0:T(8,128)(2,1)S(1)}, bf16[32,3072]{1,0:T(8,128)(2,1)S(1)}, u32[]{:S(2)}, u32[]{:S(2)}) collective-permute-start(bf16[32,3072]{1,0:T(8,128)(2,1)S(1)} %collective-permute-done.2), channel_id=1, source_target_pairs={{0,128},{1,129},{2,130},{3,131},{4,132},{5,133},{6,134},{7,135},{8... | collective-permute-start | bytes 589832 | tf_op jit(solution)/shard_map/ppermute | solution.py:57
  61.4 0.5 shard_map.77.attn_ref
  61.9 16.6 %all-to-all-done = bf16[4,96,384]{2,1,0:T(8,128)(2,1)S(1)} async-done(((bf16[4,96,384]{2,1,0:T(8,128)(2,1)}), bf16[4,96,384]{2,1,0:T(8,128)(2,1)S(1)}, u32[]{:S(2)}, u32[]{:S(2)}) %all-to-all-start) | async-done | bytes 294944 | tf_op jit(solution)/shard_map/all_to_all | solution.py:40
  78.5 1.9 %collective-permute-start.5 = (bf16[384,384]{1,0:T(8,128)(2,1)S(1)}, bf16[384,384]{1,0:T(8,128)(2,1)S(1)}, u32[]{:S(2)}, u32[]{:S(2)}) collective-permute-start(bf16[384,384]{1,0:T(8,128)(2,1)S(1)} %bitcast.25), channel_id=1, source_target_pairs={{0,768},{1,769},{2,770},{3,771},{4,772},{5,773},{6,774},{7,775},{8... | collective-permute-start | bytes 884744 | tf_op jit(solution)/shard_map/ppermute | solution.py:26
  80.4 1.9 %collective-permute-start.4 = (bf16[384,384]{1,0:T(8,128)(2,1)S(1)}, bf16[384,384]{1,0:T(8,128)(2,1)S(1)}, u32[]{:S(2)}, u32[]{:S(2)}) collective-permute-start(bf16[384,384]{1,0:T(8,128)(2,1)S(1)} %bitcast.26), channel_id=1, source_target_pairs={{0,256},{1,257},{2,258},{3,259},{4,260},{5,261},{6,262},{7,263},{8... | collective-permute-start | bytes 884744 | tf_op jit(solution)/shard_map/ppermute | solution.py:26
  82.3 5.7 %collective-permute-start.3 = (bf16[384,384]{1,0:T(8,128)(2,1)S(1)}, bf16[384,384]{1,0:T(8,128)(2,1)S(1)}, u32[]{:S(2)}, u32[]{:S(2)}) collective-permute-start(bf16[384,384]{1,0:T(8,128)(2,1)S(1)} %bitcast.27), channel_id=1, source_target_pairs={{0,512},{1,513},{2,514},{3,515},{4,516},{5,517},{6,518},{7,519},{8... | collective-permute-start | bytes 884744 | tf_op jit(solution)/shard_map/ppermute | solution.py:26
  88.1 11.5 %all_gather.7.far_any = bf16[128,3072]{1,0:T(8,128)(2,1)} all-gather(bf16[32,3072]{1,0:T(8,128)(2,1)S(1)} %collective-permute-done.6), channel_id=1, replica_groups={{0,2,4,6},{1,3,5,7},{8,10,12,14},{9,11,13,15},{16,18,20,22},{17,19,21,2..., dimensions={0}, use_global_device_ids=true | all-gather | bytes 983040 | tf_op jit(solution)/shard_map/all_gather | solution.py:31
  99.7 0.1 pad_maximum_fusion.w_ref
  99.8 9.0 %collective-permute-start.7 = (bf16[1536,384]{1,0:T(8,128)(2,1)S(1)}, bf16[1536,384]{1,0:T(8,128)(2,1)}, u32[]{:S(2)}, u32[]{:S(2)}) collective-permute-start(bf16[1536,384]{1,0:T(8,128)(2,1)S(1)} %pad_maximum_fusion.w_ref), channel_id=1, source_target_pairs={{0,8},{1,9},{2,10},{3,11},{4,12},{5,13},{6,14},{7,15},{8,0},{9,1},... | collective-permute-start | bytes 3538952 | tf_op jit(solution)/shard_map/ppermute | solution.py:26
  108.8 0.1 stack.47.rows_ref
  108.9 2.5 %collective-permute-done.7.wc_ref = bf16[1536,384]{1,0:T(8,128)(2,1)} collective-permute-done((bf16[1536,384]{1,0:T(8,128)(2,1)S(1)}, bf16[1536,384]{1,0:T(8,128)(2,1)}, u32[]{:S(2)}, u32[]{:S(2)}) %collective-permute-start.7) | collective-permute-done | bytes 1179680 | tf_op jit(solution)/shard_map/ppermute | solution.py:26
  111.4 5.9 %shard_map.78 = (bf16[256,384]{1,0:T(8,128)(2,1)}, bf16[256,384]{1,0:T(8,128)(2,1)}, bf16[256,384]{1,0:T(8,128)(2,1)}) custom-call(s32[8]{0:T(128)S(1)} %stack.47.rows_ref, f32[3,256,256]{2,1,0:T(8,128)S(1)} %shard_map.77.attn_ref, bf16[1536,384]{1,0:T(8,128)(2,1)} %copy-done.4, bf16[1536,384]{1,0:T(8,128)(2,1)} %collective-permute-done.7.wc_ref, ...), custom_call_target="tpu_custom_call" | custom-call | flops 805306368 | bytes 6291456 | tf_op jit(solution)/shard_map/pallas_call | solution.py:199
  (17 shorter events, 0.0 us)
Async XLA Ops:
  0.6 49.4 %copy-start.5 = (bf16[24,384]{1,0:T(8,128)(2,1)S(1)}, bf16[24,384]{1,0:T(8,128)(2,1)}, u32[]{:S(2)}) copy-start(bf16[24,384]{1,0:T(8,128)(2,1)} %param.8) | copy-start | bytes 55300
  0.6 29.4 %collective-permute-start = (bf16[24,384]{1,0:T(8,128)(2,1)}, bf16[24,384]{1,0:T(8,128)(2,1)S(1)}, u32[]{:S(2)}, u32[]{:S(2)}) collective-permute-start(bf16[24,384]{1,0:T(8,128)(2,1)} %param.8), channel_id=1, source_target_pairs={{0,128},{1,129},{2,130},{3,131},{4,132},{5,133},{6,134},{7,135},{8... | collective-permute-start | bytes 55304 | tf_op jit(solution)/shard_map/ppermute | solution.py:26
  16.2 0.9 copy-start.3
  19.2 42.2 %copy-start = (bf16[1,256,384]{2,1,0:T(8,128)(2,1)S(1)}, bf16[1,256,384]{2,1,0:T(8,128)(2,1)}, u32[]{:S(2)}) copy-start(bf16[1,256,384]{2,1,0:T(8,128)(2,1)} %param.5) | copy-start | bytes 589828
  19.2 42.2 %copy-start.1 = (bf16[1,256,384]{2,1,0:T(8,128)(2,1)S(1)}, bf16[1,256,384]{2,1,0:T(8,128)(2,1)}, u32[]{:S(2)}) copy-start(bf16[1,256,384]{2,1,0:T(8,128)(2,1)} %param.6) | copy-start | bytes 589828
  19.2 32.8 %collective-permute-start.2 = (bf16[32,3072]{1,0:T(8,128)(2,1)S(1)}, bf16[32,3072]{1,0:T(8,128)(2,1)S(1)}, u32[]{:S(2)}, u32[]{:S(2)}) collective-permute-start(bf16[32,3072]{1,0:T(8,128)(2,1)S(1)} %shard_map.76), channel_id=1, source_target_pairs={{0,128},{1,129},{2,130},{3,131},{4,132},{5,133},{6,134},{7,135},{8... | collective-permute-start | bytes 589832 | tf_op jit(solution)/shard_map/ppermute | solution.py:57
  30.7 19.2 %collective-permute-start.1 = (bf16[48,384]{1,0:T(8,128)(2,1)S(1)}, bf16[48,384]{1,0:T(8,128)(2,1)S(1)}, u32[]{:S(2)}, u32[]{:S(2)}) collective-permute-start(bf16[48,384]{1,0:T(8,128)(2,1)S(1)} %pad_maximum_fusion.2), channel_id=1, source_target_pairs={{0,64},{1,65},{2,66},{3,67},{4,68},{5,69},{6,70},{7,71},{8,72},{9,... | collective-permute-start | bytes 110600 | tf_op jit(solution)/shard_map/ppermute | solution.py:26
  52.7 25.7 %all-to-all-start = ((bf16[4,96,384]{2,1,0:T(8,128)(2,1)}), bf16[4,96,384]{2,1,0:T(8,128)(2,1)S(1)}, u32[]{:S(2)}, u32[]{:S(2)}) async-start(bf16[4,96,384]{2,1,0:T(8,128)(2,1)} %broadcast_in_dim.2), calls=%async_computation | async-start | bytes 589824 | tf_op jit(solution)/shard_map/all_to_all | solution.py:40
  56.2 31.9 %collective-permute-start.6 = (bf16[32,3072]{1,0:T(8,128)(2,1)S(1)}, bf16[32,3072]{1,0:T(8,128)(2,1)S(1)}, u32[]{:S(2)}, u32[]{:S(2)}) collective-permute-start(bf16[32,3072]{1,0:T(8,128)(2,1)S(1)} %collective-permute-done.2), channel_id=1, source_target_pairs={{0,128},{1,129},{2,130},{3,131},{4,132},{5,133},{6,134},{7,135},{8... | collective-permute-start | bytes 589832 | tf_op jit(solution)/shard_map/ppermute | solution.py:57
  78.5 21.2 %collective-permute-start.5 = (bf16[384,384]{1,0:T(8,128)(2,1)S(1)}, bf16[384,384]{1,0:T(8,128)(2,1)S(1)}, u32[]{:S(2)}, u32[]{:S(2)}) collective-permute-start(bf16[384,384]{1,0:T(8,128)(2,1)S(1)} %bitcast.25), channel_id=1, source_target_pairs={{0,768},{1,769},{2,770},{3,771},{4,772},{5,773},{6,774},{7,775},{8... | collective-permute-start | bytes 884744 | tf_op jit(solution)/shard_map/ppermute | solution.py:26
  80.4 19.2 %collective-permute-start.4 = (bf16[384,384]{1,0:T(8,128)(2,1)S(1)}, bf16[384,384]{1,0:T(8,128)(2,1)S(1)}, u32[]{:S(2)}, u32[]{:S(2)}) collective-permute-start(bf16[384,384]{1,0:T(8,128)(2,1)S(1)} %bitcast.26), channel_id=1, source_target_pairs={{0,256},{1,257},{2,258},{3,259},{4,260},{5,261},{6,262},{7,263},{8... | collective-permute-start | bytes 884744 | tf_op jit(solution)/shard_map/ppermute | solution.py:26
  82.3 17.3 %collective-permute-start.3 = (bf16[384,384]{1,0:T(8,128)(2,1)S(1)}, bf16[384,384]{1,0:T(8,128)(2,1)S(1)}, u32[]{:S(2)}, u32[]{:S(2)}) collective-permute-start(bf16[384,384]{1,0:T(8,128)(2,1)S(1)} %bitcast.27), channel_id=1, source_target_pairs={{0,512},{1,513},{2,514},{3,515},{4,516},{5,517},{6,518},{7,519},{8... | collective-permute-start | bytes 884744 | tf_op jit(solution)/shard_map/ppermute | solution.py:26
  99.6 11.7 %copy-start.2 = (bf16[1,256,384]{2,1,0:T(8,128)(2,1)S(1)}, bf16[1,256,384]{2,1,0:T(8,128)(2,1)}, u32[]{:S(2)}) copy-start(bf16[1,256,384]{2,1,0:T(8,128)(2,1)} %param.7) | copy-start | bytes 589828
  99.8 11.6 %copy-start.4 = (bf16[1536,384]{1,0:T(8,128)(2,1)}, bf16[1536,384]{1,0:T(8,128)(2,1)S(1)}, u32[]{:S(2)}) copy-start(bf16[1536,384]{1,0:T(8,128)(2,1)S(1)} %pad_maximum_fusion.w_ref) | copy-start | bytes 3538948
  99.8 11.6 %collective-permute-start.7 = (bf16[1536,384]{1,0:T(8,128)(2,1)S(1)}, bf16[1536,384]{1,0:T(8,128)(2,1)}, u32[]{:S(2)}, u32[]{:S(2)}) collective-permute-start(bf16[1536,384]{1,0:T(8,128)(2,1)S(1)} %pad_maximum_fusion.w_ref), channel_id=1, source_target_pairs={{0,8},{1,9},{2,10},{3,11},{4,12},{5,13},{6,14},{7,15},{8,0},{9,1},... | collective-permute-start | bytes 3538952 | tf_op jit(solution)/shard_map/ppermute | solution.py:26

commit v6 on v5

--- a/solution.py
+++ b/solution.py
@@ -10,7 +10,6 @@
 HD = 128
 AXES = ("dp", "mp")
 NY, NZ, NC, NX, NH = 4, 16, 2, 4, 2
-Y_ORDER = (0, 2, 1, 3)
 
 
 def exchange(y=0, z=0, core=0, x=0, half=0):
@@ -26,19 +25,26 @@
     return lax.ppermute(value, AXES, exchange(**moves))
 
 
-def gather_x(value):
-    groups = [[i * NH + h for i in range(NX)] for h in range(NH)]
-    return lax.all_gather(value, "mp", axis_index_groups=groups, axis=0, tiled=True)
-
-
-def share_quad(value):
-    groups = [
-        [((y * NZ) + quad * 4 + i) * NC + core for i in range(4)]
-        for y in range(NY) for quad in range(NZ // 4) for core in range(NC)
-    ]
-    copies = jnp.broadcast_to(value[None], (4,) + value.shape)
-    shared = lax.all_to_all(copies, "dp", 0, 0, axis_index_groups=groups)
-    return shared.reshape(4 * value.shape[0], value.shape[1])
+def share(value, axis, groups):
+    copies = jnp.broadcast_to(value[None], (len(groups[0]),) + value.shape)
+    shared = lax.all_to_all(copies, axis, 0, 0, axis_index_groups=groups)
+    return shared.reshape(-1, value.shape[1])
+
+
+def dp_index(y, z, core):
+    return (y * NZ + z) * NC + core
+
+
+X_GROUPS = [[x * NH + half for x in range(NX)] for half in range(NH)]
+Y_GROUPS = [[dp_index(y, z, core) for y in range(NY)] for z in range(NZ) for core in range(NC)]
+NEAR_GROUPS = [
+    [dp_index(y, quad * 4 + i, core) for i in range(4)]
+    for y in range(NY) for quad in range(4) for core in range(NC)
+]
+FAR_GROUPS = [
+    [dp_index(y, quad * 4 + i, core) for quad in range(4)]
+    for y in range(NY) for i in range(4) for core in range(NC)
+]
 
 
 def after(*values):
@@ -69,25 +75,24 @@
     return lax.dot_general(a, b, (((1,), (0,)), ((), ())), preferred_element_type=jnp.float32)
 
 
-def reorder_kernel(at_ref, in_any, out_ref, in_ref, sem):
+def reorder_kernel(core_ref, in_any, out_ref, in_ref, sem):
     load = pltpu.make_async_copy(in_any, in_ref, sem)
     load.start()
     span = in_ref.shape[1] // NY
     block = span // (NZ * NC)
-    y, z, core = at_ref[0], at_ref[1], at_ref[2]
     place = lax.broadcasted_iota(jnp.int32, (8, span), 1)
     half = sum((place >= i * NZ * block).astype(jnp.int32) for i in range(1, NC))
     slot = sum((place >= i * block).astype(jnp.int32) for i in range(1, NC * NZ))
     inside = place - slot * block
     slot = slot & (NZ - 1)
-    quad = ((slot & 1) << 3) | ((slot & 2) << 1)
-    source = (((quad ^ (z & 12)) | (slot >> 2)) * NC + (half ^ core)) * block + inside
+    z = ((slot & 3) << 2) | (slot >> 2)
+    source = (z * NC + (half ^ core_ref[0])) * block + inside
     wanted = lax.broadcasted_iota(jnp.int32, (span, span), 0) == source[0:1]
     pick = jnp.where(wanted, 1.0, 0.0).astype(jnp.bfloat16)
     load.wait()
-    for slot, i in enumerate(Y_ORDER):
-        start = pl.multiple_of((y ^ i) * span, span)
-        out_ref[:, slot * span:(slot + 1) * span] = nn(in_ref[:, pl.ds(start, span)], pick).astype(jnp.bfloat16)
+    for i in range(NY):
+        cols = pl.ds(i * span, span)
+        out_ref[:, cols] = nn(in_ref[:, cols], pick).astype(jnp.bfloat16)
 
 
 def attention_kernel(q_ref, k_ref, out_ref):
@@ -147,6 +152,7 @@
 
 VMEM = pl.BlockSpec(memory_space=pltpu.VMEM)
 ANY = pl.BlockSpec(memory_space=pl.ANY)
+ATTENTION_HINT = 8 * 10**9
 TAIL_VMEM = 52 * 1024 * 1024
 SMEM = pl.BlockSpec(memory_space=pltpu.SMEM)
 PARAMS = pltpu.CompilerParams(vmem_limit_bytes=16 * 1024 * 1024)
@@ -158,7 +164,6 @@
     q, k, v = (a.reshape(patches, width) for a in (queries, attn_keys, attn_values))
     part, model = grad_out.shape[1], grad_out.shape[2]
     dp, mp = lax.axis_index("dp"), lax.axis_index("mp")
-    core, z, y = dp % NC, (dp // NC) % NZ, dp // (NC * NZ)
 
     own = pl.pallas_call(
         reorder_kernel,
@@ -168,29 +173,26 @@
         scratch_shapes=[pltpu.VMEM((part, model), jnp.bfloat16), pltpu.SemaphoreType.DMA],
         compiler_params=PARAMS,
         cost_estimate=pl.CostEstimate(flops=2 * part * model * model // NY, bytes_accessed=4 * part * model, transcendentals=0),
-    )(jnp.stack([y, z, core]).astype(jnp.int32), grad_out.reshape(part, model))
-
+    )((dp % NC).astype(jnp.int32).reshape(1), grad_out.reshape(part, model))
+
+    weight = share(out_weight, "dp", FAR_GROUPS)
+    half_way = quarter_turn(own)
+    own = lax.all_gather(own, "mp", axis_index_groups=X_GROUPS, axis=0, tiled=True)
+    weight, half_way, own = after(weight, half_way, own)
+    weight = share(weight, "dp", NEAR_GROUPS)
+    far = quarter_turn(half_way)
+    weight = share(weight, "dp", Y_GROUPS)
+    q_late, far = after(q, far)
     attn = pl.pallas_call(
         attention_kernel,
         out_shape=jax.ShapeDtypeStruct((heads, patches, patches), jnp.float32),
         in_specs=[VMEM] * 2,
         out_specs=VMEM,
         compiler_params=PARAMS,
-        cost_estimate=pl.CostEstimate(flops=2 * patches * patches * width, bytes_accessed=1 << 20, transcendentals=0),
-    )(q, k)
-    weight = out_weight
-    arrived = swap(weight, z=8)
-    half_way = quarter_turn(own)
-    own, arrived = after(own, arrived)
-    weight = jnp.concatenate([weight, arrived], 0)
-    weight = jnp.concatenate([weight, swap(weight, z=4)], 0)
-    own = gather_x(own)
-    weight, half_way, own = after(weight, half_way, own)
-    far = quarter_turn(half_way)
-    weight = share_quad(weight)
-    weight = jnp.concatenate([weight] + [swap(weight, y=i) for i in Y_ORDER[1:]], 0)
-    far = gather_x(far)
+        cost_estimate=pl.CostEstimate(flops=ATTENTION_HINT, bytes_accessed=1 << 20, transcendentals=0),
+    )(q_late, k)
     weight, far, attn = after(weight, far, attn)
+    far = share(far, "mp", X_GROUPS)
     weights = [weight, swap(weight, core=1)]
     half = mp % NH
     rows = jnp.stack([i * NH + h for h in (half, 1 - half) for i in range(NX)]).astype(jnp.int32)

time: 118 us -> 126 us (1.068)
  the two profiles are of different devices: /device:TPU:129 before, /device:TPU:160 now
where the time goes in v6:
time: 126 us
  starting transfers between devices  64.7 us (51%)
  waiting for transfers between devices  31.2 us (25%)
  blocking collectives  15 us (12%)
  Pallas kernels  7.89 us (6%)
  local copies, waits for them, and re-layouts  6.14 us (5%)
    all_to_all x4, starting transfers between devices, share(): shared = lax.all_to_all(copies, axis, 0, 0, axis_index_groups=groups)  39.6 us
    all_to_all x4, waiting for transfers between devices, share(): shared = lax.all_to_all(copies, axis, 0, 0, axis_index_groups=groups)  26.1 us
    ppermute x2, starting transfers between devices, quarter_turn(): return lax.ppermute(value, AXES, pairs)  23 us
    all_gather x1, blocking collectives, shards(): lax.all_gather(own, 'mp', axis_index_groups=X_GROUPS, axis=0, tiled=True)  15 us
    pallas_call x1, Pallas kernels, shards(): pl.pallas_call(tail_kernel, out_shape=(grad_shape,) * 3, in_specs=[SMEM]...  5.92 us
    ppermute x2, waiting for transfers between devices, quarter_turn(): return lax.ppermute(value, AXES, pairs)  5.16 us
    broadcast_in_dim x4, local copies, waits for them, and re-layouts, share(): copies = jnp.broadcast_to(value[None], (len(groups[0]),) + value.shape)  4.22 us
  transfers between devices with their start and end apart: 7, of which 5 were waited for; matrix products, arithmetic and copies ran while one was open for 2% of the time, Pallas kernels for 2%

profile of v6, /device:TPU:160, one launch (start us, length us, event | category | flops | bytes accessed | tf_op | source)
XLA Modules:
  0.0 125.7 jit_solution(12642623409683081824)
XLA Ops:
  0.6 1.4 %broadcast_in_dim.10 = bf16[4,24,384]{2,1,0:T(8,128)(2,1)} broadcast(bf16[24,384]{1,0:T(8,128)(2,1)} %param.8), dimensions={1,2} | broadcast | bytes 92160 | tf_op jit(solution)/shard_map/broadcast_in_dim | solution.py:29
  2.0 20.4 %all-to-all-start = ((bf16[4,24,384]{2,1,0:T(8,128)(2,1)}), bf16[4,24,384]{2,1,0:T(8,128)(2,1)S(1)}, u32[]{:S(2)}, u32[]{:S(2)}) async-start(bf16[4,24,384]{2,1,0:T(8,128)(2,1)} %broadcast_in_dim.10), calls=%async_computation | async-start | bytes 147456 | tf_op jit(solution)/shard_map/all_to_all | solution.py:30
  22.4 0.9 copy-done.3
  23.4 1.5 %shard_map.76 = bf16[32,3072]{1,0:T(8,128)(2,1)S(1)} custom-call(s32[1]{0:T(128)} %bitcast.9.core_ref, bf16[32,3072]{1,0:T(8,128)(2,1)S(1)} %bitcast.25), custom_call_target="tpu_custom_call" | custom-call | flops 150994944 | bytes 393216 | tf_op jit(solution)/shard_map/pallas_call | solution.py:168
  24.9 12.1 %collective-permute-start = (bf16[32,3072]{1,0:T(8,128)(2,1)S(1)}, bf16[32,3072]{1,0:T(8,128)(2,1)S(1)}, u32[]{:S(2)}, u32[]{:S(2)}) collective-permute-start(bf16[32,3072]{1,0:T(8,128)(2,1)S(1)} %shard_map.76), channel_id=1, source_target_pairs={{0,128},{1,129},{2,130},{3,131},{4,132},{5,133},{6,134},{7,135},{8... | collective-permute-start | bytes 589832 | tf_op jit(solution)/shard_map/ppermute | solution.py:63
  37.0 15.0 %all_gather.3.own_any = bf16[128,3072]{1,0:T(8,128)(2,1)} all-gather(bf16[32,3072]{1,0:T(8,128)(2,1)S(1)} %shard_map.76), channel_id=1, replica_groups={{0,2,4,6},{1,3,5,7},{8,10,12,14},{9,11,13,15},{16,18,20,22},{17,19,21,2..., dimensions={0}, use_global_device_ids=true | all-gather | bytes 983040 | tf_op jit(solution)/shard_map/all_gather | solution.py:180
  52.0 0.7 collective-permute-done
  52.7 0.0 all-to-all-done
  52.7 0.7 broadcast_in_dim.11
  53.4 9.0 %all-to-all-start.1 = ((bf16[4,96,384]{2,1,0:T(8,128)(2,1)}), bf16[4,96,384]{2,1,0:T(8,128)(2,1)S(1)}, u32[]{:S(2)}, u32[]{:S(2)}) async-start(bf16[4,96,384]{2,1,0:T(8,128)(2,1)} %broadcast_in_dim.11), calls=%async_computation.1 | async-start | bytes 589824 | tf_op jit(solution)/shard_map/all_to_all | solution.py:30
  62.5 10.9 %collective-permute-start.1 = (bf16[32,3072]{1,0:T(8,128)(2,1)S(1)}, bf16[32,3072]{1,0:T(8,128)(2,1)S(1)}, u32[]{:S(2)}, u32[]{:S(2)}) collective-permute-start(bf16[32,3072]{1,0:T(8,128)(2,1)S(1)} %collective-permute-done), channel_id=1, source_target_pairs={{0,128},{1,129},{2,130},{3,131},{4,132},{5,133},{6,134},{7,135},{8... | collective-permute-start | bytes 589832 | tf_op jit(solution)/shard_map/ppermute | solution.py:63
  73.4 6.6 %all-to-all-done.1 = bf16[4,96,384]{2,1,0:T(8,128)(2,1)S(1)} async-done(((bf16[4,96,384]{2,1,0:T(8,128)(2,1)}), bf16[4,96,384]{2,1,0:T(8,128)(2,1)S(1)}, u32[]{:S(2)}, u32[]{:S(2)}) %all-to-all-start.1) | async-done | bytes 294944 | tf_op jit(solution)/shard_map/all_to_all | solution.py:30
  80.0 1.1 broadcast_in_dim.13
  81.1 4.6 %all-to-all-start.2 = ((bf16[4,384,384]{2,1,0:T(8,128)(2,1)}), bf16[4,384,384]{2,1,0:T(8,128)(2,1)S(1)}, u32[]{:S(2)}, u32[]{:S(2)}) async-start(bf16[4,384,384]{2,1,0:T(8,128)(2,1)} %broadcast_in_dim.13), calls=%async_computation.2 | async-start | bytes 2359296 | tf_op jit(solution)/shard_map/all_to_all | solution.py:30
  85.7 4.5 %collective-permute-done.1 = bf16[32,3072]{1,0:T(8,128)(2,1)S(1)} collective-permute-done((bf16[32,3072]{1,0:T(8,128)(2,1)S(1)}, bf16[32,3072]{1,0:T(8,128)(2,1)S(1)}, u32[]{:S(2)}, u32[]{:S(2)}) %collective-permute-start.1) | collective-permute-done | bytes 196640 | tf_op jit(solution)/shard_map/ppermute | solution.py:63
  90.2 0.5 shard_map.77.attn_ref
  90.7 6.6 %all-to-all-done.2 = bf16[4,384,384]{2,1,0:T(8,128)(2,1)S(1)} async-done(((bf16[4,384,384]{2,1,0:T(8,128)(2,1)}), bf16[4,384,384]{2,1,0:T(8,128)(2,1)S(1)}, u32[]{:S(2)}, u32[]{:S(2)}) %all-to-all-start.2) | async-done | bytes 1179680 | tf_op jit(solution)/shard_map/all_to_all | solution.py:30
  97.3 2.0 %collective-permute-start.2 = (bf16[1536,384]{1,0:T(8,128)(2,1)S(1)}, bf16[1536,384]{1,0:T(8,128)(2,1)}, u32[]{:S(2)}, u32[]{:S(2)}) collective-permute-start(bf16[1536,384]{1,0:T(8,128)(2,1)S(1)} %bitcast.26), channel_id=1, source_target_pairs={{0,8},{1,9},{2,10},{3,11},{4,12},{5,13},{6,14},{7,15},{8,0},{9,1},... | collective-permute-start | bytes 3538952 | tf_op jit(solution)/shard_map/ppermute | solution.py:25
  99.4 1.0 broadcast_in_dim.14
  100.4 5.6 %all-to-all-start.3 = ((bf16[4,32,3072]{2,1,0:T(8,128)(2,1)}), bf16[4,32,3072]{2,1,0:T(8,128)(2,1)S(1)}, u32[]{:S(2)}, u32[]{:S(2)}) async-start(bf16[4,32,3072]{2,1,0:T(8,128)(2,1)} %broadcast_in_dim.14), calls=%async_computation.3 | async-start | bytes 1572864 | tf_op jit(solution)/shard_map/all_to_all | solution.py:30
  105.9 0.1 stack.35.rows_ref
  106.0 12.9 %all-to-all-done.3 = bf16[4,32,3072]{2,1,0:T(8,128)(2,1)S(1)} async-done(((bf16[4,32,3072]{2,1,0:T(8,128)(2,1)}), bf16[4,32,3072]{2,1,0:T(8,128)(2,1)S(1)}, u32[]{:S(2)}, u32[]{:S(2)}) %all-to-all-start.3) | async-done | bytes 786464 | tf_op jit(solution)/shard_map/all_to_all | solution.py:30
  118.9 0.9 copy-done.5
  119.8 5.9 %shard_map.78 = (bf16[256,384]{1,0:T(8,128)(2,1)}, bf16[256,384]{1,0:T(8,128)(2,1)}, bf16[256,384]{1,0:T(8,128)(2,1)}) custom-call(s32[8]{0:T(128)S(1)} %stack.35.rows_ref, f32[3,256,256]{2,1,0:T(8,128)S(1)} %shard_map.77.attn_ref, bf16[1536,384]{1,0:T(8,128)(2,1)} %bitcast.27, bf16[1536,384]{1,0:T(8,128)(2,1)} %collective-permute-done.2.wc_ref, ...), custom_call_target="tpu_custom_call" | custom-call | flops 805306368 | bytes 6291456 | tf_op jit(solution)/shard_map/pallas_call | solution.py:201
  (11 shorter events, 0.0 us)
Async XLA Ops:
  2.0 50.7 %all-to-all-start = ((bf16[4,24,384]{2,1,0:T(8,128)(2,1)}), bf16[4,24,384]{2,1,0:T(8,128)(2,1)S(1)}, u32[]{:S(2)}, u32[]{:S(2)}) async-start(bf16[4,24,384]{2,1,0:T(8,128)(2,1)} %broadcast_in_dim.10), calls=%async_computation | async-start | bytes 147456 | tf_op jit(solution)/shard_map/all_to_all | solution.py:30
  22.4 0.9 copy-start.3
  24.9 27.8 %collective-permute-start = (bf16[32,3072]{1,0:T(8,128)(2,1)S(1)}, bf16[32,3072]{1,0:T(8,128)(2,1)S(1)}, u32[]{:S(2)}, u32[]{:S(2)}) collective-permute-start(bf16[32,3072]{1,0:T(8,128)(2,1)S(1)} %shard_map.76), channel_id=1, source_target_pairs={{0,128},{1,129},{2,130},{3,131},{4,132},{5,133},{6,134},{7,135},{8... | collective-permute-start | bytes 589832 | tf_op jit(solution)/shard_map/ppermute | solution.py:63
  53.4 26.5 %all-to-all-start.1 = ((bf16[4,96,384]{2,1,0:T(8,128)(2,1)}), bf16[4,96,384]{2,1,0:T(8,128)(2,1)S(1)}, u32[]{:S(2)}, u32[]{:S(2)}) async-start(bf16[4,96,384]{2,1,0:T(8,128)(2,1)} %broadcast_in_dim.11), calls=%async_computation.1 | async-start | bytes 589824 | tf_op jit(solution)/shard_map/all_to_all | solution.py:30
  62.5 27.8 %collective-permute-start.1 = (bf16[32,3072]{1,0:T(8,128)(2,1)S(1)}, bf16[32,3072]{1,0:T(8,128)(2,1)S(1)}, u32[]{:S(2)}, u32[]{:S(2)}) collective-permute-start(bf16[32,3072]{1,0:T(8,128)(2,1)S(1)} %collective-permute-done), channel_id=1, source_target_pairs={{0,128},{1,129},{2,130},{3,131},{4,132},{5,133},{6,134},{7,135},{8... | collective-permute-start | bytes 589832 | tf_op jit(solution)/shard_map/ppermute | solution.py:63
  81.1 9.1 %copy-start = (bf16[1,256,384]{2,1,0:T(8,128)(2,1)S(1)}, bf16[1,256,384]{2,1,0:T(8,128)(2,1)}, u32[]{:S(2)}) copy-start(bf16[1,256,384]{2,1,0:T(8,128)(2,1)} %param.5) | copy-start | bytes 589828
  81.1 9.1 %copy-start.1 = (bf16[1,256,384]{2,1,0:T(8,128)(2,1)S(1)}, bf16[1,256,384]{2,1,0:T(8,128)(2,1)}, u32[]{:S(2)}) copy-start(bf16[1,256,384]{2,1,0:T(8,128)(2,1)} %param.6) | copy-start | bytes 589828
  81.1 16.2 %all-to-all-start.2 = ((bf16[4,384,384]{2,1,0:T(8,128)(2,1)}), bf16[4,384,384]{2,1,0:T(8,128)(2,1)S(1)}, u32[]{:S(2)}, u32[]{:S(2)}) async-start(bf16[4,384,384]{2,1,0:T(8,128)(2,1)} %broadcast_in_dim.13), calls=%async_computation.2 | async-start | bytes 2359296 | tf_op jit(solution)/shard_map/all_to_all | solution.py:30
  97.3 3.0 %copy-start.4 = (bf16[4,384,384]{2,1,0:T(8,128)(2,1)}, bf16[4,384,384]{2,1,0:T(8,128)(2,1)S(1)}, u32[]{:S(2)}) copy-start(bf16[4,384,384]{2,1,0:T(8,128)(2,1)S(1)} %all-to-all-done.2) | copy-start | bytes 3538948
  97.3 22.4 %copy-start.2 = (bf16[1,256,384]{2,1,0:T(8,128)(2,1)S(1)}, bf16[1,256,384]{2,1,0:T(8,128)(2,1)}, u32[]{:S(2)}) copy-start(bf16[1,256,384]{2,1,0:T(8,128)(2,1)} %param.7) | copy-start | bytes 589828
  97.3 21.5 %collective-permute-start.2 = (bf16[1536,384]{1,0:T(8,128)(2,1)S(1)}, bf16[1536,384]{1,0:T(8,128)(2,1)}, u32[]{:S(2)}, u32[]{:S(2)}) collective-permute-start(bf16[1536,384]{1,0:T(8,128)(2,1)S(1)} %bitcast.26), channel_id=1, source_target_pairs={{0,8},{1,9},{2,10},{3,11},{4,12},{5,13},{6,14},{7,15},{8,0},{9,1},... | collective-permute-start | bytes 3538952 | tf_op jit(solution)/shard_map/ppermute | solution.py:25
  100.4 18.5 %all-to-all-start.3 = ((bf16[4,32,3072]{2,1,0:T(8,128)(2,1)}), bf16[4,32,3072]{2,1,0:T(8,128)(2,1)S(1)}, u32[]{:S(2)}, u32[]{:S(2)}) async-start(bf16[4,32,3072]{2,1,0:T(8,128)(2,1)} %broadcast_in_dim.14), calls=%async_computation.3 | async-start | bytes 1572864 | tf_op jit(solution)/shard_map/all_to_all | solution.py:30
  118.9 0.9 copy-start.5

commit v7 on v6

--- a/solution.py
+++ b/solution.py
@@ -10,6 +10,7 @@
 HD = 128
 AXES = ("dp", "mp")
 NY, NZ, NC, NX, NH = 4, 16, 2, 4, 2
+X_ORDER = (0, 2, 1, 3)
 
 
 def exchange(y=0, z=0, core=0, x=0, half=0):
@@ -40,10 +41,6 @@
 NEAR_GROUPS = [
     [dp_index(y, quad * 4 + i, core) for i in range(4)]
     for y in range(NY) for quad in range(4) for core in range(NC)
-]
-FAR_GROUPS = [
-    [dp_index(y, quad * 4 + i, core) for quad in range(4)]
-    for y in range(NY) for i in range(4) for core in range(NC)
 ]
 
 
@@ -75,18 +72,19 @@
     return lax.dot_general(a, b, (((1,), (0,)), ((), ())), preferred_element_type=jnp.float32)
 
 
-def reorder_kernel(core_ref, in_any, out_ref, in_ref, sem):
+def reorder_kernel(at_ref, in_any, out_ref, in_ref, sem):
     load = pltpu.make_async_copy(in_any, in_ref, sem)
     load.start()
     span = in_ref.shape[1] // NY
     block = span // (NZ * NC)
+    z, core = at_ref[0], at_ref[1]
     place = lax.broadcasted_iota(jnp.int32, (8, span), 1)
     half = sum((place >= i * NZ * block).astype(jnp.int32) for i in range(1, NC))
     slot = sum((place >= i * block).astype(jnp.int32) for i in range(1, NC * NZ))
     inside = place - slot * block
     slot = slot & (NZ - 1)
-    z = ((slot & 3) << 2) | (slot >> 2)
-    source = (z * NC + (half ^ core_ref[0])) * block + inside
+    quad = ((slot & 1) << 3) | ((slot & 2) << 1)
+    source = (((quad ^ (z & 12)) | (slot >> 2)) * NC + (half ^ core)) * block + inside
     wanted = lax.broadcasted_iota(jnp.int32, (span, span), 0) == source[0:1]
     pick = jnp.where(wanted, 1.0, 0.0).astype(jnp.bfloat16)
     load.wait()
@@ -104,33 +102,24 @@
         out_ref[head] = raised / jnp.sum(raised, axis=-1, keepdims=True)
 
 
-def tail_kernel(rows_ref, attn_ref, w_ref, wc_ref, q_any, k_any, v_any, own_any, far_any, *refs):
-    gq_ref, gk_ref, gv_ref, grad_ref, q_ref, k_ref, v_ref, g_ref, sems, band_sems = refs
+def tail_kernel(rows_ref, attn_ref, w_ref, wc_ref, own_ref, *refs):
+    far_refs, (q_any, k_any, v_any, *refs) = refs[:NX], refs[NX:]
+    gq_ref, gk_ref, gv_ref, grad_ref, q_ref, k_ref, v_ref, sems = refs
     scale = 1.0 / math.sqrt(HD)
     n_g = NX * NH
-    part = q_ref.shape[0] // n_g
-    rows, depth = own_any.shape[0], w_ref.shape[0] // NY
-    band_copies = []
-    for i in range(NY):
-        band = pl.ds(i * NC * depth, NC * depth)
-        pairs = (
-            (own_any.at[:, band], g_ref.at[:rows, band]),
-            (far_any.at[:, band], g_ref.at[rows:, band]),
-        )
-        band_copies.append([pltpu.make_async_copy(*pair, band_sems.at[i, j]) for j, pair in enumerate(pairs)])
+    part, depth = far_refs[0].shape[0], w_ref.shape[0] // NY
     copies = [
         pltpu.make_async_copy(src, dst, sems.at[i])
         for i, (src, dst) in enumerate(((v_any, v_ref), (k_any, k_ref), (q_any, q_ref)))
     ]
-    for copy in sum(band_copies, []) + copies:
+    for copy in copies:
         copy.start()
     weights = [ref[i * depth:(i + 1) * depth] for i in range(NY) for ref in (w_ref, wc_ref)]
     total = None
     for i in range(NY * NC):
-        if i % NC == 0:
-            for copy in band_copies[i // NC]:
-                copy.wait()
-        term = nn(g_ref[:, i * depth:(i + 1) * depth], weights[i])
+        band = pl.ds(i * depth, depth)
+        left = jnp.concatenate([ref[:, band] for ref in (own_ref, *far_refs)], axis=0)
+        term = nn(left, weights[i])
         total = term if total is None else total + term
     for copy in copies:
         copy.wait()
@@ -153,7 +142,8 @@
 VMEM = pl.BlockSpec(memory_space=pltpu.VMEM)
 ANY = pl.BlockSpec(memory_space=pl.ANY)
 ATTENTION_HINT = 8 * 10**9
-TAIL_VMEM = 52 * 1024 * 1024
+TAIL_VMEM = 40 * 1024 * 1024
+REORDER_VMEM = 60 * 1024 * 1024
 SMEM = pl.BlockSpec(memory_space=pltpu.SMEM)
 PARAMS = pltpu.CompilerParams(vmem_limit_bytes=16 * 1024 * 1024)
 
@@ -164,6 +154,7 @@
     q, k, v = (a.reshape(patches, width) for a in (queries, attn_keys, attn_values))
     part, model = grad_out.shape[1], grad_out.shape[2]
     dp, mp = lax.axis_index("dp"), lax.axis_index("mp")
+    core, z = dp % NC, (dp // NC) % NZ
 
     own = pl.pallas_call(
         reorder_kernel,
@@ -171,12 +162,16 @@
         in_specs=[SMEM, ANY],
         out_specs=VMEM,
         scratch_shapes=[pltpu.VMEM((part, model), jnp.bfloat16), pltpu.SemaphoreType.DMA],
-        compiler_params=PARAMS,
+        compiler_params=pltpu.CompilerParams(vmem_limit_bytes=REORDER_VMEM),
         cost_estimate=pl.CostEstimate(flops=2 * part * model * model // NY, bytes_accessed=4 * part * model, transcendentals=0),
-    )((dp % NC).astype(jnp.int32).reshape(1), grad_out.reshape(part, model))
-
-    weight = share(out_weight, "dp", FAR_GROUPS)
+    )(jnp.stack([z, core]).astype(jnp.int32), grad_out.reshape(part, model))
+
+    weight = out_weight
+    arrived = swap(weight, z=8)
     half_way = quarter_turn(own)
+    own, arrived = after(own, arrived)
+    weight = jnp.concatenate([weight, arrived], 0)
+    weight = jnp.concatenate([weight, swap(weight, z=4)], 0)
     own = lax.all_gather(own, "mp", axis_index_groups=X_GROUPS, axis=0, tiled=True)
     weight, half_way, own = after(weight, half_way, own)
     weight = share(weight, "dp", NEAR_GROUPS)
@@ -191,28 +186,27 @@
         compiler_params=PARAMS,
         cost_estimate=pl.CostEstimate(flops=ATTENTION_HINT, bytes_accessed=1 << 20, transcendentals=0),
     )(q_late, k)
-    weight, far, attn = after(weight, far, attn)
-    far = share(far, "mp", X_GROUPS)
+    weight, attn, far = after(weight, attn, far)
+    far = [far] + [swap(far, x=i) for i in X_ORDER[1:]]
     weights = [weight, swap(weight, core=1)]
     half = mp % NH
-    rows = jnp.stack([i * NH + h for h in (half, 1 - half) for i in range(NX)]).astype(jnp.int32)
+    rows = [i * NH + half for i in range(NX)] + [mp ^ (i * NH + 1) for i in X_ORDER]
+    rows = jnp.stack(rows).astype(jnp.int32)
 
     grad_shape = jax.ShapeDtypeStruct((patches, width), jnp.bfloat16)
     outs = pl.pallas_call(
         tail_kernel,
         out_shape=(grad_shape,) * 3,
-        in_specs=[SMEM] + [VMEM] * 3 + [ANY] * 5,
+        in_specs=[SMEM] + [VMEM] * (4 + len(far)) + [ANY] * 3,
         out_specs=(VMEM,) * 3,
         scratch_shapes=[
             pltpu.VMEM((patches, width), jnp.bfloat16),
             *[pltpu.VMEM((patches, width), jnp.bfloat16)] * 3,
-            pltpu.VMEM((patches, model), jnp.bfloat16),
             pltpu.SemaphoreType.DMA((3,)),
-            pltpu.SemaphoreType.DMA((NY, 2)),
         ],
         compiler_params=pltpu.CompilerParams(vmem_limit_bytes=TAIL_VMEM),
         cost_estimate=pl.CostEstimate(flops=2 * patches * width * (model + 4 * patches), bytes_accessed=6 << 20, transcendentals=0),
-    )(rows, attn, *weights, q, k, v, own, far)
+    )(rows, attn, *weights, own, *far, q, k, v)
     return tuple(o.reshape(1, patches, width) for o in outs)
 
 

time: 126 us -> 130 us (1.032)
  the two profiles are of different devices: /device:TPU:160 before, /device:TPU:128 now
where the time goes in v7:
time: 130 us; the launch traced here: 129 us
  starting transfers between devices  64.1 us (49%)
  waiting for transfers between devices  33.5 us (26%)
  blocking collectives  14.6 us (11%)
  Pallas kernels  8.56 us (7%)
  local copies, waits for them, and re-layouts  6.04 us (5%)
  other arithmetic  1.33 us (1%)
    ppermute x6, starting transfers between devices, swap(): return lax.ppermute(value, AXES, exchange(**moves))  38.3 us
    all_to_all x2, waiting for transfers between devices, share(): shared = lax.all_to_all(copies, axis, 0, 0, axis_index_groups=groups)  25.3 us
    all_gather x1, blocking collectives, shards(): lax.all_gather(own, 'mp', axis_index_groups=X_GROUPS, axis=0, tiled=True)  14.6 us
    all_to_all x2, starting transfers between devices, share(): shared = lax.all_to_all(copies, axis, 0, 0, axis_index_groups=groups)  13.6 us
    ppermute x2, starting transfers between devices, quarter_turn(): return lax.ppermute(value, AXES, pairs)  12.2 us
    ppermute x6, waiting for transfers between devices, swap(): return lax.ppermute(value, AXES, exchange(**moves))  7.49 us
    pallas_call x1, Pallas kernels, shards(): pl.pallas_call(tail_kernel, out_shape=(grad_shape,) * 3, in_specs=[SMEM]...  4.93 us
    unnamed x16, local copies, waits for them, and re-layouts  4.07 us
  transfers between devices with their start and end apart: 10, of which 6 were waited for; matrix products, arithmetic and copies ran while one was open for 2% of the time, Pallas kernels for 3%

profile of v7, /device:TPU:128, one launch (start us, length us, event | category | flops | bytes accessed | tf_op | source)
XLA Modules:
  0.0 129.0 jit_solution(16612328628861682009)
XLA Ops:
  0.6 15.7 %collective-permute-start = (bf16[24,384]{1,0:T(8,128)(2,1)}, bf16[24,384]{1,0:T(8,128)(2,1)S(1)}, u32[]{:S(2)}, u32[]{:S(2)}) collective-permute-start(bf16[24,384]{1,0:T(8,128)(2,1)} %param.8), channel_id=1, source_target_pairs={{0,128},{1,129},{2,130},{3,131},{4,132},{5,133},{6,134},{7,135},{8... | collective-permute-start | bytes 55304 | tf_op jit(solution)/shard_map/ppermute | solution.py:26
  17.0 3.2 %shard_map.76 = bf16[32,3072]{1,0:T(8,128)(2,1)} custom-call(s32[2]{0:T(128)} %pad_add_fusion.at_ref, bf16[32,3072]{1,0:T(8,128)(2,1)} %bitcast.27), custom_call_target="tpu_custom_call" | custom-call | flops 150994944 | bytes 393216 | tf_op jit(solution)/shard_map/pallas_call | solution.py:159
  20.2 1.9 %collective-permute-start.2 = (bf16[32,3072]{1,0:T(8,128)(2,1)}, bf16[32,3072]{1,0:T(8,128)(2,1)S(1)}, u32[]{:S(2)}, u32[]{:S(2)}) collective-permute-start(bf16[32,3072]{1,0:T(8,128)(2,1)} %shard_map.76), channel_id=1, source_target_pairs={{0,128},{1,129},{2,130},{3,131},{4,132},{5,133},{6,134},{7,135},{8... | collective-permute-start | bytes 589832 | tf_op jit(solution)/shard_map/ppermute | solution.py:60
  22.1 0.7 pad_maximum_fusion.1
  22.8 10.2 %collective-permute-start.1 = (bf16[48,384]{1,0:T(8,128)(2,1)S(1)}, bf16[48,384]{1,0:T(8,128)(2,1)S(1)}, u32[]{:S(2)}, u32[]{:S(2)}) collective-permute-start(bf16[48,384]{1,0:T(8,128)(2,1)S(1)} %pad_maximum_fusion.1), channel_id=1, source_target_pairs={{0,64},{1,65},{2,66},{3,67},{4,68},{5,69},{6,70},{7,71},{8,72},{9,... | collective-permute-start | bytes 110600 | tf_op jit(solution)/shard_map/ppermute | solution.py:26
  33.0 14.6 %all_gather.3.own_ref = bf16[128,3072]{1,0:T(8,128)(2,1)S(1)} all-gather(bf16[32,3072]{1,0:T(8,128)(2,1)} %shard_map.76), channel_id=1, replica_groups={{0,2,4,6},{1,3,5,7},{8,10,12,14},{9,11,13,15},{16,18,20,22},{17,19,21,2..., dimensions={0}, use_global_device_ids=true | all-gather | bytes 983040 | tf_op jit(solution)/shard_map/all_gather | solution.py:175
  48.4 0.7 broadcast_in_dim.6
  49.1 6.6 %all-to-all-start = ((bf16[4,96,384]{2,1,0:T(8,128)(2,1)}), bf16[4,96,384]{2,1,0:T(8,128)(2,1)S(1)}, u32[]{:S(2)}, u32[]{:S(2)}) async-start(bf16[4,96,384]{2,1,0:T(8,128)(2,1)} %broadcast_in_dim.6), calls=%async_computation | async-start | bytes 589824 | tf_op jit(solution)/shard_map/all_to_all | solution.py:31
  55.7 10.3 %collective-permute-start.3 = (bf16[32,3072]{1,0:T(8,128)(2,1)S(1)}, bf16[32,3072]{1,0:T(8,128)(2,1)S(1)}, u32[]{:S(2)}, u32[]{:S(2)}) collective-permute-start(bf16[32,3072]{1,0:T(8,128)(2,1)S(1)} %collective-permute-done.2), channel_id=1, source_target_pairs={{0,128},{1,129},{2,130},{3,131},{4,132},{5,133},{6,134},{7,135},{8... | collective-permute-start | bytes 589832 | tf_op jit(solution)/shard_map/ppermute | solution.py:60
  66.0 13.2 %all-to-all-done = bf16[4,96,384]{2,1,0:T(8,128)(2,1)S(1)} async-done(((bf16[4,96,384]{2,1,0:T(8,128)(2,1)}), bf16[4,96,384]{2,1,0:T(8,128)(2,1)S(1)}, u32[]{:S(2)}, u32[]{:S(2)}) %all-to-all-start) | async-done | bytes 294944 | tf_op jit(solution)/shard_map/all_to_all | solution.py:31
  79.2 1.1 broadcast_in_dim.15
  80.4 7.0 %all-to-all-start.1 = ((bf16[4,384,384]{2,1,0:T(8,128)(2,1)}), bf16[4,384,384]{2,1,0:T(8,128)(2,1)S(1)}, u32[]{:S(2)}, u32[]{:S(2)}) async-start(bf16[4,384,384]{2,1,0:T(8,128)(2,1)} %broadcast_in_dim.15), calls=%async_computation.1 | async-start | bytes 2359296 | tf_op jit(solution)/shard_map/all_to_all | solution.py:31
  88.1 0.9 copy-done
  88.9 12.1 %all-to-all-done.1 = bf16[4,384,384]{2,1,0:T(8,128)(2,1)S(1)} async-done(((bf16[4,384,384]{2,1,0:T(8,128)(2,1)}), bf16[4,384,384]{2,1,0:T(8,128)(2,1)S(1)}, u32[]{:S(2)}, u32[]{:S(2)}) %all-to-all-start.1) | async-done | bytes 1179680 | tf_op jit(solution)/shard_map/all_to_all | solution.py:31
  101.1 1.9 %collective-permute-start.4 = (bf16[1536,384]{1,0:T(8,128)(2,1)S(1)}, bf16[1536,384]{1,0:T(8,128)(2,1)S(1)}, u32[]{:S(2)}, u32[]{:S(2)}) collective-permute-start(bf16[1536,384]{1,0:T(8,128)(2,1)S(1)} %bitcast.19), channel_id=1, source_target_pairs={{0,8},{1,9},{2,10},{3,11},{4,12},{5,13},{6,14},{7,15},{8,0},{9,1},... | collective-permute-start | bytes 3538952 | tf_op jit(solution)/shard_map/ppermute | solution.py:26
  103.0 2.5 %collective-permute-start.7 = (bf16[32,3072]{1,0:T(8,128)(2,1)}, bf16[32,3072]{1,0:T(8,128)(2,1)}, u32[]{:S(2)}, u32[]{:S(2)}) collective-permute-start(bf16[32,3072]{1,0:T(8,128)(2,1)} %copy-done.5), channel_id=1, source_target_pairs={{0,6},{1,7},{2,4},{3,5},{4,2},{5,3},{6,0},{7,1},{8,14},{9,15},{10,... | collective-permute-start | bytes 589832 | tf_op jit(solution)/shard_map/ppermute | solution.py:26
  105.6 2.1 %collective-permute-start.6 = (bf16[32,3072]{1,0:T(8,128)(2,1)}, bf16[32,3072]{1,0:T(8,128)(2,1)}, u32[]{:S(2)}, u32[]{:S(2)}) collective-permute-start(bf16[32,3072]{1,0:T(8,128)(2,1)} %copy-done.5), channel_id=1, source_target_pairs={{0,2},{1,3},{2,0},{3,1},{4,6},{5,7},{6,4},{7,5},{8,10},{9,11},{10,... | collective-permute-start | bytes 589832 | tf_op jit(solution)/shard_map/ppermute | solution.py:26
  107.7 5.7 %collective-permute-start.5 = (bf16[32,3072]{1,0:T(8,128)(2,1)}, bf16[32,3072]{1,0:T(8,128)(2,1)}, u32[]{:S(2)}, u32[]{:S(2)}) collective-permute-start(bf16[32,3072]{1,0:T(8,128)(2,1)} %copy-done.5), channel_id=1, source_target_pairs={{0,4},{1,5},{2,6},{3,7},{4,0},{5,1},{6,2},{7,3},{8,12},{9,13},{10,... | collective-permute-start | bytes 589832 | tf_op jit(solution)/shard_map/ppermute | solution.py:26
  113.7 1.8 %collective-permute-done.6.refs_2_ = bf16[32,3072]{1,0:T(8,128)(2,1)} collective-permute-done((bf16[32,3072]{1,0:T(8,128)(2,1)}, bf16[32,3072]{1,0:T(8,128)(2,1)}, u32[]{:S(2)}, u32[]{:S(2)}) %collective-permute-start.6) | collective-permute-done | bytes 196640 | tf_op jit(solution)/shard_map/ppermute | solution.py:26
  115.5 5.5 %collective-permute-done.5.refs_1_ = bf16[32,3072]{1,0:T(8,128)(2,1)} collective-permute-done((bf16[32,3072]{1,0:T(8,128)(2,1)}, bf16[32,3072]{1,0:T(8,128)(2,1)}, u32[]{:S(2)}, u32[]{:S(2)}) %collective-permute-start.5) | collective-permute-done | bytes 196640 | tf_op jit(solution)/shard_map/ppermute | solution.py:26
  121.1 1.1 copy-done.1
  122.2 0.9 copy-done.4
  123.1 0.9 copy-done.6
  124.0 4.9 %shard_map.78 = (bf16[256,384]{1,0:T(8,128)(2,1)}, bf16[256,384]{1,0:T(8,128)(2,1)}, bf16[256,384]{1,0:T(8,128)(2,1)}) custom-call(s32[8]{0:T(128)S(1)} %stack.44.rows_ref, f32[3,256,256]{2,1,0:T(8,128)S(1)} %copy-done.1, bf16[1536,384]{1,0:T(8,128)(2,1)S(1)} %bitcast.20, bf16[1536,384]{1,0:T(8,128)(2,1)S(1)} %collective-permute-done.4.wc_ref, ...), custom_call_target="tpu_custom_call" | custom-call | flops 805306368 | bytes 6291456 | tf_op jit(solution)/shard_map/pallas_call | solution.py:197
  (22 shorter events, 2.2 us)
Async XLA Ops:
  0.6 47.1 %copy-start.7 = (bf16[24,384]{1,0:T(8,128)(2,1)S(1)}, bf16[24,384]{1,0:T(8,128)(2,1)}, u32[]{:S(2)}) copy-start(bf16[24,384]{1,0:T(8,128)(2,1)} %param.8) | copy-start | bytes 55300
  0.6 21.5 %collective-permute-start = (bf16[24,384]{1,0:T(8,128)(2,1)}, bf16[24,384]{1,0:T(8,128)(2,1)S(1)}, u32[]{:S(2)}, u32[]{:S(2)}) collective-permute-start(bf16[24,384]{1,0:T(8,128)(2,1)} %param.8), channel_id=1, source_target_pairs={{0,128},{1,129},{2,130},{3,131},{4,132},{5,133},{6,134},{7,135},{8... | collective-permute-start | bytes 55304 | tf_op jit(solution)/shard_map/ppermute | solution.py:26
  20.2 28.2 %collective-permute-start.2 = (bf16[32,3072]{1,0:T(8,128)(2,1)}, bf16[32,3072]{1,0:T(8,128)(2,1)S(1)}, u32[]{:S(2)}, u32[]{:S(2)}) collective-permute-start(bf16[32,3072]{1,0:T(8,128)(2,1)} %shard_map.76), channel_id=1, source_target_pairs={{0,128},{1,129},{2,130},{3,131},{4,132},{5,133},{6,134},{7,135},{8... | collective-permute-start | bytes 589832 | tf_op jit(solution)/shard_map/ppermute | solution.py:60
  22.8 24.9 %collective-permute-start.1 = (bf16[48,384]{1,0:T(8,128)(2,1)S(1)}, bf16[48,384]{1,0:T(8,128)(2,1)S(1)}, u32[]{:S(2)}, u32[]{:S(2)}) collective-permute-start(bf16[48,384]{1,0:T(8,128)(2,1)S(1)} %pad_maximum_fusion.1), channel_id=1, source_target_pairs={{0,64},{1,65},{2,66},{3,67},{4,68},{5,69},{6,70},{7,71},{8,72},{9,... | collective-permute-start | bytes 110600 | tf_op jit(solution)/shard_map/ppermute | solution.py:26
  49.1 30.1 %all-to-all-start = ((bf16[4,96,384]{2,1,0:T(8,128)(2,1)}), bf16[4,96,384]{2,1,0:T(8,128)(2,1)S(1)}, u32[]{:S(2)}, u32[]{:S(2)}) async-start(bf16[4,96,384]{2,1,0:T(8,128)(2,1)} %broadcast_in_dim.6), calls=%async_computation | async-start | bytes 589824 | tf_op jit(solution)/shard_map/all_to_all | solution.py:31
  55.7 31.6 %collective-permute-start.3 = (bf16[32,3072]{1,0:T(8,128)(2,1)S(1)}, bf16[32,3072]{1,0:T(8,128)(2,1)S(1)}, u32[]{:S(2)}, u32[]{:S(2)}) collective-permute-start(bf16[32,3072]{1,0:T(8,128)(2,1)S(1)} %collective-permute-done.2), channel_id=1, source_target_pairs={{0,128},{1,129},{2,130},{3,131},{4,132},{5,133},{6,134},{7,135},{8... | collective-permute-start | bytes 589832 | tf_op jit(solution)/shard_map/ppermute | solution.py:60
  80.4 7.0 %copy-start.2 = (bf16[1,256,384]{2,1,0:T(8,128)(2,1)S(1)}, bf16[1,256,384]{2,1,0:T(8,128)(2,1)}, u32[]{:S(2)}) copy-start(bf16[1,256,384]{2,1,0:T(8,128)(2,1)} %param.5) | copy-start | bytes 589828
  80.4 7.0 %copy-start.3 = (bf16[1,256,384]{2,1,0:T(8,128)(2,1)S(1)}, bf16[1,256,384]{2,1,0:T(8,128)(2,1)}, u32[]{:S(2)}) copy-start(bf16[1,256,384]{2,1,0:T(8,128)(2,1)} %param.6) | copy-start | bytes 589828
  80.4 20.7 %all-to-all-start.1 = ((bf16[4,384,384]{2,1,0:T(8,128)(2,1)}), bf16[4,384,384]{2,1,0:T(8,128)(2,1)S(1)}, u32[]{:S(2)}, u32[]{:S(2)}) async-start(bf16[4,384,384]{2,1,0:T(8,128)(2,1)} %broadcast_in_dim.15), calls=%async_computation.1 | async-start | bytes 2359296 | tf_op jit(solution)/shard_map/all_to_all | solution.py:31
  87.4 0.7 copy-start.5
  88.1 0.9 copy-start
  101.1 20.0 %collective-permute-start.4 = (bf16[1536,384]{1,0:T(8,128)(2,1)S(1)}, bf16[1536,384]{1,0:T(8,128)(2,1)S(1)}, u32[]{:S(2)}, u32[]{:S(2)}) collective-permute-start(bf16[1536,384]{1,0:T(8,128)(2,1)S(1)} %bitcast.19), channel_id=1, source_target_pairs={{0,8},{1,9},{2,10},{3,11},{4,12},{5,13},{6,14},{7,15},{8,0},{9,1},... | collective-permute-start | bytes 3538952 | tf_op jit(solution)/shard_map/ppermute | solution.py:26
  103.0 10.7 %collective-permute-start.7 = (bf16[32,3072]{1,0:T(8,128)(2,1)}, bf16[32,3072]{1,0:T(8,128)(2,1)}, u32[]{:S(2)}, u32[]{:S(2)}) collective-permute-start(bf16[32,3072]{1,0:T(8,128)(2,1)} %copy-done.5), channel_id=1, source_target_pairs={{0,6},{1,7},{2,4},{3,5},{4,2},{5,3},{6,0},{7,1},{8,14},{9,15},{10,... | collective-permute-start | bytes 589832 | tf_op jit(solution)/shard_map/ppermute | solution.py:26
  105.6 9.9 %collective-permute-start.6 = (bf16[32,3072]{1,0:T(8,128)(2,1)}, bf16[32,3072]{1,0:T(8,128)(2,1)}, u32[]{:S(2)}, u32[]{:S(2)}) collective-permute-start(bf16[32,3072]{1,0:T(8,128)(2,1)} %copy-done.5), channel_id=1, source_target_pairs={{0,2},{1,3},{2,0},{3,1},{4,6},{5,7},{6,4},{7,5},{8,10},{9,11},{10,... | collective-permute-start | bytes 589832 | tf_op jit(solution)/shard_map/ppermute | solution.py:26
  107.7 13.3 %collective-permute-start.5 = (bf16[32,3072]{1,0:T(8,128)(2,1)}, bf16[32,3072]{1,0:T(8,128)(2,1)}, u32[]{:S(2)}, u32[]{:S(2)}) collective-permute-start(bf16[32,3072]{1,0:T(8,128)(2,1)} %copy-done.5), channel_id=1, source_target_pairs={{0,4},{1,5},{2,6},{3,7},{4,0},{5,1},{6,2},{7,3},{8,12},{9,13},{10,... | collective-permute-start | bytes 589832 | tf_op jit(solution)/shard_map/ppermute | solution.py:26
  121.0 1.1 copy-start.1
  122.2 0.9 copy-start.4
  123.1 0.9 copy-start.6

commit v8 on v3

--- a/solution.py
+++ b/solution.py
@@ -11,7 +11,6 @@
 HD = 128
 AXES = ("dp", "mp")
 NY, NZ, NC, NX, NH = 4, 16, 2, 4, 2
-Y_ORDER = (0, 2, 1, 3)
 
 
 def exchange(y=0, z=0, core=0, x=0, half=0):
@@ -30,6 +29,16 @@
 def gather_x(value):
     groups = [[i * NH + h for i in range(NX)] for h in range(NH)]
     return lax.all_gather(value, "mp", axis_index_groups=groups, axis=0, tiled=True)
+
+
+def share_quads(value):
+    groups = [
+        [(y * NZ + quad * 4 + i) * NC + core for y in range(NY) for i in range(4)]
+        for quad in range(NZ // 4) for core in range(NC)
+    ]
+    copies = jnp.broadcast_to(value[None], (NY * 4,) + value.shape)
+    shared = lax.all_to_all(copies, "dp", 0, 0, axis_index_groups=groups)
+    return shared.reshape(-1, value.shape[1])
 
 
 def after(*values):
@@ -60,13 +69,13 @@
     return lax.dot_general(a, b, (((1,), (0,)), ((), ())), preferred_element_type=jnp.float32)
 
 
-def reorder_kernel(y_ref, source_ref, in_ref, out_ref):
+def reorder_kernel(source_ref, in_ref, out_ref):
     span = source_ref.shape[1]
     wanted = lax.broadcasted_iota(jnp.int32, (span, span), 0) == source_ref[...]
     pick = jnp.where(wanted, 1.0, 0.0).astype(jnp.bfloat16)
-    for slot, i in enumerate(Y_ORDER):
-        start = pl.multiple_of((y_ref[0] ^ i) * span, span)
-        out_ref[:, slot * span:(slot + 1) * span] = nn(in_ref[:, pl.ds(start, span)], pick).astype(jnp.bfloat16)
+    for i in range(NY):
+        cols = slice(i * span, (i + 1) * span)
+        out_ref[:, cols] = nn(in_ref[:, cols], pick).astype(jnp.bfloat16)
 
 
 def attention_kernel(q_ref, k_ref, out_ref):
@@ -78,17 +87,25 @@
         out_ref[head] = raised / jnp.sum(raised, axis=-1, keepdims=True)
 
 
-def tail_kernel(rows_ref, attn_ref, q_ref, k_ref, v_ref, own_ref, far_ref, w_ref, wc_ref, *refs):
-    gq_ref, gk_ref, gv_ref, grad_ref = refs
+def tail_kernel(rows_ref, attn_ref, w_ref, wc_ref, own_ref, far_ref, q_any, k_any, v_any, *refs):
+    gq_ref, gk_ref, gv_ref, grad_ref, q_ref, k_ref, v_ref, sems = refs
     scale = 1.0 / math.sqrt(HD)
-    n_g, depth = NX * NH, w_ref.shape[0] // NY
-    part = q_ref.shape[0] // n_g
-    parts = [ref[i * depth:(i + 1) * depth] for i in range(NY) for ref in (w_ref, wc_ref)]
-    left = jnp.concatenate([own_ref[...], far_ref[...]], axis=0)
+    n_g = NX * NH
+    part, depth = q_ref.shape[0] // n_g, w_ref.shape[0] // NY
+    copies = [
+        pltpu.make_async_copy(src, dst, sems.at[i])
+        for i, (src, dst) in enumerate(((v_any, v_ref), (k_any, k_ref), (q_any, q_ref)))
+    ]
+    for copy in copies:
+        copy.start()
+    weights = [ref[i * depth:(i + 1) * depth] for i in range(NY) for ref in (w_ref, wc_ref)]
     total = None
-    for i, piece in enumerate(parts):
-        term = nn(left[:, i * depth:(i + 1) * depth], piece)
+    for i in range(NY * NC):
+        band = pl.ds(i * depth, depth)
+        term = nn(jnp.concatenate([own_ref[:, band], far_ref[:, band]], axis=0), weights[i])
         total = term if total is None else total + term
+    for copy in copies:
+        copy.wait()
     total = total.astype(jnp.bfloat16)
     for slot in range(n_g):
         row = pl.multiple_of(rows_ref[slot] * part, part)
@@ -106,6 +123,8 @@
 
 
 VMEM = pl.BlockSpec(memory_space=pltpu.VMEM)
+ANY = pl.BlockSpec(memory_space=pl.ANY)
+TAIL_VMEM = 52 * 1024 * 1024
 SMEM = pl.BlockSpec(memory_space=pltpu.SMEM)
 PARAMS = pltpu.CompilerParams(vmem_limit_bytes=16 * 1024 * 1024)
 
@@ -115,25 +134,32 @@
     heads = width // HD
     q, k, v = (a.reshape(patches, width) for a in (queries, attn_keys, attn_values))
     part, model = grad_out.shape[1], grad_out.shape[2]
+    dp, mp = lax.axis_index("dp"), lax.axis_index("mp")
+    core, z = dp % NC, (dp // NC) % NZ
+
     block = out_weight.shape[0]
-    dp, mp = lax.axis_index("dp"), lax.axis_index("mp")
-    core, z, y = dp % NC, (dp // NC) % NZ, dp // (NC * NZ)
-
     span = NZ * NC * block
     place = np.arange(span)
-    z_bits = (place // block) % NZ
-    z_xor = sum(((z_bits >> b) & 1) << (3 - b) for b in range(4))
-    core_xor = place // (NZ * block)
-    source = ((jnp.asarray(z_xor) ^ z) * NC + (jnp.asarray(core_xor) ^ core)) * block + jnp.asarray(place % block)
+    slot = (place // block) % NZ
+    quad = jnp.asarray((slot & 1) << 3 | (slot & 2) << 1)
+    source = (((quad ^ (z & 12)) | jnp.asarray(slot >> 2)) * NC + (jnp.asarray(place // (NZ * block)) ^ core)) * block
+    source = source + jnp.asarray(place % block)
     own = pl.pallas_call(
         reorder_kernel,
         out_shape=jax.ShapeDtypeStruct((part, model), jnp.bfloat16),
-        in_specs=[SMEM, VMEM, VMEM],
+        in_specs=[VMEM, VMEM],
         out_specs=VMEM,
         compiler_params=PARAMS,
         cost_estimate=pl.CostEstimate(flops=2 * part * model * span, bytes_accessed=4 * part * model, transcendentals=0),
-    )(y.reshape(1), source.astype(jnp.int32).reshape(1, span), grad_out.reshape(part, model))
-
+    )(source.astype(jnp.int32).reshape(1, span), grad_out.reshape(part, model))
+
+    weight = out_weight
+    arrived = swap(weight, z=8)
+    half_way = quarter_turn(own)
+    own, arrived = after(own, arrived)
+    weight = jnp.concatenate([weight, arrived], 0)
+    weight = jnp.concatenate([weight, swap(weight, z=4)], 0)
+    own = gather_x(own)
     attn = pl.pallas_call(
         attention_kernel,
         out_shape=jax.ShapeDtypeStruct((heads, patches, patches), jnp.float32),
@@ -142,18 +168,9 @@
         compiler_params=PARAMS,
         cost_estimate=pl.CostEstimate(flops=2 * patches * patches * width, bytes_accessed=1 << 20, transcendentals=0),
     )(q, k)
-    weight = out_weight
-    arrived = swap(weight, z=8)
-    half_way = quarter_turn(own)
-    own, arrived = after(own, arrived)
-    weight = jnp.concatenate([weight, arrived], 0)
-    weight = jnp.concatenate([weight, swap(weight, z=4)], 0)
-    own = gather_x(own)
     weight, half_way, own = after(weight, half_way, own)
     far = quarter_turn(half_way)
-    weight = jnp.concatenate([weight, swap(weight, z=2)], 0)
-    weight = jnp.concatenate([weight, swap(weight, z=1)], 0)
-    weight = jnp.concatenate([weight] + [swap(weight, y=i) for i in Y_ORDER[1:]], 0)
+    weight = share_quads(weight)
     far = gather_x(far)
     weight, far, attn = after(weight, far, attn)
     weights = [weight, swap(weight, core=1)]
@@ -164,12 +181,16 @@
     outs = pl.pallas_call(
         tail_kernel,
         out_shape=(grad_shape,) * 3,
-        in_specs=[SMEM] + [VMEM] * (6 + len(weights)),
+        in_specs=[SMEM] + [VMEM] * 5 + [ANY] * 3,
         out_specs=(VMEM,) * 3,
-        scratch_shapes=[pltpu.VMEM((patches, width), jnp.bfloat16)],
-        compiler_params=PARAMS,
+        scratch_shapes=[
+            pltpu.VMEM((patches, width), jnp.bfloat16),
+            *[pltpu.VMEM((patches, width), jnp.bfloat16)] * 3,
+            pltpu.SemaphoreType.DMA((3,)),
+        ],
+        compiler_params=pltpu.CompilerParams(vmem_limit_bytes=TAIL_VMEM),
         cost_estimate=pl.CostEstimate(flops=2 * patches * width * (model + 4 * patches), bytes_accessed=6 << 20, transcendentals=0),
-    )(rows, attn, q, k, v, own, far, *weights)
+    )(rows, attn, *weights, own, far, q, k, v)
     return tuple(o.reshape(1, patches, width) for o in outs)
 
 

time: 120 us -> 135 us (1.12)
  the two profiles are of different devices: /device:TPU:65 before, /device:TPU:41 now
where the time goes in v8:
time: 135 us; the launch traced here: 134 us
  starting transfers between devices  76.1 us (56%)
  blocking collectives  23.8 us (18%)
  waiting for transfers between devices  22.7 us (17%)
  Pallas kernels  7.3 us (5%)
  local copies, waits for them, and re-layouts  2.16 us (2%)
  other arithmetic  1.49 us (1%)
    ppermute x3, starting transfers between devices, swap(): return lax.ppermute(value, AXES, exchange(**moves))  43.2 us
    ppermute x2, starting transfers between devices, quarter_turn(): return lax.ppermute(value, AXES, pairs)  25.4 us
    all_gather x2, blocking collectives, gather_x(): lax.all_gather(value, 'mp', axis_index_groups=groups, axis=0, tiled=True)  23.8 us
    ppermute x2, waiting for transfers between devices, quarter_turn(): return lax.ppermute(value, AXES, pairs)  20.2 us
    all_to_all x1, starting transfers between devices, share_quads(): shared = lax.all_to_all(copies, 'dp', 0, 0, axis_index_groups=groups)  7.53 us
    pallas_call x1, Pallas kernels, shards(): pl.pallas_call(tail_kernel, out_shape=(grad_shape,) * 3, in_specs=[SMEM]...  5.9 us
  transfers between devices with their start and end apart: 6, of which 2 were waited for; matrix products, arithmetic and copies ran while one was open for 1% of the time, Pallas kernels for 1%

profile of v8, /device:TPU:41, one launch (start us, length us, event | category | flops | bytes accessed | tf_op | source)
XLA Modules:
  0.0 134.3 jit_solution(16175458704866935238)
XLA Ops:
  0.6 0.0 copy-start.5
  0.6 15.4 %collective-permute-start = (bf16[24,384]{1,0:T(8,128)(2,1)}, bf16[24,384]{1,0:T(8,128)(2,1)S(1)}, u32[]{:S(2)}, u32[]{:S(2)}) collective-permute-start(bf16[24,384]{1,0:T(8,128)(2,1)} %param.12), channel_id=1, source_target_pairs={{0,128},{1,129},{2,130},{3,131},{4,132},{5,133},{6,134},{7,135},{8... | collective-permute-start | bytes 55304 | tf_op jit(solution)/shard_map/ppermute | solution.py:26
  16.1 0.8 multiply_add_fusion
  16.9 0.0 copy-start.3
  16.9 0.9 copy-done.3
  17.8 0.9 shard_map.112
  18.8 14.6 %collective-permute-start.2 = (bf16[32,3072]{1,0:T(8,128)(2,1)S(1)}, bf16[32,3072]{1,0:T(8,128)(2,1)S(1)}, u32[]{:S(2)}, u32[]{:S(2)}) collective-permute-start(bf16[32,3072]{1,0:T(8,128)(2,1)S(1)} %shard_map.112), channel_id=1, source_target_pairs={{0,128},{1,129},{2,130},{3,131},{4,132},{5,133},{6,134},{7,135},{8... | collective-permute-start | bytes 589832 | tf_op jit(solution)/shard_map/ppermute | solution.py:57
  33.3 0.0 collective-permute-done
  33.3 0.7 pad_maximum_fusion.1
  34.1 4.0 %collective-permute-start.1 = (bf16[48,384]{1,0:T(8,128)(2,1)S(1)}, bf16[48,384]{1,0:T(8,128)(2,1)S(1)}, u32[]{:S(2)}, u32[]{:S(2)}) collective-permute-start(bf16[48,384]{1,0:T(8,128)(2,1)S(1)} %pad_maximum_fusion.1), channel_id=1, source_target_pairs={{0,64},{1,65},{2,66},{3,67},{4,68},{5,69},{6,70},{7,71},{8,72},{9,... | collective-permute-start | bytes 110600 | tf_op jit(solution)/shard_map/ppermute | solution.py:26
  38.1 12.0 %all_gather.6.own_ref = bf16[128,3072]{1,0:T(8,128)(2,1)} all-gather(bf16[32,3072]{1,0:T(8,128)(2,1)S(1)} %shard_map.112), channel_id=1, replica_groups={{0,2,4,6},{1,3,5,7},{8,10,12,14},{9,11,13,15},{16,18,20,22},{17,19,21,2..., dimensions={0}, use_global_device_ids=true | all-gather | bytes 983040 | tf_op jit(solution)/shard_map/all_gather | solution.py:31
  50.1 0.0 collective-permute-done.1
  50.1 0.0 collective-permute-done.2
  50.1 1.1 broadcast_in_dim.2
  51.3 7.5 %all-to-all-start = ((bf16[16,96,384]{2,1,0:T(8,128)(2,1)}), bf16[16,96,384]{2,1,0:T(8,128)(2,1)S(1)}, u32[]{:S(2)}, u32[]{:S(2)}) async-start(bf16[16,96,384]{2,1,0:T(8,128)(2,1)} %broadcast_in_dim.2), calls=%async_computation | async-start | bytes 2359296 | tf_op jit(solution)/shard_map/all_to_all | solution.py:40
  58.8 10.8 %collective-permute-start.3 = (bf16[32,3072]{1,0:T(8,128)(2,1)S(1)}, bf16[32,3072]{1,0:T(8,128)(2,1)S(1)}, u32[]{:S(2)}, u32[]{:S(2)}) collective-permute-start(bf16[32,3072]{1,0:T(8,128)(2,1)S(1)} %collective-permute-done.2), channel_id=1, source_target_pairs={{0,128},{1,129},{2,130},{3,131},{4,132},{5,133},{6,134},{7,135},{8... | collective-permute-start | bytes 589832 | tf_op jit(solution)/shard_map/ppermute | solution.py:57
  69.7 0.5 shard_map.113.attn_ref
  70.1 20.2 %collective-permute-done.3 = bf16[32,3072]{1,0:T(8,128)(2,1)S(1)} collective-permute-done((bf16[32,3072]{1,0:T(8,128)(2,1)S(1)}, bf16[32,3072]{1,0:T(8,128)(2,1)S(1)}, u32[]{:S(2)}, u32[]{:S(2)}) %collective-permute-start.3) | collective-permute-done | bytes 196640 | tf_op jit(solution)/shard_map/ppermute | solution.py:57
  90.3 11.8 %all_gather.7.far_ref = bf16[128,3072]{1,0:T(8,128)(2,1)} all-gather(bf16[32,3072]{1,0:T(8,128)(2,1)S(1)} %collective-permute-done.3), channel_id=1, replica_groups={{0,2,4,6},{1,3,5,7},{8,10,12,14},{9,11,13,15},{16,18,20,22},{17,19,21,2..., dimensions={0}, use_global_device_ids=true | all-gather | bytes 983040 | tf_op jit(solution)/shard_map/all_gather | solution.py:31
  102.1 0.0 all-to-all-done
  102.1 23.7 %collective-permute-start.4 = (bf16[1536,384]{1,0:T(8,128)(2,1)S(1)}, bf16[1536,384]{1,0:T(8,128)(2,1)}, u32[]{:S(2)}, u32[]{:S(2)}) collective-permute-start(bf16[1536,384]{1,0:T(8,128)(2,1)S(1)} %bitcast.22), channel_id=1, source_target_pairs={{0,8},{1,9},{2,10},{3,11},{4,12},{5,13},{6,14},{7,15},{8,0},{9,1},... | collective-permute-start | bytes 3538952 | tf_op jit(solution)/shard_map/ppermute | solution.py:26
  125.8 0.1 stack.35.rows_ref
  125.9 2.5 %collective-permute-done.4.wc_ref = bf16[1536,384]{1,0:T(8,128)(2,1)} collective-permute-done((bf16[1536,384]{1,0:T(8,128)(2,1)S(1)}, bf16[1536,384]{1,0:T(8,128)(2,1)}, u32[]{:S(2)}, u32[]{:S(2)}) %collective-permute-start.4) | collective-permute-done | bytes 1179680 | tf_op jit(solution)/shard_map/ppermute | solution.py:26
  128.4 5.9 %shard_map.114 = (bf16[256,384]{1,0:T(8,128)(2,1)}, bf16[256,384]{1,0:T(8,128)(2,1)}, bf16[256,384]{1,0:T(8,128)(2,1)}) custom-call(s32[8]{0:T(128)S(1)} %stack.35.rows_ref, f32[3,256,256]{2,1,0:T(8,128)S(1)} %shard_map.113.attn_ref, bf16[1536,384]{1,0:T(8,128)(2,1)} %bitcast.23, bf16[1536,384]{1,0:T(8,128)(2,1)} %collective-permute-done.4.wc_ref, ...), custom_call_target="tpu_custom_call" | custom-call | flops 805306368 | bytes 6291456 | tf_op jit(solution)/shard_map/pallas_call | solution.py:181
  (11 shorter events, 0.0 us)
Async XLA Ops:
  0.6 49.5 %copy-start.5 = (bf16[24,384]{1,0:T(8,128)(2,1)S(1)}, bf16[24,384]{1,0:T(8,128)(2,1)}, u32[]{:S(2)}) copy-start(bf16[24,384]{1,0:T(8,128)(2,1)} %param.12) | copy-start | bytes 55300
  0.6 32.7 %collective-permute-start = (bf16[24,384]{1,0:T(8,128)(2,1)}, bf16[24,384]{1,0:T(8,128)(2,1)S(1)}, u32[]{:S(2)}, u32[]{:S(2)}) collective-permute-start(bf16[24,384]{1,0:T(8,128)(2,1)} %param.12), channel_id=1, source_target_pairs={{0,128},{1,129},{2,130},{3,131},{4,132},{5,133},{6,134},{7,135},{8... | collective-permute-start | bytes 55304 | tf_op jit(solution)/shard_map/ppermute | solution.py:26
  16.9 0.9 copy-start.3
  18.8 31.4 %collective-permute-start.2 = (bf16[32,3072]{1,0:T(8,128)(2,1)S(1)}, bf16[32,3072]{1,0:T(8,128)(2,1)S(1)}, u32[]{:S(2)}, u32[]{:S(2)}) collective-permute-start(bf16[32,3072]{1,0:T(8,128)(2,1)S(1)} %shard_map.112), channel_id=1, source_target_pairs={{0,128},{1,129},{2,130},{3,131},{4,132},{5,133},{6,134},{7,135},{8... | collective-permute-start | bytes 589832 | tf_op jit(solution)/shard_map/ppermute | solution.py:57
  34.1 16.0 %collective-permute-start.1 = (bf16[48,384]{1,0:T(8,128)(2,1)S(1)}, bf16[48,384]{1,0:T(8,128)(2,1)S(1)}, u32[]{:S(2)}, u32[]{:S(2)}) collective-permute-start(bf16[48,384]{1,0:T(8,128)(2,1)S(1)} %pad_maximum_fusion.1), channel_id=1, source_target_pairs={{0,64},{1,65},{2,66},{3,67},{4,68},{5,69},{6,70},{7,71},{8,72},{9,... | collective-permute-start | bytes 110600 | tf_op jit(solution)/shard_map/ppermute | solution.py:26
  51.3 18.4 %copy-start = (bf16[1,256,384]{2,1,0:T(8,128)(2,1)S(1)}, bf16[1,256,384]{2,1,0:T(8,128)(2,1)}, u32[]{:S(2)}) copy-start(bf16[1,256,384]{2,1,0:T(8,128)(2,1)} %param.9) | copy-start | bytes 589828
  51.3 18.4 %copy-start.1 = (bf16[1,256,384]{2,1,0:T(8,128)(2,1)S(1)}, bf16[1,256,384]{2,1,0:T(8,128)(2,1)}, u32[]{:S(2)}) copy-start(bf16[1,256,384]{2,1,0:T(8,128)(2,1)} %param.10) | copy-start | bytes 589828
  51.3 50.8 %all-to-all-start = ((bf16[16,96,384]{2,1,0:T(8,128)(2,1)}), bf16[16,96,384]{2,1,0:T(8,128)(2,1)S(1)}, u32[]{:S(2)}, u32[]{:S(2)}) async-start(bf16[16,96,384]{2,1,0:T(8,128)(2,1)} %broadcast_in_dim.2), calls=%async_computation | async-start | bytes 2359296 | tf_op jit(solution)/shard_map/all_to_all | solution.py:40
  58.8 69.6 %copy-start.2 = (bf16[1,256,384]{2,1,0:T(8,128)(2,1)S(1)}, bf16[1,256,384]{2,1,0:T(8,128)(2,1)}, u32[]{:S(2)}) copy-start(bf16[1,256,384]{2,1,0:T(8,128)(2,1)} %param.11) | copy-start | bytes 589828
  58.8 31.5 %collective-permute-start.3 = (bf16[32,3072]{1,0:T(8,128)(2,1)S(1)}, bf16[32,3072]{1,0:T(8,128)(2,1)S(1)}, u32[]{:S(2)}, u32[]{:S(2)}) collective-permute-start(bf16[32,3072]{1,0:T(8,128)(2,1)S(1)} %collective-permute-done.2), channel_id=1, source_target_pairs={{0,128},{1,129},{2,130},{3,131},{4,132},{5,133},{6,134},{7,135},{8... | collective-permute-start | bytes 589832 | tf_op jit(solution)/shard_map/ppermute | solution.py:57
  102.1 26.3 %copy-start.4 = (bf16[16,96,384]{2,1,0:T(8,128)(2,1)}, bf16[16,96,384]{2,1,0:T(8,128)(2,1)S(1)}, u32[]{:S(2)}) copy-start(bf16[16,96,384]{2,1,0:T(8,128)(2,1)S(1)} %all-to-all-done) | copy-start | bytes 3538948
  102.1 26.3 %collective-permute-start.4 = (bf16[1536,384]{1,0:T(8,128)(2,1)S(1)}, bf16[1536,384]{1,0:T(8,128)(2,1)}, u32[]{:S(2)}, u32[]{:S(2)}) collective-permute-start(bf16[1536,384]{1,0:T(8,128)(2,1)S(1)} %bitcast.22), channel_id=1, source_target_pairs={{0,8},{1,9},{2,10},{3,11},{4,12},{5,13},{6,14},{7,15},{8,0},{9,1},... | collective-permute-start | bytes 3538952 | tf_op jit(solution)/shard_map/ppermute | solution.py:26

commit v9 on v3

--- a/solution.py
+++ b/solution.py
@@ -30,6 +30,16 @@
 def gather_x(value):
     groups = [[i * NH + h for i in range(NX)] for h in range(NH)]
     return lax.all_gather(value, "mp", axis_index_groups=groups, axis=0, tiled=True)
+
+
+def share_quad(value):
+    groups = [
+        [((y * NZ) + quad * 4 + i) * NC + core for i in range(4)]
+        for y in range(NY) for quad in range(NZ // 4) for core in range(NC)
+    ]
+    copies = jnp.broadcast_to(value[None], (4,) + value.shape)
+    shared = lax.all_to_all(copies, "dp", 0, 0, axis_index_groups=groups)
+    return shared.reshape(4 * value.shape[0], value.shape[1])
 
 
 def after(*values):
@@ -78,17 +88,35 @@
         out_ref[head] = raised / jnp.sum(raised, axis=-1, keepdims=True)
 
 
-def tail_kernel(rows_ref, attn_ref, q_ref, k_ref, v_ref, own_ref, far_ref, w_ref, wc_ref, *refs):
-    gq_ref, gk_ref, gv_ref, grad_ref = refs
+def first_half_kernel(w_ref, own_any, far_any, q_any, k_any, v_any, sum_ref, rest_ref, q_ref, k_ref, v_ref, g_ref, band_sems, sems):
+    rows, depth = own_any.shape[0], w_ref.shape[0] // NY
+    first, later = [], []
+    for i in range(NY):
+        mine, other, place = pl.ds(NC * i * depth, depth), pl.ds((NC * i + 1) * depth, depth), pl.ds(i * depth, depth)
+        for j, src in enumerate((own_any, far_any)):
+            half = pl.ds(j * rows, rows)
+            first.append(pltpu.make_async_copy(src.at[:, mine], g_ref.at[half, place], band_sems.at[0, i, j]))
+            later.append(pltpu.make_async_copy(src.at[:, other], rest_ref.at[half, place], band_sems.at[1, i, j]))
+    for i, (src, dst) in enumerate(((v_any, v_ref), (k_any, k_ref), (q_any, q_ref))):
+        later.append(pltpu.make_async_copy(src, dst, sems.at[i]))
+    for copy in first + later:
+        copy.start()
+    total = None
+    for i in range(NY):
+        for copy in first[2 * i:2 * i + 2]:
+            copy.wait()
+        term = nn(g_ref[:, i * depth:(i + 1) * depth], w_ref[i * depth:(i + 1) * depth])
+        total = term if total is None else total + term
+    sum_ref[...] = total
+    for copy in later:
+        copy.wait()
+
+
+def tail_kernel(rows_ref, attn_ref, wc_ref, sum_ref, rest_ref, q_ref, k_ref, v_ref, gq_ref, gk_ref, gv_ref, grad_ref):
     scale = 1.0 / math.sqrt(HD)
-    n_g, depth = NX * NH, w_ref.shape[0] // NY
+    n_g = NX * NH
     part = q_ref.shape[0] // n_g
-    parts = [ref[i * depth:(i + 1) * depth] for i in range(NY) for ref in (w_ref, wc_ref)]
-    left = jnp.concatenate([own_ref[...], far_ref[...]], axis=0)
-    total = None
-    for i, piece in enumerate(parts):
-        term = nn(left[:, i * depth:(i + 1) * depth], piece)
-        total = term if total is None else total + term
+    total = sum_ref[...] + nn(rest_ref[...], wc_ref[...])
     total = total.astype(jnp.bfloat16)
     for slot in range(n_g):
         row = pl.multiple_of(rows_ref[slot] * part, part)
@@ -106,6 +134,8 @@
 
 
 VMEM = pl.BlockSpec(memory_space=pltpu.VMEM)
+ANY = pl.BlockSpec(memory_space=pl.ANY)
+FIRST_VMEM = 51 * 1024 * 1024
 SMEM = pl.BlockSpec(memory_space=pltpu.SMEM)
 PARAMS = pltpu.CompilerParams(vmem_limit_bytes=16 * 1024 * 1024)
 
@@ -115,16 +145,16 @@
     heads = width // HD
     q, k, v = (a.reshape(patches, width) for a in (queries, attn_keys, attn_values))
     part, model = grad_out.shape[1], grad_out.shape[2]
-    block = out_weight.shape[0]
     dp, mp = lax.axis_index("dp"), lax.axis_index("mp")
     core, z, y = dp % NC, (dp // NC) % NZ, dp // (NC * NZ)
 
+    block = out_weight.shape[0]
     span = NZ * NC * block
     place = np.arange(span)
-    z_bits = (place // block) % NZ
-    z_xor = sum(((z_bits >> b) & 1) << (3 - b) for b in range(4))
-    core_xor = place // (NZ * block)
-    source = ((jnp.asarray(z_xor) ^ z) * NC + (jnp.asarray(core_xor) ^ core)) * block + jnp.asarray(place % block)
+    slot = (place // block) % NZ
+    quad = jnp.asarray((slot & 1) << 3 | (slot & 2) << 1)
+    source = (((quad ^ (z & 12)) | jnp.asarray(slot >> 2)) * NC + (jnp.asarray(place // (NZ * block)) ^ core)) * block
+    source = source + jnp.asarray(place % block)
     own = pl.pallas_call(
         reorder_kernel,
         out_shape=jax.ShapeDtypeStruct((part, model), jnp.bfloat16),
@@ -151,25 +181,42 @@
     own = gather_x(own)
     weight, half_way, own = after(weight, half_way, own)
     far = quarter_turn(half_way)
-    weight = jnp.concatenate([weight, swap(weight, z=2)], 0)
-    weight = jnp.concatenate([weight, swap(weight, z=1)], 0)
+    weight = share_quad(weight)
     weight = jnp.concatenate([weight] + [swap(weight, y=i) for i in Y_ORDER[1:]], 0)
     far = gather_x(far)
     weight, far, attn = after(weight, far, attn)
-    weights = [weight, swap(weight, core=1)]
+    across = swap(weight, core=1)
     half = mp % NH
     rows = jnp.stack([i * NH + h for h in (half, 1 - half) for i in range(NX)]).astype(jnp.int32)
 
     grad_shape = jax.ShapeDtypeStruct((patches, width), jnp.bfloat16)
+    half_width = model // NC
+    partial, rest, q_in, k_in, v_in = pl.pallas_call(
+        first_half_kernel,
+        out_shape=(
+            jax.ShapeDtypeStruct((patches, width), jnp.float32),
+            jax.ShapeDtypeStruct((patches, half_width), jnp.bfloat16),
+            *(grad_shape,) * 3,
+        ),
+        in_specs=[VMEM] + [ANY] * 5,
+        out_specs=(VMEM,) * 5,
+        scratch_shapes=[
+            pltpu.VMEM((patches, half_width), jnp.bfloat16),
+            pltpu.SemaphoreType.DMA((NC, NY, 2)),
+            pltpu.SemaphoreType.DMA((3,)),
+        ],
+        compiler_params=pltpu.CompilerParams(vmem_limit_bytes=FIRST_VMEM),
+        cost_estimate=pl.CostEstimate(flops=2 * patches * width * half_width, bytes_accessed=3 << 20, transcendentals=0),
+    )(weight, own, far, q, k, v)
     outs = pl.pallas_call(
         tail_kernel,
         out_shape=(grad_shape,) * 3,
-        in_specs=[SMEM] + [VMEM] * (6 + len(weights)),
+        in_specs=[SMEM] + [VMEM] * 7,
         out_specs=(VMEM,) * 3,
         scratch_shapes=[pltpu.VMEM((patches, width), jnp.bfloat16)],
         compiler_params=PARAMS,
-        cost_estimate=pl.CostEstimate(flops=2 * patches * width * (model + 4 * patches), bytes_accessed=6 << 20, transcendentals=0),
-    )(rows, attn, q, k, v, own, far, *weights)
+        cost_estimate=pl.CostEstimate(flops=2 * patches * width * (half_width + 4 * patches), bytes_accessed=6 << 20, transcendentals=0),
+    )(rows, attn, across, partial, rest, q_in, k_in, v_in)
     return tuple(o.reshape(1, patches, width) for o in outs)
 
 

time: 120 us -> 116 us (0.967)
  the two profiles are of different devices: /device:TPU:65 before, /device:TPU:129 now
where the time goes in v9:
time: 116 us
  starting transfers between devices  58.4 us (50%)
  blocking collectives  24.8 us (21%)
  waiting for transfers between devices  19.5 us (17%)
  Pallas kernels  7.9 us (7%)
  other arithmetic  2.64 us (2%)
  local copies, waits for them, and re-layouts  1.78 us (2%)
    ppermute x6, starting transfers between devices, swap(): return lax.ppermute(value, AXES, exchange(**moves))  39 us
    all_gather x2, blocking collectives, gather_x(): lax.all_gather(value, 'mp', axis_index_groups=groups, axis=0, tiled=True)  24.8 us
    all_to_all x1, waiting for transfers between devices, share_quad(): shared = lax.all_to_all(copies, 'dp', 0, 0, axis_index_groups=groups)  16.6 us
    ppermute x2, starting transfers between devices, quarter_turn(): return lax.ppermute(value, AXES, pairs)  16 us
    all_to_all x1, starting transfers between devices, share_quad(): shared = lax.all_to_all(copies, 'dp', 0, 0, axis_index_groups=groups)  3.45 us
    pallas_call x1, Pallas kernels, shards(): pl.pallas_call(first_half_kernel, out_shape=(jax.ShapeDtypeStruct((patche...  3.4 us
    pallas_call x1, Pallas kernels, shards(): pl.pallas_call(tail_kernel, out_shape=(grad_shape,) * 3, in_specs=[SMEM]...  3.09 us
  transfers between devices with their start and end apart: 9, of which 3 were waited for; matrix products, arithmetic and copies ran while one was open for 1% of the time, Pallas kernels for 4%

profile of v9, /device:TPU:129, one launch (start us, length us, event | category | flops | bytes accessed | tf_op | source)
XLA Modules:
  0.0 115.8 jit_solution(6353380371636596486)
XLA Ops:
  0.6 15.4 %collective-permute-start = (bf16[24,384]{1,0:T(8,128)(2,1)}, bf16[24,384]{1,0:T(8,128)(2,1)S(1)}, u32[]{:S(2)}, u32[]{:S(2)}) collective-permute-start(bf16[24,384]{1,0:T(8,128)(2,1)} %param.12), channel_id=1, source_target_pairs={{0,128},{1,129},{2,130},{3,131},{4,132},{5,133},{6,134},{7,135},{8... | collective-permute-start | bytes 55304 | tf_op jit(solution)/shard_map/ppermute | solution.py:27
  16.1 0.8 multiply_add_fusion
  16.9 0.9 copy-done.3
  17.8 0.9 shard_map.112
  18.8 10.8 %collective-permute-start.2 = (bf16[32,3072]{1,0:T(8,128)(2,1)S(1)}, bf16[32,3072]{1,0:T(8,128)(2,1)S(1)}, u32[]{:S(2)}, u32[]{:S(2)}) collective-permute-start(bf16[32,3072]{1,0:T(8,128)(2,1)S(1)} %shard_map.112), channel_id=1, source_target_pairs={{0,128},{1,129},{2,130},{3,131},{4,132},{5,133},{6,134},{7,135},{8... | collective-permute-start | bytes 589832 | tf_op jit(solution)/shard_map/ppermute | solution.py:58
  29.6 0.7 pad_maximum_fusion.2
  30.3 5.2 %collective-permute-start.1 = (bf16[48,384]{1,0:T(8,128)(2,1)S(1)}, bf16[48,384]{1,0:T(8,128)(2,1)S(1)}, u32[]{:S(2)}, u32[]{:S(2)}) collective-permute-start(bf16[48,384]{1,0:T(8,128)(2,1)S(1)} %pad_maximum_fusion.2), channel_id=1, source_target_pairs={{0,64},{1,65},{2,66},{3,67},{4,68},{5,69},{6,70},{7,71},{8,72},{9,... | collective-permute-start | bytes 110600 | tf_op jit(solution)/shard_map/ppermute | solution.py:27
  35.5 13.2 %all_gather.6.own_any = bf16[128,3072]{1,0:T(8,128)(2,1)} all-gather(bf16[32,3072]{1,0:T(8,128)(2,1)S(1)} %shard_map.112), channel_id=1, replica_groups={{0,2,4,6},{1,3,5,7},{8,10,12,14},{9,11,13,15},{16,18,20,22},{17,19,21,2..., dimensions={0}, use_global_device_ids=true | all-gather | bytes 983040 | tf_op jit(solution)/shard_map/all_gather | solution.py:32
  48.7 0.9 collective-permute-done.1
  49.6 2.0 %collective-permute-done.2 = bf16[32,3072]{1,0:T(8,128)(2,1)S(1)} collective-permute-done((bf16[32,3072]{1,0:T(8,128)(2,1)S(1)}, bf16[32,3072]{1,0:T(8,128)(2,1)S(1)}, u32[]{:S(2)}, u32[]{:S(2)}) %collective-permute-start.2) | collective-permute-done | bytes 196640 | tf_op jit(solution)/shard_map/ppermute | solution.py:58
  51.6 0.7 broadcast_in_dim.2
  52.3 3.5 %all-to-all-start = ((bf16[4,96,384]{2,1,0:T(8,128)(2,1)}), bf16[4,96,384]{2,1,0:T(8,128)(2,1)S(1)}, u32[]{:S(2)}, u32[]{:S(2)}) async-start(bf16[4,96,384]{2,1,0:T(8,128)(2,1)} %broadcast_in_dim.2), calls=%async_computation | async-start | bytes 589824 | tf_op jit(solution)/shard_map/all_to_all | solution.py:41
  55.8 5.2 %collective-permute-start.6 = (bf16[32,3072]{1,0:T(8,128)(2,1)S(1)}, bf16[32,3072]{1,0:T(8,128)(2,1)S(1)}, u32[]{:S(2)}, u32[]{:S(2)}) collective-permute-start(bf16[32,3072]{1,0:T(8,128)(2,1)S(1)} %collective-permute-done.2), channel_id=1, source_target_pairs={{0,128},{1,129},{2,130},{3,131},{4,132},{5,133},{6,134},{7,135},{8... | collective-permute-start | bytes 589832 | tf_op jit(solution)/shard_map/ppermute | solution.py:58
  61.0 0.5 shard_map.113.attn_ref
  61.5 16.6 %all-to-all-done = bf16[4,96,384]{2,1,0:T(8,128)(2,1)S(1)} async-done(((bf16[4,96,384]{2,1,0:T(8,128)(2,1)}), bf16[4,96,384]{2,1,0:T(8,128)(2,1)S(1)}, u32[]{:S(2)}, u32[]{:S(2)}) %all-to-all-start) | async-done | bytes 294944 | tf_op jit(solution)/shard_map/all_to_all | solution.py:41
  78.0 1.9 %collective-permute-start.5 = (bf16[384,384]{1,0:T(8,128)(2,1)S(1)}, bf16[384,384]{1,0:T(8,128)(2,1)S(1)}, u32[]{:S(2)}, u32[]{:S(2)}) collective-permute-start(bf16[384,384]{1,0:T(8,128)(2,1)S(1)} %bitcast.23), channel_id=1, source_target_pairs={{0,768},{1,769},{2,770},{3,771},{4,772},{5,773},{6,774},{7,775},{8... | collective-permute-start | bytes 884744 | tf_op jit(solution)/shard_map/ppermute | solution.py:27
  80.0 1.9 %collective-permute-start.4 = (bf16[384,384]{1,0:T(8,128)(2,1)S(1)}, bf16[384,384]{1,0:T(8,128)(2,1)S(1)}, u32[]{:S(2)}, u32[]{:S(2)}) collective-permute-start(bf16[384,384]{1,0:T(8,128)(2,1)S(1)} %bitcast.24), channel_id=1, source_target_pairs={{0,256},{1,257},{2,258},{3,259},{4,260},{5,261},{6,262},{7,263},{8... | collective-permute-start | bytes 884744 | tf_op jit(solution)/shard_map/ppermute | solution.py:27
  81.9 5.7 %collective-permute-start.3 = (bf16[384,384]{1,0:T(8,128)(2,1)S(1)}, bf16[384,384]{1,0:T(8,128)(2,1)S(1)}, u32[]{:S(2)}, u32[]{:S(2)}) collective-permute-start(bf16[384,384]{1,0:T(8,128)(2,1)S(1)} %bitcast.25), channel_id=1, source_target_pairs={{0,512},{1,513},{2,514},{3,515},{4,516},{5,517},{6,518},{7,519},{8... | collective-permute-start | bytes 884744 | tf_op jit(solution)/shard_map/ppermute | solution.py:27
  87.7 11.5 %all_gather.7.far_any = bf16[128,3072]{1,0:T(8,128)(2,1)} all-gather(bf16[32,3072]{1,0:T(8,128)(2,1)S(1)} %collective-permute-done.6), channel_id=1, replica_groups={{0,2,4,6},{1,3,5,7},{8,10,12,14},{9,11,13,15},{16,18,20,22},{17,19,21,2..., dimensions={0}, use_global_device_ids=true | all-gather | bytes 983040 | tf_op jit(solution)/shard_map/all_gather | solution.py:32
  99.2 1.1 pad_maximum_fusion.w_ref
  100.4 8.8 %collective-permute-start.7 = (bf16[1536,384]{1,0:T(8,128)(2,1)}, bf16[1536,384]{1,0:T(8,128)(2,1)S(1)}, u32[]{:S(2)}, u32[]{:S(2)}) collective-permute-start(bf16[1536,384]{1,0:T(8,128)(2,1)} %pad_maximum_fusion.w_ref), channel_id=1, source_target_pairs={{0,8},{1,9},{2,10},{3,11},{4,12},{5,13},{6,14},{7,15},{8,0},{9,1},... | collective-permute-start | bytes 3538952 | tf_op jit(solution)/shard_map/ppermute | solution.py:27
  109.2 0.1 stack.35.rows_ref
  109.3 3.4 %shard_map.114 = (f32[256,384]{1,0:T(8,128)S(1)}, bf16[256,1536]{1,0:T(8,128)(2,1)S(1)}, bf16[256,384]{1,0:T(8,128)(2,1)S(1)}, bf16[256,384]{1,0:T(8,128)(2,1)S(1)}, bf16[256,384]{1,0:T(8,128)(2,1)S(1)}) custom-call(bf16[1536,384]{1,0:T(8,128)(2,1)} %pad_maximum_fusion.w_ref, bf16[128,3072]{1,0:T(8,128)(2,1)} %all_gather.6.own_any, ...), custom_call_target="tpu_custom_call" | custom-call | flops 301989888 | bytes 3145728 | tf_op jit(solution)/shard_map/pallas_call | solution.py:194
  112.7 3.1 %shard_map.115 = (bf16[256,384]{1,0:T(8,128)(2,1)}, bf16[256,384]{1,0:T(8,128)(2,1)}, bf16[256,384]{1,0:T(8,128)(2,1)}) custom-call(s32[8]{0:T(128)S(1)} %stack.35.rows_ref, f32[3,256,256]{2,1,0:T(8,128)S(1)} %shard_map.113.attn_ref, bf16[1536,384]{1,0:T(8,128)(2,1)S(1)} %collective-permute-done.7.wc_ref, f32[256,384]{1,0:T(8,128)S(1)} %get-tuple-element.27.sum_ref, ...), custom_call_target="tpu_custom_call" | custom-call | flops 503316480 | bytes 6291456 | tf_op jit(solution)/shard_map/pallas_call | solution.py:211
  (17 shorter events, 0.1 us)
Async XLA Ops:
  0.6 48.9 %copy-start.4 = (bf16[24,384]{1,0:T(8,128)(2,1)S(1)}, bf16[24,384]{1,0:T(8,128)(2,1)}, u32[]{:S(2)}) copy-start(bf16[24,384]{1,0:T(8,128)(2,1)} %param.12) | copy-start | bytes 55300
  0.6 28.9 %collective-permute-start = (bf16[24,384]{1,0:T(8,128)(2,1)}, bf16[24,384]{1,0:T(8,128)(2,1)S(1)}, u32[]{:S(2)}, u32[]{:S(2)}) collective-permute-start(bf16[24,384]{1,0:T(8,128)(2,1)} %param.12), channel_id=1, source_target_pairs={{0,128},{1,129},{2,130},{3,131},{4,132},{5,133},{6,134},{7,135},{8... | collective-permute-start | bytes 55304 | tf_op jit(solution)/shard_map/ppermute | solution.py:27
  16.9 0.9 copy-start.3
  18.8 42.2 %copy-start = (bf16[1,256,384]{2,1,0:T(8,128)(2,1)S(1)}, bf16[1,256,384]{2,1,0:T(8,128)(2,1)}, u32[]{:S(2)}) copy-start(bf16[1,256,384]{2,1,0:T(8,128)(2,1)} %param.9) | copy-start | bytes 589828
  18.8 42.2 %copy-start.1 = (bf16[1,256,384]{2,1,0:T(8,128)(2,1)S(1)}, bf16[1,256,384]{2,1,0:T(8,128)(2,1)}, u32[]{:S(2)}) copy-start(bf16[1,256,384]{2,1,0:T(8,128)(2,1)} %param.10) | copy-start | bytes 589828
  18.8 32.8 %collective-permute-start.2 = (bf16[32,3072]{1,0:T(8,128)(2,1)S(1)}, bf16[32,3072]{1,0:T(8,128)(2,1)S(1)}, u32[]{:S(2)}, u32[]{:S(2)}) collective-permute-start(bf16[32,3072]{1,0:T(8,128)(2,1)S(1)} %shard_map.112), channel_id=1, source_target_pairs={{0,128},{1,129},{2,130},{3,131},{4,132},{5,133},{6,134},{7,135},{8... | collective-permute-start | bytes 589832 | tf_op jit(solution)/shard_map/ppermute | solution.py:58
  30.3 19.2 %collective-permute-start.1 = (bf16[48,384]{1,0:T(8,128)(2,1)S(1)}, bf16[48,384]{1,0:T(8,128)(2,1)S(1)}, u32[]{:S(2)}, u32[]{:S(2)}) collective-permute-start(bf16[48,384]{1,0:T(8,128)(2,1)S(1)} %pad_maximum_fusion.2), channel_id=1, source_target_pairs={{0,64},{1,65},{2,66},{3,67},{4,68},{5,69},{6,70},{7,71},{8,72},{9,... | collective-permute-start | bytes 110600 | tf_op jit(solution)/shard_map/ppermute | solution.py:27
  52.3 25.7 %all-to-all-start = ((bf16[4,96,384]{2,1,0:T(8,128)(2,1)}), bf16[4,96,384]{2,1,0:T(8,128)(2,1)S(1)}, u32[]{:S(2)}, u32[]{:S(2)}) async-start(bf16[4,96,384]{2,1,0:T(8,128)(2,1)} %broadcast_in_dim.2), calls=%async_computation | async-start | bytes 589824 | tf_op jit(solution)/shard_map/all_to_all | solution.py:41
  55.8 31.9 %collective-permute-start.6 = (bf16[32,3072]{1,0:T(8,128)(2,1)S(1)}, bf16[32,3072]{1,0:T(8,128)(2,1)S(1)}, u32[]{:S(2)}, u32[]{:S(2)}) collective-permute-start(bf16[32,3072]{1,0:T(8,128)(2,1)S(1)} %collective-permute-done.2), channel_id=1, source_target_pairs={{0,128},{1,129},{2,130},{3,131},{4,132},{5,133},{6,134},{7,135},{8... | collective-permute-start | bytes 589832 | tf_op jit(solution)/shard_map/ppermute | solution.py:58
  78.0 21.2 %collective-permute-start.5 = (bf16[384,384]{1,0:T(8,128)(2,1)S(1)}, bf16[384,384]{1,0:T(8,128)(2,1)S(1)}, u32[]{:S(2)}, u32[]{:S(2)}) collective-permute-start(bf16[384,384]{1,0:T(8,128)(2,1)S(1)} %bitcast.23), channel_id=1, source_target_pairs={{0,768},{1,769},{2,770},{3,771},{4,772},{5,773},{6,774},{7,775},{8... | collective-permute-start | bytes 884744 | tf_op jit(solution)/shard_map/ppermute | solution.py:27
  80.0 19.2 %collective-permute-start.4 = (bf16[384,384]{1,0:T(8,128)(2,1)S(1)}, bf16[384,384]{1,0:T(8,128)(2,1)S(1)}, u32[]{:S(2)}, u32[]{:S(2)}) collective-permute-start(bf16[384,384]{1,0:T(8,128)(2,1)S(1)} %bitcast.24), channel_id=1, source_target_pairs={{0,256},{1,257},{2,258},{3,259},{4,260},{5,261},{6,262},{7,263},{8... | collective-permute-start | bytes 884744 | tf_op jit(solution)/shard_map/ppermute | solution.py:27
  81.9 17.3 %collective-permute-start.3 = (bf16[384,384]{1,0:T(8,128)(2,1)S(1)}, bf16[384,384]{1,0:T(8,128)(2,1)S(1)}, u32[]{:S(2)}, u32[]{:S(2)}) collective-permute-start(bf16[384,384]{1,0:T(8,128)(2,1)S(1)} %bitcast.25), channel_id=1, source_target_pairs={{0,512},{1,513},{2,514},{3,515},{4,516},{5,517},{6,518},{7,519},{8... | collective-permute-start | bytes 884744 | tf_op jit(solution)/shard_map/ppermute | solution.py:27
  99.2 10.1 %copy-start.2 = (bf16[1,256,384]{2,1,0:T(8,128)(2,1)S(1)}, bf16[1,256,384]{2,1,0:T(8,128)(2,1)}, u32[]{:S(2)}) copy-start(bf16[1,256,384]{2,1,0:T(8,128)(2,1)} %param.11) | copy-start | bytes 589828
  100.4 12.3 %collective-permute-start.7 = (bf16[1536,384]{1,0:T(8,128)(2,1)}, bf16[1536,384]{1,0:T(8,128)(2,1)S(1)}, u32[]{:S(2)}, u32[]{:S(2)}) collective-permute-start(bf16[1536,384]{1,0:T(8,128)(2,1)} %pad_maximum_fusion.w_ref), channel_id=1, source_target_pairs={{0,8},{1,9},{2,10},{3,11},{4,12},{5,13},{6,14},{7,15},{8,0},{9,1},... | collective-permute-start | bytes 3538952 | tf_op jit(solution)/shard_map/ppermute | solution.py:27

commit v10 on v9

--- a/solution.py
+++ b/solution.py
@@ -153,16 +153,20 @@
     place = np.arange(span)
     slot = (place // block) % NZ
     quad = jnp.asarray((slot & 1) << 3 | (slot & 2) << 1)
-    source = (((quad ^ (z & 12)) | jnp.asarray(slot >> 2)) * NC + (jnp.asarray(place // (NZ * block)) ^ core)) * block
-    source = source + jnp.asarray(place % block)
-    own = pl.pallas_call(
+    def order(z):
+        source = ((quad ^ (z & 12)) | jnp.asarray(slot >> 2)) * NC + (jnp.asarray(place // (NZ * block)) ^ core)
+        source = source * block + jnp.asarray(place % block)
+        return y.reshape(1), source.astype(jnp.int32).reshape(1, span)
+
+    reorder = pl.pallas_call(
         reorder_kernel,
         out_shape=jax.ShapeDtypeStruct((part, model), jnp.bfloat16),
         in_specs=[SMEM, VMEM, VMEM],
         out_specs=VMEM,
         compiler_params=PARAMS,
         cost_estimate=pl.CostEstimate(flops=2 * part * model * span, bytes_accessed=4 * part * model, transcendentals=0),
-    )(y.reshape(1), source.astype(jnp.int32).reshape(1, span), grad_out.reshape(part, model))
+    )
+    own = grad_out.reshape(part, model)
 
     attn = pl.pallas_call(
         attention_kernel,
@@ -176,11 +180,12 @@
     arrived = swap(weight, z=8)
     half_way = quarter_turn(own)
     own, arrived = after(own, arrived)
+    own = reorder(*order(z), own)
     weight = jnp.concatenate([weight, arrived], 0)
     weight = jnp.concatenate([weight, swap(weight, z=4)], 0)
     own = gather_x(own)
     weight, half_way, own = after(weight, half_way, own)
-    far = quarter_turn(half_way)
+    far = quarter_turn(reorder(*order(z ^ (NZ // 2)), half_way))
     weight = share_quad(weight)
     weight = jnp.concatenate([weight] + [swap(weight, y=i) for i in Y_ORDER[1:]], 0)
     far = gather_x(far)

time: 116 us -> 120 us (1.034)
  the two profiles are of different devices: /device:TPU:129 before, /device:TPU:1 now
where the time goes in v10:
time: 120 us
  starting transfers between devices  71.2 us (59%)
  blocking collectives  23.4 us (20%)
  waiting for transfers between devices  11 us (9%)
  Pallas kernels  8.85 us (7%)
  other arithmetic  2.65 us (2%)
  local copies, waits for them, and re-layouts  1.78 us (1%)
    ppermute x6, starting transfers between devices, swap(): return lax.ppermute(value, AXES, exchange(**moves))  41.4 us
    ppermute x2, starting transfers between devices, quarter_turn(): return lax.ppermute(value, AXES, pairs)  26.1 us
    all_gather x2, blocking collectives, gather_x(): lax.all_gather(value, 'mp', axis_index_groups=groups, axis=0, tiled=True)  23.4 us
    ppermute x2, waiting for transfers between devices, quarter_turn(): return lax.ppermute(value, AXES, pairs)  11 us
    all_to_all x1, starting transfers between devices, share_quad(): shared = lax.all_to_all(copies, 'dp', 0, 0, axis_index_groups=groups)  3.71 us
    pallas_call x1, Pallas kernels, shards(): pl.pallas_call(first_half_kernel, out_shape=(jax.ShapeDtypeStruct((patche...  3.4 us
    pallas_call x1, Pallas kernels, shards(): pl.pallas_call(tail_kernel, out_shape=(grad_shape,) * 3, in_specs=[SMEM]...  3.09 us
  transfers between devices with their start and end apart: 9, of which 1 were waited for; matrix products, arithmetic and copies ran while one was open for 1% of the time, Pallas kernels for 5%

profile of v10, /device:TPU:1, one launch (start us, length us, event | category | flops | bytes accessed | tf_op | source)
XLA Modules:
  0.0 119.7 jit_solution(12048334990521227754)
XLA Ops:
  0.6 16.3 %collective-permute-start = (bf16[24,384]{1,0:T(8,128)(2,1)}, bf16[24,384]{1,0:T(8,128)(2,1)S(1)}, u32[]{:S(2)}, u32[]{:S(2)}) collective-permute-start(bf16[24,384]{1,0:T(8,128)(2,1)} %param.15), channel_id=1, source_target_pairs={{0,128},{1,129},{2,130},{3,131},{4,132},{5,133},{6,134},{7,135},{8... | collective-permute-start | bytes 55304 | tf_op jit(solution)/shard_map/ppermute | solution.py:27
  16.9 15.4 %collective-permute-start.2 = (bf16[32,3072]{1,0:T(8,128)(2,1)}, bf16[32,3072]{1,0:T(8,128)(2,1)S(1)}, u32[]{:S(2)}, u32[]{:S(2)}) collective-permute-start(bf16[32,3072]{1,0:T(8,128)(2,1)} %bitcast.22), channel_id=1, source_target_pairs={{0,128},{1,129},{2,130},{3,131},{4,132},{5,133},{6,134},{7,135},{8... | collective-permute-start | bytes 589832 | tf_op jit(solution)/shard_map/ppermute | solution.py:58
  32.4 0.8 fusion.3
  33.2 0.7 pad_maximum_fusion.2
  33.9 4.0 %collective-permute-start.1 = (bf16[48,384]{1,0:T(8,128)(2,1)S(1)}, bf16[48,384]{1,0:T(8,128)(2,1)S(1)}, u32[]{:S(2)}, u32[]{:S(2)}) collective-permute-start(bf16[48,384]{1,0:T(8,128)(2,1)S(1)} %pad_maximum_fusion.2), channel_id=1, source_target_pairs={{0,64},{1,65},{2,66},{3,67},{4,68},{5,69},{6,70},{7,71},{8,72},{9,... | collective-permute-start | bytes 110600 | tf_op jit(solution)/shard_map/ppermute | solution.py:27
  37.9 0.9 copy-done.3
  38.9 0.9 shard_map.139
  39.8 0.0 copy-start
  39.8 11.8 %all_gather.6.own_any = bf16[128,3072]{1,0:T(8,128)(2,1)} all-gather(bf16[32,3072]{1,0:T(8,128)(2,1)S(1)} %shard_map.139), channel_id=1, replica_groups={{0,2,4,6},{1,3,5,7},{8,10,12,14},{9,11,13,15},{16,18,20,22},{17,19,21,2..., dimensions={0}, use_global_device_ids=true | all-gather | bytes 983040 | tf_op jit(solution)/shard_map/all_gather | solution.py:32
  51.7 0.7 broadcast_in_dim.2
  52.4 3.7 %all-to-all-start = ((bf16[4,96,384]{2,1,0:T(8,128)(2,1)}), bf16[4,96,384]{2,1,0:T(8,128)(2,1)S(1)}, u32[]{:S(2)}, u32[]{:S(2)}) async-start(bf16[4,96,384]{2,1,0:T(8,128)(2,1)} %broadcast_in_dim.2), calls=%async_computation | async-start | bytes 589824 | tf_op jit(solution)/shard_map/all_to_all | solution.py:41
  56.1 0.9 shard_map.140
  57.1 10.6 %collective-permute-start.6 = (bf16[32,3072]{1,0:T(8,128)(2,1)S(1)}, bf16[32,3072]{1,0:T(8,128)(2,1)S(1)}, u32[]{:S(2)}, u32[]{:S(2)}) collective-permute-start(bf16[32,3072]{1,0:T(8,128)(2,1)S(1)} %shard_map.140), channel_id=1, source_target_pairs={{0,128},{1,129},{2,130},{3,131},{4,132},{5,133},{6,134},{7,135},{8... | collective-permute-start | bytes 589832 | tf_op jit(solution)/shard_map/ppermute | solution.py:58
  67.8 0.5 shard_map.141.attn_ref
  68.2 4.6 %collective-permute-start.5 = (bf16[384,384]{1,0:T(8,128)(2,1)S(1)}, bf16[384,384]{1,0:T(8,128)(2,1)S(1)}, u32[]{:S(2)}, u32[]{:S(2)}) collective-permute-start(bf16[384,384]{1,0:T(8,128)(2,1)S(1)} %bitcast.24), channel_id=1, source_target_pairs={{0,768},{1,769},{2,770},{3,771},{4,772},{5,773},{6,774},{7,775},{8... | collective-permute-start | bytes 884744 | tf_op jit(solution)/shard_map/ppermute | solution.py:27
  72.8 1.9 %collective-permute-start.4 = (bf16[384,384]{1,0:T(8,128)(2,1)S(1)}, bf16[384,384]{1,0:T(8,128)(2,1)S(1)}, u32[]{:S(2)}, u32[]{:S(2)}) collective-permute-start(bf16[384,384]{1,0:T(8,128)(2,1)S(1)} %bitcast.25), channel_id=1, source_target_pairs={{0,256},{1,257},{2,258},{3,259},{4,260},{5,261},{6,262},{7,263},{8... | collective-permute-start | bytes 884744 | tf_op jit(solution)/shard_map/ppermute | solution.py:27
  74.7 3.1 %collective-permute-start.3 = (bf16[384,384]{1,0:T(8,128)(2,1)S(1)}, bf16[384,384]{1,0:T(8,128)(2,1)S(1)}, u32[]{:S(2)}, u32[]{:S(2)}) collective-permute-start(bf16[384,384]{1,0:T(8,128)(2,1)S(1)} %bitcast.26), channel_id=1, source_target_pairs={{0,512},{1,513},{2,514},{3,515},{4,516},{5,517},{6,518},{7,519},{8... | collective-permute-start | bytes 884744 | tf_op jit(solution)/shard_map/ppermute | solution.py:27
  77.9 11.0 %collective-permute-done.6 = bf16[32,3072]{1,0:T(8,128)(2,1)S(1)} collective-permute-done((bf16[32,3072]{1,0:T(8,128)(2,1)S(1)}, bf16[32,3072]{1,0:T(8,128)(2,1)S(1)}, u32[]{:S(2)}, u32[]{:S(2)}) %collective-permute-start.6) | collective-permute-done | bytes 196640 | tf_op jit(solution)/shard_map/ppermute | solution.py:58
  88.8 11.5 %all_gather.7.far_any = bf16[128,3072]{1,0:T(8,128)(2,1)} all-gather(bf16[32,3072]{1,0:T(8,128)(2,1)S(1)} %collective-permute-done.6), channel_id=1, replica_groups={{0,2,4,6},{1,3,5,7},{8,10,12,14},{9,11,13,15},{16,18,20,22},{17,19,21,2..., dimensions={0}, use_global_device_ids=true | all-gather | bytes 983040 | tf_op jit(solution)/shard_map/all_gather | solution.py:32
  100.4 1.2 pad_maximum_fusion.w_ref
  101.5 11.5 %collective-permute-start.7 = (bf16[1536,384]{1,0:T(8,128)(2,1)}, bf16[1536,384]{1,0:T(8,128)(2,1)S(1)}, u32[]{:S(2)}, u32[]{:S(2)}) collective-permute-start(bf16[1536,384]{1,0:T(8,128)(2,1)} %pad_maximum_fusion.w_ref), channel_id=1, source_target_pairs={{0,8},{1,9},{2,10},{3,11},{4,12},{5,13},{6,14},{7,15},{8,0},{9,1},... | collective-permute-start | bytes 3538952 | tf_op jit(solution)/shard_map/ppermute | solution.py:27
  113.1 0.1 stack.35.rows_ref
  113.1 3.4 %shard_map.142 = (f32[256,384]{1,0:T(8,128)S(1)}, bf16[256,1536]{1,0:T(8,128)(2,1)S(1)}, bf16[256,384]{1,0:T(8,128)(2,1)S(1)}, bf16[256,384]{1,0:T(8,128)(2,1)S(1)}, bf16[256,384]{1,0:T(8,128)(2,1)S(1)}) custom-call(bf16[1536,384]{1,0:T(8,128)(2,1)} %pad_maximum_fusion.w_ref, bf16[128,3072]{1,0:T(8,128)(2,1)} %all_gather.6.own_any, ...), custom_call_target="tpu_custom_call" | custom-call | flops 301989888 | bytes 3145728 | tf_op jit(solution)/shard_map/pallas_call | solution.py:199
  116.6 3.1 %shard_map.143 = (bf16[256,384]{1,0:T(8,128)(2,1)}, bf16[256,384]{1,0:T(8,128)(2,1)}, bf16[256,384]{1,0:T(8,128)(2,1)}) custom-call(s32[8]{0:T(128)S(1)} %stack.35.rows_ref, f32[3,256,256]{2,1,0:T(8,128)S(1)} %shard_map.141.attn_ref, bf16[1536,384]{1,0:T(8,128)(2,1)S(1)} %collective-permute-done.7.wc_ref, f32[256,384]{1,0:T(8,128)S(1)} %get-tuple-element.27.sum_ref, ...), custom_call_target="tpu_custom_call" | custom-call | flops 503316480 | bytes 6291456 | tf_op jit(solution)/shard_map/pallas_call | solution.py:216
  (19 shorter events, 0.1 us)
Async XLA Ops:
  0.6 51.0 %copy-start.4 = (bf16[24,384]{1,0:T(8,128)(2,1)S(1)}, bf16[24,384]{1,0:T(8,128)(2,1)}, u32[]{:S(2)}) copy-start(bf16[24,384]{1,0:T(8,128)(2,1)} %param.15) | copy-start | bytes 55300
  0.6 32.5 %collective-permute-start = (bf16[24,384]{1,0:T(8,128)(2,1)}, bf16[24,384]{1,0:T(8,128)(2,1)S(1)}, u32[]{:S(2)}, u32[]{:S(2)}) collective-permute-start(bf16[24,384]{1,0:T(8,128)(2,1)} %param.15), channel_id=1, source_target_pairs={{0,128},{1,129},{2,130},{3,131},{4,132},{5,133},{6,134},{7,135},{8... | collective-permute-start | bytes 55304 | tf_op jit(solution)/shard_map/ppermute | solution.py:27
  16.9 34.8 %collective-permute-start.2 = (bf16[32,3072]{1,0:T(8,128)(2,1)}, bf16[32,3072]{1,0:T(8,128)(2,1)S(1)}, u32[]{:S(2)}, u32[]{:S(2)}) collective-permute-start(bf16[32,3072]{1,0:T(8,128)(2,1)} %bitcast.22), channel_id=1, source_target_pairs={{0,128},{1,129},{2,130},{3,131},{4,132},{5,133},{6,134},{7,135},{8... | collective-permute-start | bytes 589832 | tf_op jit(solution)/shard_map/ppermute | solution.py:58
  33.9 17.7 %collective-permute-start.1 = (bf16[48,384]{1,0:T(8,128)(2,1)S(1)}, bf16[48,384]{1,0:T(8,128)(2,1)S(1)}, u32[]{:S(2)}, u32[]{:S(2)}) collective-permute-start(bf16[48,384]{1,0:T(8,128)(2,1)S(1)} %pad_maximum_fusion.2), channel_id=1, source_target_pairs={{0,64},{1,65},{2,66},{3,67},{4,68},{5,69},{6,70},{7,71},{8,72},{9,... | collective-permute-start | bytes 110600 | tf_op jit(solution)/shard_map/ppermute | solution.py:27
  37.9 0.9 copy-start.3
  39.8 27.9 %copy-start = (bf16[1,256,384]{2,1,0:T(8,128)(2,1)S(1)}, bf16[1,256,384]{2,1,0:T(8,128)(2,1)}, u32[]{:S(2)}) copy-start(bf16[1,256,384]{2,1,0:T(8,128)(2,1)} %param.12) | copy-start | bytes 589828
  39.8 27.9 %copy-start.1 = (bf16[1,256,384]{2,1,0:T(8,128)(2,1)S(1)}, bf16[1,256,384]{2,1,0:T(8,128)(2,1)}, u32[]{:S(2)}) copy-start(bf16[1,256,384]{2,1,0:T(8,128)(2,1)} %param.13) | copy-start | bytes 589828
  52.4 15.8 %all-to-all-start = ((bf16[4,96,384]{2,1,0:T(8,128)(2,1)}), bf16[4,96,384]{2,1,0:T(8,128)(2,1)S(1)}, u32[]{:S(2)}, u32[]{:S(2)}) async-start(bf16[4,96,384]{2,1,0:T(8,128)(2,1)} %broadcast_in_dim.2), calls=%async_computation | async-start | bytes 589824 | tf_op jit(solution)/shard_map/all_to_all | solution.py:41
  57.1 31.7 %collective-permute-start.6 = (bf16[32,3072]{1,0:T(8,128)(2,1)S(1)}, bf16[32,3072]{1,0:T(8,128)(2,1)S(1)}, u32[]{:S(2)}, u32[]{:S(2)}) collective-permute-start(bf16[32,3072]{1,0:T(8,128)(2,1)S(1)} %shard_map.140), channel_id=1, source_target_pairs={{0,128},{1,129},{2,130},{3,131},{4,132},{5,133},{6,134},{7,135},{8... | collective-permute-start | bytes 589832 | tf_op jit(solution)/shard_map/ppermute | solution.py:58
  68.2 32.1 %collective-permute-start.5 = (bf16[384,384]{1,0:T(8,128)(2,1)S(1)}, bf16[384,384]{1,0:T(8,128)(2,1)S(1)}, u32[]{:S(2)}, u32[]{:S(2)}) collective-permute-start(bf16[384,384]{1,0:T(8,128)(2,1)S(1)} %bitcast.24), channel_id=1, source_target_pairs={{0,768},{1,769},{2,770},{3,771},{4,772},{5,773},{6,774},{7,775},{8... | collective-permute-start | bytes 884744 | tf_op jit(solution)/shard_map/ppermute | solution.py:27
  72.8 27.5 %collective-permute-start.4 = (bf16[384,384]{1,0:T(8,128)(2,1)S(1)}, bf16[384,384]{1,0:T(8,128)(2,1)S(1)}, u32[]{:S(2)}, u32[]{:S(2)}) collective-permute-start(bf16[384,384]{1,0:T(8,128)(2,1)S(1)} %bitcast.25), channel_id=1, source_target_pairs={{0,256},{1,257},{2,258},{3,259},{4,260},{5,261},{6,262},{7,263},{8... | collective-permute-start | bytes 884744 | tf_op jit(solution)/shard_map/ppermute | solution.py:27
  74.7 25.6 %collective-permute-start.3 = (bf16[384,384]{1,0:T(8,128)(2,1)S(1)}, bf16[384,384]{1,0:T(8,128)(2,1)S(1)}, u32[]{:S(2)}, u32[]{:S(2)}) collective-permute-start(bf16[384,384]{1,0:T(8,128)(2,1)S(1)} %bitcast.26), channel_id=1, source_target_pairs={{0,512},{1,513},{2,514},{3,515},{4,516},{5,517},{6,518},{7,519},{8... | collective-permute-start | bytes 884744 | tf_op jit(solution)/shard_map/ppermute | solution.py:27
  100.3 12.8 %copy-start.2 = (bf16[1,256,384]{2,1,0:T(8,128)(2,1)S(1)}, bf16[1,256,384]{2,1,0:T(8,128)(2,1)}, u32[]{:S(2)}) copy-start(bf16[1,256,384]{2,1,0:T(8,128)(2,1)} %param.14) | copy-start | bytes 589828
  101.5 15.0 %collective-permute-start.7 = (bf16[1536,384]{1,0:T(8,128)(2,1)}, bf16[1536,384]{1,0:T(8,128)(2,1)S(1)}, u32[]{:S(2)}, u32[]{:S(2)}) collective-permute-start(bf16[1536,384]{1,0:T(8,128)(2,1)} %pad_maximum_fusion.w_ref), channel_id=1, source_target_pairs={{0,8},{1,9},{2,10},{3,11},{4,12},{5,13},{6,14},{7,15},{8,0},{9,1},... | collective-permute-start | bytes 3538952 | tf_op jit(solution)/shard_map/ppermute | solution.py:27
